TPU v7x, 512 devices: a whole 4x8x8 slice. The times are simulated.
512 devices in a mesh: dp: 128 (over z, y, core), mp: 4 (over x).
Axes of the slice: x: 4, y: 8, z: 8, core: 2. Of those that a mesh axis runs over, the one named last changes fastest.
Arguments:
- tokens: bfloat16 [16384, 8192], P('dp', 'mp'), may hold values from -6 to 6
- fixed_value_weight: bfloat16 [8192, 1024], P('mp', 'dp'), may hold values from -0.0625 to 0.0625
- output_gradient: bfloat16 [16384, 1024], P('dp', 'mp'), may hold values from -6 to 6
- adapter_down_factor: bfloat16 [128, 8192, 64], P('dp', 'mp'), may hold values from -0.0625 to 0.0625
- adapter_up_factor: bfloat16 [128, 64, 1024], P('dp', None, 'mp'), may hold values from -0.75 to 0.75
- adapter_per_token: int32 [16384, 1], P('dp'), may hold values from 0 to 127; in each aligned block of 128 rows (0 to 127, 128 to 255, ...) at most 2 rows name the same one
- adapter_owner_index: int32 [128], replicated, may hold values from 0 to 127, each once
Outputs:
- projected: bfloat16 [16384, 1024], P('dp', 'mp')
- activation_gradient: bfloat16 [16384, 8192], P('dp', 'mp')
- down_factor_gradient: float32 [128, 8192, 64], P('dp', 'mp')
- up_factor_gradient: float32 [128, 64, 1024], P('dp', None, 'mp')
Inputs may be any that keep to these rules, and one draw needn't show every extreme that they name: `adapter_per_token`: among the tokens of one index of dp no adapter is named more than 2 times, and in some indices one is named exactly 2 times; every adapter is named by some token. `adapter_owner_index`: every owner index is named by exactly one adapter.
All inputs are finite; a program needn't handle non-finite values.
Results may differ from a plain program's by a relative error of at most 0.0037.
Values may be sent and summed in bfloat16 or wider, within the bound.
No kernel may reach another device: no remote copies, remote signals or barrier semaphores. Data moves between devices by JAX's collectives and lax.ppermute only.
A program may use at most 64 MiB of HBM per device.

v0:
```python
import jax
import jax.numpy as jnp
from jax import lax
from jax.sharding import PartitionSpec as P

adapter_scale = 0.5


def route_places(adapter_per_token, adapter_owner_index, owners, capacity):
    adapters = adapter_owner_index.shape[0]
    matches_adapter = adapter_per_token == jnp.arange(adapters, dtype=jnp.int32)[None, :]
    targets = jnp.sum(jnp.where(matches_adapter, adapter_owner_index[None, :], 0), axis=1)
    matches = (targets[:, None] == jnp.arange(owners, dtype=jnp.int32)[None, :]).astype(jnp.int32)
    before = jnp.cumsum(matches, axis=0) - matches
    places = jnp.sum(before * matches, axis=1)
    return targets * capacity + places


def spread(values, position, owners, capacity):
    buffer = jnp.zeros((owners * capacity, values.shape[1]), values.dtype).at[position].set(values)
    return buffer.reshape(owners, capacity, values.shape[1])


def collect(returned, position):
    return returned.reshape(-1, returned.shape[2])[position]


def reduce_trailing(left, right):
    return lax.dot_general(
        left, right, (((1,), (1,)), ((), ())), preferred_element_type=jnp.float32
    )


def reduce_leading(left, right):
    return lax.dot_general(
        left, right, (((0,), (0,)), ((), ())), preferred_element_type=jnp.float32
    )


def body(
    tokens,
    fixed_value_weight,
    output_gradient,
    adapter_down_factor,
    adapter_up_factor,
    adapter_per_token,
    adapter_owner_index,
):
    owners = lax.axis_size("dp")
    token_count = tokens.shape[0]
    capacity = max(2, 2 * token_count // owners)
    position = route_places(adapter_per_token, adapter_owner_index, owners, capacity)
    down_matrix = adapter_down_factor[0]
    upper_matrix = adapter_up_factor[0]
    outgoing_rows = spread(tokens, position, owners, capacity)
    outgoing_grad = spread(output_gradient, position, owners, capacity)
    arrived_rows = lax.all_to_all(outgoing_rows, "dp", split_axis=0, concat_axis=0, tiled=True)
    flat_rows = arrived_rows.reshape(-1, arrived_rows.shape[2])
    low_part = jnp.dot(flat_rows, down_matrix, preferred_element_type=jnp.float32)
    hidden_state = lax.psum(low_part, "mp").astype(jnp.bfloat16)
    extra_output = (
        adapter_scale * jnp.dot(hidden_state, upper_matrix, preferred_element_type=jnp.float32)
    ).astype(jnp.bfloat16)
    back_out = lax.all_to_all(
        extra_output.reshape(owners, capacity, -1), "dp", split_axis=0, concat_axis=0, tiled=True
    )
    arrived_grad = lax.all_to_all(outgoing_grad, "dp", split_axis=0, concat_axis=0, tiled=True)
    flat_gradient = arrived_grad.reshape(-1, arrived_grad.shape[2])
    grad_part = reduce_trailing(flat_gradient, upper_matrix)
    message_rows = lax.psum(grad_part, "mp").astype(jnp.bfloat16)
    extra_input = (adapter_scale * reduce_trailing(message_rows, down_matrix)).astype(jnp.bfloat16)
    back_input = lax.all_to_all(
        extra_input.reshape(owners, capacity, -1), "dp", split_axis=0, concat_axis=0, tiled=True
    )
    down_factor_gradient = adapter_scale * reduce_leading(flat_rows, message_rows)
    up_factor_gradient = adapter_scale * reduce_leading(hidden_state, flat_gradient)
    full_weight = lax.all_gather(fixed_value_weight, "dp", axis=1, tiled=True)
    base_sum = lax.psum_scatter(
        jnp.dot(tokens, full_weight, preferred_element_type=jnp.float32),
        "mp",
        scatter_dimension=1,
        tiled=True,
    )
    plain_input = reduce_trailing(
        lax.all_gather(output_gradient, "mp", axis=1, tiled=True), full_weight
    )
    projected = (base_sum + collect(back_out, position).astype(jnp.float32)).astype(jnp.bfloat16)
    activation_gradient = (plain_input + collect(back_input, position).astype(jnp.float32)).astype(
        jnp.bfloat16
    )
    return (projected, activation_gradient, down_factor_gradient[None], up_factor_gradient[None])


def solution(mesh):
    return jax.shard_map(
        body,
        mesh=mesh,
        in_specs=(
            P("dp", "mp"),
            P("mp", "dp"),
            P("dp", "mp"),
            P("dp", "mp", None),
            P("dp", None, "mp"),
            P("dp", None),
            P(),
        ),
        out_specs=(P("dp", "mp"), P("dp", "mp"), P("dp", "mp", None), P("dp", None, "mp")),
        check_vma=False,
    )
```

profile of v0, /device:TPU:1, one launch (start us, length us, event | category | flops | bytes accessed | tf_op | source)
XLA Modules:
  0.0 169.3 jit_solution(12872546488019439339)
XLA Ops:
  7.2 0.0 copy-start
  7.2 0.0 copy-start.2
  7.2 0.0 all-gather.2.cloned.1.call-start
  7.2 0.7 all-gather.2.cloned.1.call-update
  7.9 0.8 select_reduce_fusion.1
  8.8 0.1 fusion.12
  8.9 0.2 reduce_window_sum.11
  9.0 0.2 select_reduce_fusion
  9.2 1.4 scatter_custom_fusion.1
  10.6 0.7 reshape.64
  11.3 18.4 %all-to-all-start.2 = ((bf16[128,2,256]{2,1,0:T(2,128)(2,1)}), bf16[128,2,256]{2,1,0:T(2,128)(2,1)S(1)}, u32[]{:S(2)}, u32[]{:S(2)}) async-start(bf16[128,2,256]{2,1,0:T(2,128)(2,1)} %reshape.64), calls=%async_computation.3 | async-start | bytes 262144 | tf_op jit(solution)/shard_map/all_to_all | solution.py:67
  29.8 2.2 %scatter_custom_fusion = bf16[256,2048]{1,0:T(8,128)(2,1)S(1)} fusion(s32[128]{0:T(128)S(1)} %fusion.20, bf16[128,2048]{1,0:T(8,128)(2,1)} %param.7, bf16[]{:T(256)} %constant.5.clone.1), kind=kCustom, calls=%fused_computation.14 | custom fusion | bytes 1049088 | tf_op jit(solution)/shard_map/scatter | solution.py:20
  32.0 1.5 reshape.60
  33.5 9.0 %all-to-all-done.2 = bf16[128,2,256]{2,1,0:T(2,128)(2,1)S(1)} async-done(((bf16[128,2,256]{2,1,0:T(2,128)(2,1)}), bf16[128,2,256]{2,1,0:T(2,128)(2,1)S(1)}, u32[]{:S(2)}, u32[]{:S(2)}) %all-to-all-start.2) | async-done | bytes 131104 | tf_op jit(solution)/shard_map/all_to_all | solution.py:67
  42.5 5.6 %all-to-all-start = ((bf16[128,2,2048]{2,1,0:T(2,128)(2,1)}), bf16[128,2,2048]{2,1,0:T(2,128)(2,1)S(1)}, u32[]{:S(2)}, u32[]{:S(2)}) async-start(bf16[128,2,2048]{2,1,0:T(2,128)(2,1)} %reshape.60), calls=%async_computation.1 | async-start | bytes 2097152 | tf_op jit(solution)/shard_map/all_to_all | solution.py:57
  48.1 0.1 reshape.65
  48.1 0.0 copy-done.2
  48.2 0.2 fusion.13
  48.3 30.8 %all-to-all-done = bf16[128,2,2048]{2,1,0:T(2,128)(2,1)S(1)} async-done(((bf16[128,2,2048]{2,1,0:T(2,128)(2,1)}), bf16[128,2,2048]{2,1,0:T(2,128)(2,1)S(1)}, u32[]{:S(2)}, u32[]{:S(2)}) %all-to-all-start) | async-done | bytes 1048608 | tf_op jit(solution)/shard_map/all_to_all | solution.py:57
  79.1 0.4 reshape.61
  79.5 0.0 copy-done
  79.5 0.0 copy-start.1
  79.5 0.4 fusion.8
  80.0 15.0 %all-reduce.2 = (bf16[256,64]{0,1:T(8,128)(2,1)S(1)}, bf16[256,64]{0,1:T(8,128)(2,1)S(1)}) all-reduce(f32[256,64]{0,1:T(8,128)S(1)} %fusion.8, f32[256,64]{0,1:T(8,128)S(1)} %fusion.13), channel_id=1, replica_groups=mesh['dp'=128,'mp'=4] {'mp'}, use_global_device_ids=true, to_apply=%region_5.6 | all-reduce | flops 32768 | bytes 196608 | tf_op jit(solution)/shard_map/psum | solution.py:60
  95.0 0.2 fusion.3
  95.2 0.7 reshape.62
  95.9 10.3 %all-to-all-start.1 = ((bf16[128,2,256]{2,1,0:T(2,128)(2,1)}), bf16[128,2,256]{2,1,0:T(2,128)(2,1)S(1)}, u32[]{:S(2)}, u32[]{:S(2)}) async-start(bf16[128,2,256]{2,1,0:T(2,128)(2,1)} %reshape.62), calls=%async_computation.2 | async-start | bytes 262144 | tf_op jit(solution)/shard_map/all_to_all | solution.py:64
  106.2 0.5 fusion
  106.7 1.5 reshape.66
  108.2 0.0 copy-start.3
  108.2 11.0 %all-to-all-done.1 = bf16[128,2,256]{2,1,0:T(2,128)(2,1)S(1)} async-done(((bf16[128,2,256]{2,1,0:T(2,128)(2,1)}), bf16[128,2,256]{2,1,0:T(2,128)(2,1)S(1)}, u32[]{:S(2)}, u32[]{:S(2)}) %all-to-all-start.1) | async-done | bytes 131104 | tf_op jit(solution)/shard_map/all_to_all | solution.py:64
  119.1 5.7 %all-to-all-start.3 = ((bf16[128,2,2048]{2,1,0:T(2,128)(2,1)}), bf16[128,2,2048]{2,1,0:T(2,128)(2,1)S(1)}, u32[]{:S(2)}, u32[]{:S(2)}) async-start(bf16[128,2,2048]{2,1,0:T(2,128)(2,1)} %reshape.66), calls=%async_computation.4 | async-start | bytes 2097152 | tf_op jit(solution)/shard_map/all_to_all | solution.py:72
  124.9 0.0 reduce-scatter.2.cloned.1.call-start
  124.9 0.0 all-gather.2.cloned.1.call-done
  124.9 0.0 copy-done.1
  125.0 4.5 %fusion.21 = f32[128,1024]{1,0:T(8,128)} fusion(bf16[128,2048]{1,0:T(8,128)(2,1)S(1)} %copy-done.1, bf16[2048,1024]{0,1:T(8,128)(2,1)} %all-gather.2.cloned.1.call-done), kind=kOutput, calls=%fused_computation.37 | convolution fusion | flops 536870912 | bytes 5242880 | tf_op jit(solution)/shard_map/dot_general | solution.py:79
  129.5 0.0 reduce-scatter.2.cloned.1.call-update
  129.5 0.0 copy-done.3
  129.5 10.3 %all_gather.7 = bf16[128,1024]{1,0:T(8,128)(2,1)S(1)} all-gather(bf16[128,256]{1,0:T(8,128)(2,1)S(1)} %copy-done.3), channel_id=1, replica_groups=mesh['dp'=128,'mp'=4] {'mp'}, dimensions={1}, use_global_device_ids=true | all-gather | bytes 327680 | tf_op jit(solution)/shard_map/all_gather | solution.py:85
  139.8 0.8 fusion.4
  140.5 1.1 fusion.2
  141.6 0.1 reshape.63
  141.7 0.8 gather_fusion
  142.5 13.3 %all-to-all-done.3 = bf16[128,2,2048]{2,1,0:T(2,128)(2,1)S(1)} async-done(((bf16[128,2,2048]{2,1,0:T(2,128)(2,1)}), bf16[128,2,2048]{2,1,0:T(2,128)(2,1)S(1)}, u32[]{:S(2)}, u32[]{:S(2)}) %all-to-all-start.3) | async-done | bytes 1048608 | tf_op jit(solution)/shard_map/all_to_all | solution.py:72
  155.9 0.4 reshape.67
  156.3 0.9 gather_fusion.1
  157.3 3.7 %fusion.1 = bf16[128,2048]{1,0:T(8,128)(2,1)} fusion(bf16[128,1024]{1,0:T(8,128)(2,1)S(1)} %all_gather.7, bf16[2048,1024]{0,1:T(8,128)(2,1)} %all-gather.2.cloned.1.call-done, bf16[128,2048]{1,0:T(8,128)(2,1)S(1)} %gather_fusion.1), kind=kOutput, calls=%fused_computation.7 | convolution fusion | flops 537657344 | bytes 5505024 | tf_op jit(solution)/shard_map/dot_general | solution.py:29
  161.0 1.5 add_convert_fusion
  (3 shorter events, 0.0 us)
Async XLA Ops:
  7.2 72.3 %copy-start = (bf16[1,2048,64]{1,2,0:T(8,128)(2,1)S(1)}, bf16[1,2048,64]{1,2,0:T(8,128)(2,1)}, u32[]{:S(2)}) copy-start(bf16[1,2048,64]{1,2,0:T(8,128)(2,1)} %param.10) | copy-start | bytes 786436
  7.2 41.0 %copy-start.2 = (bf16[1,64,256]{2,1,0:T(8,128)(2,1)S(1)}, bf16[1,64,256]{2,1,0:T(8,128)(2,1)}, u32[]{:S(2)}) copy-start(bf16[1,64,256]{2,1,0:T(8,128)(2,1)} %param.11) | copy-start | bytes 98308
  7.2 117.7 %all-gather.2.cloned.1.call-start = ((), (), s32[]{:S(2)}) async-start(), calls=%async_computation.5 | async-start | bytes 4227072 | tf_op jit(solution)/shard_map/all_gather | solution.py:77
  11.3 31.2 %all-to-all-start.2 = ((bf16[128,2,256]{2,1,0:T(2,128)(2,1)}), bf16[128,2,256]{2,1,0:T(2,128)(2,1)S(1)}, u32[]{:S(2)}, u32[]{:S(2)}) async-start(bf16[128,2,256]{2,1,0:T(2,128)(2,1)} %reshape.64), calls=%async_computation.3 | async-start | bytes 262144 | tf_op jit(solution)/shard_map/all_to_all | solution.py:67
  42.5 36.6 %all-to-all-start = ((bf16[128,2,2048]{2,1,0:T(2,128)(2,1)}), bf16[128,2,2048]{2,1,0:T(2,128)(2,1)S(1)}, u32[]{:S(2)}, u32[]{:S(2)}) async-start(bf16[128,2,2048]{2,1,0:T(2,128)(2,1)} %reshape.60), calls=%async_computation.1 | async-start | bytes 2097152 | tf_op jit(solution)/shard_map/all_to_all | solution.py:57
  79.5 45.4 %copy-start.1 = (bf16[128,2048]{1,0:T(8,128)(2,1)S(1)}, bf16[128,2048]{1,0:T(8,128)(2,1)}, u32[]{:S(2)}) copy-start(bf16[128,2048]{1,0:T(8,128)(2,1)} %param.7) | copy-start | bytes 1572868
  95.9 23.2 %all-to-all-start.1 = ((bf16[128,2,256]{2,1,0:T(2,128)(2,1)}), bf16[128,2,256]{2,1,0:T(2,128)(2,1)S(1)}, u32[]{:S(2)}, u32[]{:S(2)}) async-start(bf16[128,2,256]{2,1,0:T(2,128)(2,1)} %reshape.62), calls=%async_computation.2 | async-start | bytes 262144 | tf_op jit(solution)/shard_map/all_to_all | solution.py:64
  108.2 21.3 %copy-start.3 = (bf16[128,256]{1,0:T(8,128)(2,1)S(1)}, bf16[128,256]{1,0:T(8,128)(2,1)}, u32[]{:S(2)}) copy-start(bf16[128,256]{1,0:T(8,128)(2,1)} %param.9) | copy-start | bytes 196612
  119.1 36.7 %all-to-all-start.3 = ((bf16[128,2,2048]{2,1,0:T(2,128)(2,1)}), bf16[128,2,2048]{2,1,0:T(2,128)(2,1)S(1)}, u32[]{:S(2)}, u32[]{:S(2)}) async-start(bf16[128,2,2048]{2,1,0:T(2,128)(2,1)} %reshape.66), calls=%async_computation.4 | async-start | bytes 2097152 | tf_op jit(solution)/shard_map/all_to_all | solution.py:72
  124.9 36.1 %reduce-scatter.2.cloned.1.call-start = ((), (), s32[]{:S(2)}) async-start(), calls=%async_computation.6 | async-start | bytes 655360 | tf_op jit(solution)/shard_map/reduce_scatter | solution.py:78
Sparse Core Ops, SparseCore 0:
  11.2 107.4 all-gather.1
  129.6 25.0 reduce-scatter.1
where the time goes:
time: 170 us; the launch traced here: 169 us
  waiting for transfers between devices  64.8 us (38%)
  starting transfers between devices  40.1 us (24%)
  blocking collectives  25.3 us (15%)
  between operations  14.2 us (8%)
  matrix products  11.3 us (7%)
  local copies, waits for them, and re-layouts  10.8 us (6%)
  other arithmetic  2.83 us (2%)
    all_to_all x1, waiting for transfers between devices, body(): lax.all_to_all(outgoing_rows, 'dp', split_axis=0, concat_axis=0, tiled=True)  30.8 us
    all_to_all x1, starting transfers between devices, body(): lax.all_to_all(outgoing_grad, 'dp', split_axis=0, concat_axis=0, tiled=True)  18.4 us
    psum x1, blocking collectives, body(): hidden_state = lax.psum(low_part, 'mp').astype(jnp.bfloat16)  15 us
    all_to_all x1, waiting for transfers between devices, body(): lax.all_to_all(extra_input.reshape(owners, capacity, -1), 'dp', split_axi...  13.3 us
    all_to_all x1, waiting for transfers between devices, body(): lax.all_to_all(extra_output.reshape(owners, capacity, -1), 'dp', split_ax...  11 us
    all_to_all x1, starting transfers between devices, body(): lax.all_to_all(extra_output.reshape(owners, capacity, -1), 'dp', split_ax...  10.3 us
    all_gather x1, blocking collectives, body(): lax.all_gather(output_gradient, 'mp', axis=1, tiled=True)  10.3 us
    all_to_all x1, waiting for transfers between devices, body(): lax.all_to_all(outgoing_grad, 'dp', split_axis=0, concat_axis=0, tiled=True)  8.99 us
  transfers between devices with their start and end apart: 6, of which 4 were waited for; matrix products, arithmetic and copies ran while one was open for 14% of the time, Pallas kernels for 0%

commit v1 on v0

v1 whole, which is shorter than its diff:
```python
import jax
import jax.numpy as jnp
from jax import lax
from jax.sharding import PartitionSpec as P

adapter_scale = 0.5
f32 = jnp.float32
bf16 = jnp.bfloat16


def dot(left, right, contract):
    return lax.dot_general(left, right, ((contract[0], contract[1]), ((), ())), preferred_element_type=f32)


def slot_matrix(adapter_per_token, adapter_owner_index, owners, capacity):
    token_count = adapter_per_token.shape[0]
    adapters = adapter_owner_index.shape[0]
    adapter_of = adapter_per_token.reshape(1, token_count)
    names = (adapter_of == lax.broadcasted_iota(jnp.int32, (adapters, token_count), 0)).astype(bf16)
    owned = (
        adapter_owner_index[None, :] == lax.broadcasted_iota(jnp.int32, (owners, adapters), 0)
    ).astype(bf16)
    matches = dot(owned, names, ((1,), (0,)))
    earlier = (
        lax.broadcasted_iota(jnp.int32, (token_count, token_count), 0)
        < lax.broadcasted_iota(jnp.int32, (token_count, token_count), 1)
    ).astype(bf16)
    before = dot(matches.astype(bf16), earlier, ((1,), (0,)))
    place = jnp.arange(capacity, dtype=f32)[None, :, None]
    picks = jnp.where(before[:, None, :] == place, matches[:, None, :], 0.0).astype(bf16)
    return picks.reshape(owners * capacity, token_count)


def body(
    tokens,
    fixed_value_weight,
    output_gradient,
    adapter_down_factor,
    adapter_up_factor,
    adapter_per_token,
    adapter_owner_index,
):
    owners = lax.axis_size("dp")
    parts = lax.axis_size("mp")
    token_count, width = tokens.shape
    features = output_gradient.shape[1]
    rank = adapter_down_factor.shape[2]
    capacity = max(2, 2 * token_count // owners)
    slots = owners * capacity
    down_matrix = adapter_down_factor[0]
    upper_matrix = adapter_up_factor[0]

    full_weight = lax.all_gather(fixed_value_weight, "dp", axis=1, tiled=True)

    picks = slot_matrix(adapter_per_token, adapter_owner_index, owners, capacity)
    both = jnp.concatenate([tokens, output_gradient], axis=1)
    outgoing = dot(picks, both, ((1,), (0,))).astype(bf16).reshape(owners, capacity, width + features)
    arrived = lax.all_to_all(outgoing, "dp", split_axis=0, concat_axis=0, tiled=True)
    arrived = arrived.reshape(slots, width + features)
    rows, grads = arrived[:, :width], arrived[:, width:]
    low = jnp.concatenate(
        [dot(rows, down_matrix, ((1,), (0,))), dot(grads, upper_matrix, ((1,), (1,)))], axis=1
    )
    own_gradient = output_gradient.reshape(slots, 2 * rank).astype(f32)
    sent = jnp.concatenate([low, own_gradient], axis=0)
    exchanged = lax.all_to_all(
        jnp.broadcast_to(sent[None], (parts,) + sent.shape), "mp", split_axis=0, concat_axis=0, tiled=True
    )
    summed = jnp.sum(exchanged[:, :slots], axis=0).astype(bf16)
    hidden, signal = summed[:, :rank], summed[:, rank:]
    whole_gradient = (
        exchanged[:, slots:].astype(bf16).reshape(parts, token_count, features).transpose(1, 0, 2)
    ).reshape(token_count, parts * features)
    extra_input = (adapter_scale * dot(signal, down_matrix, ((1,), (1,)))).astype(bf16)
    extra_output = (adapter_scale * dot(hidden, upper_matrix, ((1,), (0,)))).astype(bf16)
    back = jnp.concatenate([extra_input, extra_output], axis=1).reshape(owners, capacity, width + features)
    returned = lax.all_to_all(back, "dp", split_axis=0, concat_axis=0, tiled=True)
    returned = returned.reshape(slots, width + features)
    down_factor_gradient = adapter_scale * dot(rows, signal, ((0,), (0,)))
    up_factor_gradient = adapter_scale * dot(hidden, grads, ((0,), (0,)))

    base = dot(tokens, full_weight, ((1,), (0,)))
    base = base.reshape(token_count, parts, features).transpose(1, 0, 2)
    pieces = lax.all_to_all(base, "mp", split_axis=0, concat_axis=0, tiled=True)
    plain_input = dot(whole_gradient, full_weight, ((1,), (1,)))
    collected = dot(picks, returned, ((0,), (0,)))
    activation_gradient = (plain_input + collected[:, :width]).astype(bf16)
    projected = (jnp.sum(pieces, axis=0) + collected[:, width:]).astype(bf16)
    return (projected, activation_gradient, down_factor_gradient[None], up_factor_gradient[None])


def solution(mesh):
    return jax.shard_map(
        body,
        mesh=mesh,
        in_specs=(
            P("dp", "mp"),
            P("mp", "dp"),
            P("dp", "mp"),
            P("dp", "mp", None),
            P("dp", None, "mp"),
            P("dp", None),
            P(),
        ),
        out_specs=(P("dp", "mp"), P("dp", "mp"), P("dp", "mp", None), P("dp", None, "mp")),
        check_vma=False,
    )
```

time: 170 us -> 159 us (0.935)
  the two profiles are of different devices: /device:TPU:1 before, /device:TPU:88 now
where the time goes in v1:
time: 159 us
  waiting for transfers between devices  69.5 us (44%)
  starting transfers between devices  32.9 us (21%)
  blocking collectives  19.2 us (12%)
  between operations  14.2 us (9%)
  matrix products  13.6 us (9%)
  local copies, waits for them, and re-layouts  8.53 us (5%)
    all_to_all x1, waiting for transfers between devices, body(): lax.all_to_all(outgoing, 'dp', split_axis=0, concat_axis=0, tiled=True)  32.2 us
    all_gather x1, waiting for transfers between devices, body(): full_weight = lax.all_gather(fixed_value_weight, 'dp', axis=1, tiled=True)  30.8 us
    all_to_all x1, blocking collectives, body(): lax.all_to_all(jnp.broadcast_to(sent[None], (parts,) + sent.shape), 'mp',...  19.2 us
    all_to_all x1, starting transfers between devices, body(): lax.all_to_all(outgoing, 'dp', split_axis=0, concat_axis=0, tiled=True)  16.4 us
    dot_general x12, matrix products, dot(): lax.dot_general(left, right, ((contract[0], contract[1]), ((), ())), pref...  13.6 us
    all_to_all x1, starting transfers between devices, body(): lax.all_to_all(back, 'dp', split_axis=0, concat_axis=0, tiled=True)  8.67 us
    all_to_all x1, starting transfers between devices, body(): pieces = lax.all_to_all(base, 'mp', split_axis=0, concat_axis=0, tiled=True)  7.83 us
    all_to_all x1, waiting for transfers between devices, body(): pieces = lax.all_to_all(base, 'mp', split_axis=0, concat_axis=0, tiled=True)  5.78 us
  transfers between devices with their start and end apart: 4, of which 3 were waited for; matrix products, arithmetic and copies ran while one was open for 13% of the time, Pallas kernels for 0%

profile of v1, /device:TPU:88, one launch (start us, length us, event | category | flops | bytes accessed | tf_op | source)
XLA Modules:
  0.0 158.9 jit_solution(15863544226887061013)
XLA Ops:
  7.2 0.0 copy-start
  7.2 0.0 all-gather.2.cloned.1.call-start
  7.2 0.7 all-gather.2.cloned.1.call-update
  7.9 0.1 eq.52
  8.1 0.8 fusion.22
  8.9 0.1 fusion.23
  9.0 0.1 eq.47
  9.1 1.6 %convolution_convert_fusion = bf16[256,2304]{1,0:T(8,128)(2,1)S(1)} fusion(bf16[128,256]{1,0:T(8,128)(2,1)} %param.9, bf16[128,2048]{1,0:T(8,128)(2,1)} %param.7, bf16[256,128]{1,0:T(8,128)(2,1)S(1)} %bitcast.37, f32[256,128]{1,0:T(8,128)S(1)} %bitcast.36, f32[256]{0:T(256)S(1)} %eq.52), kind=kOutput, calls=%fused_computation | convolution fusion | flops 152829952 | bytes 1967104 | tf_op jit(solution)/shard_map/dot_general | solution.py:12
  10.7 1.3 reshape.41
  12.0 0.0 copy-start.3
  12.0 16.4 %all-to-all-start.1 = ((bf16[128,2,2304]{2,1,0:T(2,128)(2,1)}), bf16[128,2,2304]{2,1,0:T(2,128)(2,1)S(1)}, u32[]{:S(2)}, u32[]{:S(2)}) async-start(bf16[128,2,2304]{2,1,0:T(2,128)(2,1)} %reshape.41), calls=%async_computation.1 | async-start | bytes 2359296 | tf_op jit(solution)/shard_map/all_to_all | solution.py:58
  28.4 0.0 copy-done.3
  28.5 0.1 copy.28
  28.6 0.0 copy-start.4
  28.6 32.2 %all-to-all-done.1 = bf16[128,2,2304]{2,1,0:T(2,128)(2,1)S(1)} async-done(((bf16[128,2,2304]{2,1,0:T(2,128)(2,1)}), bf16[128,2,2304]{2,1,0:T(2,128)(2,1)S(1)}, u32[]{:S(2)}, u32[]{:S(2)}) %all-to-all-start.1) | async-done | bytes 1179680 | tf_op jit(solution)/shard_map/all_to_all | solution.py:58
  60.8 0.5 reshape.42
  61.2 0.0 copy-done.4
  61.2 0.2 fusion.17
  61.4 0.0 copy-done
  61.4 0.5 fusion.7
  61.9 0.1 copy.29
  62.0 0.1 broadcast_in_dim.36
  62.1 19.2 %all_to_all.20 = f32[4,512,128]{2,1,0:T(8,128)S(1)} all-to-all(f32[4,512,128]{2,1,0:T(8,128)S(1)} %broadcast_in_dim.36), channel_id=1, replica_groups=mesh['dp'=128,'mp'=4] {'mp'}, dimensions={0} | all-to-all | bytes 2097152 | tf_op jit(solution)/shard_map/all_to_all | solution.py:66
  81.3 0.0 copy-start.1
  81.4 1.0 copy-done.1
  82.3 0.2 fusion.4
  82.5 0.5 fusion
  83.0 0.1 pad_maximum_fusion
  83.1 1.3 reshape.43
  84.4 8.7 %all-to-all-start.3 = ((bf16[128,2,2304]{2,1,0:T(2,128)(2,1)}), bf16[128,2,2304]{2,1,0:T(2,128)(2,1)S(1)}, u32[]{:S(2)}, u32[]{:S(2)}) async-start(bf16[128,2,2304]{2,1,0:T(2,128)(2,1)} %reshape.43), calls=%async_computation.3 | async-start | bytes 2359296 | tf_op jit(solution)/shard_map/all_to_all | solution.py:77
  93.1 0.1 fusion.14
  93.1 1.1 slice.63
  94.2 0.8 reshape.44
  95.0 0.0 copy-start.2
  95.0 1.2 copy.33
  96.2 0.8 fusion.5
  97.0 1.2 fusion.2
  98.2 30.8 %all-gather.2.cloned.1.call-done = bf16[2048,1024]{0,1:T(8,128)(2,1)} async-done(((bf16[2048,8]{0,1:T(8,128)(2,1)}), bf16[2048,1024]{0,1:T(8,128)(2,1)}) %all-gather.2.cloned.1.call-update) | async-done | bytes 4194320 | tf_op jit(solution)/shard_map/all_gather | solution.py:53
  129.0 0.0 copy-done.2
  129.1 3.7 %fusion.35 = f32[128,1024]{1,0:T(8,128)S(1)} fusion(bf16[128,2048]{1,0:T(8,128)(2,1)S(1)} %copy-done.2, bf16[2048,1024]{0,1:T(8,128)(2,1)} %all-gather.2.cloned.1.call-done), kind=kOutput, calls=%fused_computation.53 | convolution fusion | flops 536870912 | bytes 5242880 | tf_op jit(solution)/shard_map/dot_general | solution.py:12
  132.8 0.9 copy.41
  133.6 0.0 all-to-all-done.3
  133.6 7.8 %all-to-all-start = ((f32[4,128,256]{2,1,0:T(8,128)}), f32[4,128,256]{2,1,0:T(8,128)S(1)}, u32[]{:S(2)}, u32[]{:S(2)}) async-start(f32[4,128,256]{2,1,0:T(8,128)} %bitcast.32), calls=%async_computation | async-start | bytes 1048576 | tf_op jit(solution)/shard_map/all_to_all | solution.py:84
  141.5 0.4 convolution_bitcast_fusion
  141.8 3.7 %fusion.1 = bf16[128,2048]{1,0:T(8,128)(2,1)} fusion(bf16[128,1024]{0,1:T(8,128)(2,1)S(1)} %bitcast.34, bf16[2048,1024]{0,1:T(8,128)(2,1)} %all-gather.2.cloned.1.call-done, f32[128,2304]{1,0:T(8,128)S(1)} %convolution_bitcast_fusion), kind=kOutput, calls=%fused_computation.5 | convolution fusion | flops 537395200 | bytes 6029312 | tf_op jit(solution)/shard_map/dot_general | solution.py:12
  145.6 5.8 %all-to-all-done = f32[4,128,256]{2,1,0:T(8,128)S(1)} async-done(((f32[4,128,256]{2,1,0:T(8,128)}), f32[4,128,256]{2,1,0:T(8,128)S(1)}, u32[]{:S(2)}, u32[]{:S(2)}) %all-to-all-start) | async-done | bytes 524320 | tf_op jit(solution)/shard_map/all_to_all | solution.py:84
  151.4 0.6 fusion.15
  (6 shorter events, 0.2 us)
Async XLA Ops:
  7.2 54.2 %copy-start = (bf16[1,2048,64]{1,2,0:T(8,128)(2,1)S(1)}, bf16[1,2048,64]{1,2,0:T(8,128)(2,1)}, u32[]{:S(2)}) copy-start(bf16[1,2048,64]{1,2,0:T(8,128)(2,1)} %param.10) | copy-start | bytes 786436
  7.2 121.9 %all-gather.2.cloned.1.call-start = ((), (), s32[]{:S(2)}) async-start(), calls=%async_computation.4 | async-start | bytes 4227072 | tf_op jit(solution)/shard_map/all_gather | solution.py:53
  12.0 16.4 %copy-start.3 = (bf16[128,256]{1,0:T(8,128)(2,1)S(1)}, bf16[128,256]{1,0:T(8,128)(2,1)}, u32[]{:S(2)}) copy-start(bf16[128,256]{1,0:T(8,128)(2,1)} %param.9) | copy-start | bytes 196612
  12.0 48.7 %all-to-all-start.1 = ((bf16[128,2,2304]{2,1,0:T(2,128)(2,1)}), bf16[128,2,2304]{2,1,0:T(2,128)(2,1)S(1)}, u32[]{:S(2)}, u32[]{:S(2)}) async-start(bf16[128,2,2304]{2,1,0:T(2,128)(2,1)} %reshape.41), calls=%async_computation.1 | async-start | bytes 2359296 | tf_op jit(solution)/shard_map/all_to_all | solution.py:58
  28.6 32.7 %copy-start.4 = (bf16[1,64,256]{2,1,0:T(8,128)(2,1)S(1)}, bf16[1,64,256]{2,1,0:T(8,128)(2,1)}, u32[]{:S(2)}) copy-start(bf16[1,64,256]{2,1,0:T(8,128)(2,1)} %param.11) | copy-start | bytes 98308
  81.3 1.0 copy-start.1
  84.4 49.3 %all-to-all-start.3 = ((bf16[128,2,2304]{2,1,0:T(2,128)(2,1)}), bf16[128,2,2304]{2,1,0:T(2,128)(2,1)S(1)}, u32[]{:S(2)}, u32[]{:S(2)}) async-start(bf16[128,2,2304]{2,1,0:T(2,128)(2,1)} %reshape.43), calls=%async_computation.3 | async-start | bytes 2359296 | tf_op jit(solution)/shard_map/all_to_all | solution.py:77
  95.0 34.0 %copy-start.2 = (bf16[128,2048]{1,0:T(8,128)(2,1)S(1)}, bf16[128,2048]{1,0:T(8,128)(2,1)}, u32[]{:S(2)}) copy-start(bf16[128,2048]{1,0:T(8,128)(2,1)} %param.7) | copy-start | bytes 1572868
  133.6 17.7 %all-to-all-start = ((f32[4,128,256]{2,1,0:T(8,128)}), f32[4,128,256]{2,1,0:T(8,128)S(1)}, u32[]{:S(2)}, u32[]{:S(2)}) async-start(f32[4,128,256]{2,1,0:T(8,128)} %bitcast.32), calls=%async_computation | async-start | bytes 1048576 | tf_op jit(solution)/shard_map/all_to_all | solution.py:84
Sparse Core Ops, SparseCore 0:
  11.1 117.8 all-gather.1

commit v2 on v1

v2 whole, which is shorter than its diff:
```python
import jax
import jax.numpy as jnp
from jax import lax
from jax.experimental import pallas as pl
from jax.experimental.pallas import tpu as pltpu
from jax.sharding import PartitionSpec as P

adapter_scale = 0.5
f32 = jnp.float32
bf16 = jnp.bfloat16
VMEM_LIMIT = 48 * 1024 * 1024

N_Z, N_Y, N_C = 8, 8, 2
CLASSES = 4
FOLD = 4
CHUNK = 512


def chip_class(z, y):
    return (z + 2 * y) % CLASSES


def contract(left, right, left_dim, right_dim):
    return lax.dot_general(
        left, right, (((left_dim,), (right_dim,)), ((), ())), preferred_element_type=f32
    )


def call(kernel, outs, name, flops, nbytes, limit=VMEM_LIMIT, **kwargs):
    return pl.pallas_call(
        kernel,
        out_shape=outs,
        name=name,
        compiler_params=pltpu.CompilerParams(vmem_limit_bytes=limit),
        cost_estimate=pl.CostEstimate(flops=flops, bytes_accessed=nbytes, transcendentals=0),
        **kwargs,
    )


def paired(rows):
    return rows.reshape(rows.shape[0] // 2, 2, rows.shape[1])


def flat(pairs):
    return pairs.reshape(pairs.shape[0] * 2, pairs.shape[2])


def spread_kernel(
    adapter_hbm,
    owner_hbm,
    tokens_hbm,
    grads_hbm,
    weight_hbm,
    out_ref,
    picks_ref,
    adapter_ref,
    owner_ref,
    tokens_ref,
    grads_ref,
    weight_ref,
    sems,
):
    copies = [
        pltpu.make_async_copy(source, target, sems.at[at])
        for at, (source, target) in enumerate(
            (
                (adapter_hbm, adapter_ref),
                (owner_hbm, owner_ref),
                (weight_hbm, weight_ref),
                (grads_hbm, grads_ref),
                (tokens_hbm, tokens_ref),
            )
        )
    ]
    for copy in copies:
        copy.start()
    slots, token_count = picks_ref.shape
    adapters = owner_ref.shape[1]
    width, features = tokens_ref.shape[1], grads_ref.shape[1]
    own_features = weight_ref.shape[0]
    slices = CLASSES * N_C
    depth = width // slices

    copies[0].wait()
    copies[1].wait()
    row = lax.broadcasted_iota(jnp.int32, (slots, adapters), 0)
    owned = (owner_ref[...] == lax.shift_right_logical(row, 1)).astype(f32).astype(bf16)
    names = (
        adapter_ref[...] == lax.broadcasted_iota(jnp.int32, (adapters, token_count), 0)
    ).astype(f32).astype(bf16)
    matches = contract(owned, names, 1, 0)
    earlier = (
        lax.broadcasted_iota(jnp.int32, (token_count, token_count), 0)
        < lax.broadcasted_iota(jnp.int32, (token_count, token_count), 1)
    ).astype(f32).astype(bf16)
    before = contract(matches.astype(bf16), earlier, 1, 0)
    place = jnp.bitwise_and(lax.broadcasted_iota(jnp.int32, (slots, token_count), 0), 1).astype(f32)
    picks = jnp.where(before == place, matches, 0.0).astype(bf16)
    picks_ref[...] = picks

    copies[2].wait()
    stacked = jnp.concatenate(
        [weight_ref[:, piece * depth : (piece + 1) * depth] for piece in range(slices)], axis=0
    )
    shape = (slots, slices * own_features)
    row = lax.broadcasted_iota(jnp.int32, shape, 0)
    column = lax.broadcasted_iota(jnp.int32, shape, 1)
    device = lax.shift_right_logical(row, 1)
    z, y = lax.shift_right_logical(device, 4), jnp.bitwise_and(lax.shift_right_logical(device, 1), N_Y - 1)
    held = jnp.bitwise_and(z + 2 * y, CLASSES - 1) * N_C + jnp.bitwise_and(device, 1)
    first = held * own_features + jnp.bitwise_and(row, 1) * FOLD
    for k in range(FOLD):
        chosen = (column == first + k).astype(f32).astype(bf16)
        start = width + features + k * depth
        out_ref[:, :, start : start + depth] = paired(contract(chosen, stacked, 1, 0).astype(bf16))

    copies[3].wait()
    out_ref[:, :, width : width + features] = paired(contract(picks, grads_ref[...], 1, 0).astype(bf16))
    copies[4].wait()
    for start in range(0, width, CHUNK):
        at = pl.ds(start, CHUNK)
        out_ref[:, :, at] = paired(contract(picks, tokens_ref[:, at], 1, 0).astype(bf16))


def order_kernel(across_ref, own_ref, a_ref, b_ref, c_ref, out_ref, canonical_ref):
    parts, _, features = canonical_ref.shape
    for shift, grads_ref in enumerate((own_ref, a_ref, b_ref, c_ref)):
        canonical_ref[lax.rem(across_ref[0] + parts - shift, parts)] = grads_ref[...]
    rows = out_ref.shape[2]
    for k in range(FOLD):
        total = jnp.zeros(out_ref.shape[1:], f32)
        for block in range(parts):
            at = lax.broadcasted_iota(jnp.int32, (features, rows), 0) + block * features
            row = lax.broadcasted_iota(jnp.int32, (features, rows), 1)
            chosen = (at == FOLD * row + k).astype(f32).astype(bf16)
            total += contract(canonical_ref[block], chosen, 1, 0)
        out_ref[k] = total.astype(bf16)


def low_kernel(arrived_ref, down_ref, upper_ref, out_ref, weight_ref):
    width = down_ref.shape[1]
    features = upper_ref.shape[1]
    hidden = jnp.zeros((weight_ref.shape[0], down_ref.shape[0]), f32)
    for start in range(0, width, CHUNK):
        at = pl.ds(start, CHUNK)
        hidden += contract(flat(arrived_ref[:, :, at]), down_ref[:, at], 1, 1)
    signal = contract(flat(arrived_ref[:, :, width : width + features]), upper_ref[...], 1, 1)
    low = jnp.concatenate([hidden, signal], axis=1)
    for part in range(out_ref.shape[0]):
        out_ref[part] = low
    weight_ref[...] = flat(arrived_ref[:, :, width + features :])


def back_kernel(parts_ref, down_ref, upper_ref, low_ref, out_ref):
    rank, width = down_ref.shape
    total = parts_ref[0]
    for part in range(1, parts_ref.shape[0]):
        total = total + parts_ref[part]
    low = total.astype(bf16)
    low_ref[...] = low
    for start in range(0, width, CHUNK):
        at = pl.ds(start, CHUNK)
        out_ref[:, :, at] = paired(
            (adapter_scale * contract(low[:, rank:], down_ref[:, at], 1, 0)).astype(bf16)
        )
    out_ref[:, :, width:] = paired(
        (adapter_scale * contract(low[:, :rank], upper_ref[...], 1, 0)).astype(bf16)
    )


def factor_kernel(arrived_ref, low_ref, down_out_ref, upper_out_ref):
    rank, width = down_out_ref.shape
    features = upper_out_ref.shape[1]
    low = low_ref[...]
    for start in range(0, width, CHUNK):
        at = pl.ds(start, CHUNK)
        down_out_ref[:, at] = adapter_scale * contract(low[:, rank:], flat(arrived_ref[:, :, at]), 0, 0)
    upper_out_ref[...] = adapter_scale * contract(
        low[:, :rank], flat(arrived_ref[:, :, width : width + features]), 0, 0
    )


def finish_kernel(picks_ref, returned_ref, input_ref, own_ref, a_ref, b_ref, c_ref, out_ref, grad_ref):
    width = input_ref.shape[1]
    picks = picks_ref[...]
    for start in range(0, width, CHUNK):
        at = pl.ds(start, CHUNK)
        grad_ref[:, at] = (
            input_ref[:, at] + contract(picks, flat(returned_ref[:, :, at]), 0, 0)
        ).astype(bf16)
    base = own_ref[...] + a_ref[...] + b_ref[...] + c_ref[...]
    out_ref[...] = (base + contract(picks, flat(returned_ref[:, :, width:]), 0, 0)).astype(bf16)


def stack_kernel(*refs):
    for at, ref in enumerate(refs[:-1]):
        refs[-1][at] = ref[...]


def base_kernel(order_ref, tokens_ref, grads_ref, own_ref, other_ref, *refs):
    input_ref, *forward_refs, whole_ref = refs
    parts, _, features = whole_ref.shape
    rows, depth = own_ref.shape[1], own_ref.shape[2] // FOLD
    totals = [jnp.zeros((tokens_ref.shape[0], rows), f32) for _ in range(FOLD)]
    for step in range(2 * CLASSES):
        weight_ref = own_ref if step < CLASSES else other_ref
        at = pl.ds(pl.multiple_of(order_ref[step] * depth, depth), depth)
        part = tokens_ref[:, at]
        total = jnp.zeros((tokens_ref.shape[0], depth), f32)
        for k in range(FOLD):
            weight = weight_ref[step % CLASSES, :, k * depth : (k + 1) * depth]
            totals[k] += contract(part, weight, 1, 1)
            total += contract(grads_ref[k], weight, 1, 0)
        input_ref[:, at] = total
    for block in range(parts):
        total = jnp.zeros(whole_ref.shape[1:], f32)
        for k in range(FOLD):
            at = lax.broadcasted_iota(jnp.int32, (rows, features), 1) + block * features
            row = lax.broadcasted_iota(jnp.int32, (rows, features), 0)
            chosen = (at == FOLD * row + k).astype(f32).astype(bf16)
            rest = totals[k]
            for _ in range(3):
                term = rest.astype(bf16)
                total += contract(term, chosen, 1, 0)
                rest = rest - term.astype(f32)
        whole_ref[block] = total
    for shift, forward_ref in enumerate(forward_refs):
        forward_ref[...] = whole_ref[lax.rem(order_ref[2 * CLASSES] + shift, parts)]


def neighbour(value, dz, dy):
    pairs = []
    for z in range(N_Z):
        for y in range(N_Y):
            for core in range(N_C):
                target = ((z + dz) % N_Z) * N_Y + (y + dy) % N_Y
                pairs.append(((z * N_Y + y) * N_C + core, target * N_C + core))
    return lax.ppermute(value, "dp", pairs)


def other_core(value):
    return lax.ppermute(value, "dp", [(i, i ^ 1) for i in range(N_Z * N_Y * N_C)])


def body(
    tokens,
    fixed_value_weight,
    output_gradient,
    adapter_down_factor,
    adapter_up_factor,
    adapter_per_token,
    adapter_owner_index,
):
    owners = lax.axis_size("dp")
    parts = lax.axis_size("mp")
    token_count, width = tokens.shape
    features = output_gradient.shape[1]
    rank = adapter_down_factor.shape[2]
    adapters = adapter_owner_index.shape[0]
    capacity = 2
    slots = owners * capacity
    own_features = fixed_value_weight.shape[1]
    slices = CLASSES * N_C
    depth = width // slices
    carried = own_features * depth // capacity
    columns = width + features + carried
    all_features = owners * own_features

    me = lax.axis_index("dp")
    z, y, core = me // (N_Y * N_C), (me // N_C) % N_Y, me % N_C
    across = lax.axis_index("mp")
    down = adapter_down_factor[0].T
    upper = adapter_up_factor[0]
    hbm = pl.BlockSpec(memory_space=pltpu.HBM)
    vmem = pl.BlockSpec(memory_space=pltpu.VMEM)
    smem = pl.BlockSpec(memory_space=pltpu.SMEM)

    def around(value, shift):
        return lax.ppermute(value, "mp", [(i, (i + shift) % parts) for i in range(parts)])

    grads = [output_gradient] + [around(output_gradient, shift) for shift in range(1, parts)]

    outgoing, picks = call(
        spread_kernel,
        (
            jax.ShapeDtypeStruct((owners, capacity, columns), bf16),
            jax.ShapeDtypeStruct((slots, token_count), bf16),
        ),
        "spread",
        2 * slots * token_count * columns,
        2 * (slots + token_count) * columns,
        limit=62 * 1024 * 1024,
        in_specs=[hbm] * 5,
        out_specs=(vmem, vmem),
        scratch_shapes=[
            pltpu.VMEM((1, token_count), jnp.int32),
            pltpu.VMEM((1, adapters), jnp.int32),
            pltpu.VMEM(tokens.shape, bf16),
            pltpu.VMEM(output_gradient.shape, bf16),
            pltpu.VMEM((own_features, width), bf16),
            pltpu.SemaphoreType.DMA((5,)),
        ],
    )(
        adapter_per_token.reshape(1, token_count),
        adapter_owner_index.reshape(1, adapters),
        tokens,
        output_gradient,
        fixed_value_weight.T,
    )
    arrived = lax.all_to_all(outgoing, "dp", split_axis=0, concat_axis=0, tiled=True)
    whole_gradient = call(
        order_kernel,
        jax.ShapeDtypeStruct((FOLD, token_count, slots), bf16),
        "order",
        8 * token_count * features * slots * FOLD,
        8 * token_count * features,
        in_specs=[smem] + [vmem] * 4,
        out_specs=vmem,
        scratch_shapes=[pltpu.VMEM((parts, token_count, features), bf16)],
    )(across.reshape(1).astype(jnp.int32), *grads)
    down, upper, whole_gradient = lax.optimization_barrier((down, upper, whole_gradient))

    low_parts, weight = call(
        low_kernel,
        (
            jax.ShapeDtypeStruct((parts, slots, 2 * rank), f32),
            jax.ShapeDtypeStruct((slots, carried), bf16),
        ),
        "low_rank",
        2 * slots * rank * (width + features),
        2 * slots * columns,
    )(arrived, down, upper)
    low_parts = lax.all_to_all(low_parts, "mp", split_axis=0, concat_axis=0, tiled=True)
    near = (weight, neighbour(weight, 1, 0), neighbour(weight, -1, 0), neighbour(weight, 0, 1))

    low, back = call(
        back_kernel,
        (
            jax.ShapeDtypeStruct((slots, 2 * rank), bf16),
            jax.ShapeDtypeStruct((owners, capacity, width + features), bf16),
        ),
        "back",
        2 * slots * rank * (width + features),
        2 * slots * (width + features),
    )(low_parts, down, upper)
    returned = lax.all_to_all(back, "dp", split_axis=0, concat_axis=0, tiled=True)

    down_out, upper_out = call(
        factor_kernel,
        (
            jax.ShapeDtypeStruct((rank, width), f32),
            jax.ShapeDtypeStruct((rank, features), f32),
        ),
        "factor_gradients",
        2 * slots * rank * (width + features),
        6 * slots * (width + features),
    )(arrived, low)

    near = lax.optimization_barrier((back, near))[1]
    gathered = call(
        stack_kernel,
        jax.ShapeDtypeStruct((CLASSES, slots, carried), bf16),
        "stack",
        0,
        4 * CLASSES * slots * carried,
    )(*near)
    swapped = other_core(gathered)
    mine = chip_class(z, y)
    offsets = [0, CLASSES - 1, 1, 2]
    order = [(((mine + offset) % CLASSES) * N_C + core) for offset in offsets]
    order += [(((mine + offset) % CLASSES) * N_C + 1 - core) for offset in offsets]
    order = jnp.stack(order + [across]).astype(jnp.int32)
    plain_input, *forward = call(
        base_kernel,
        [jax.ShapeDtypeStruct((token_count, width), f32)]
        + [jax.ShapeDtypeStruct((token_count, features), f32)] * parts,
        "base",
        4 * token_count * width * all_features,
        2 * width * all_features,
        in_specs=[smem] + [vmem] * 4,
        out_specs=[vmem] * (parts + 1),
        scratch_shapes=[pltpu.VMEM((parts, token_count, features), f32)],
    )(order, tokens, whole_gradient, gathered, swapped)
    sums = [forward[0]] + [around(forward[shift], shift) for shift in range(1, parts)]

    projected, activation_gradient = call(
        finish_kernel,
        (
            jax.ShapeDtypeStruct((token_count, features), bf16),
            jax.ShapeDtypeStruct((token_count, width), bf16),
        ),
        "finish",
        2 * slots * token_count * (width + features),
        2 * slots * (width + features),
    )(picks, returned, plain_input, *sums)
    return (projected, activation_gradient, down_out.T[None], upper_out[None])


def solution(mesh):
    return jax.shard_map(
        body,
        mesh=mesh,
        in_specs=(
            P("dp", "mp"),
            P("mp", "dp"),
            P("dp", "mp"),
            P("dp", "mp", None),
            P("dp", None, "mp"),
            P("dp", None),
            P(),
        ),
        out_specs=(P("dp", "mp"), P("dp", "mp"), P("dp", "mp", None), P("dp", None, "mp")),
        check_vma=False,
    )
```

time: 159 us -> 137 us (0.86)
  the two profiles are of different devices: /device:TPU:88 before, /device:TPU:1 now
where the time goes in v2:
time: 137 us; the launch traced here: 136 us
  starting transfers between devices  60.9 us (44%)
  waiting for transfers between devices  41 us (30%)
  Pallas kernels  17 us (12%)
  blocking collectives  10.8 us (8%)
  local copies, waits for them, and re-layouts  5.64 us (4%)
    all_to_all x1, waiting for transfers between devices, body(): lax.all_to_all(outgoing, 'dp', split_axis=0, concat_axis=0, tiled=True)  30 us
    ppermute x6, starting transfers between devices, around(): lax.ppermute(value, 'mp', [(i, (i + shift) % parts) for i in range(parts)])  19.7 us
    all_to_all x1, starting transfers between devices, body(): lax.all_to_all(outgoing, 'dp', split_axis=0, concat_axis=0, tiled=True)  18.6 us
    all_to_all x1, blocking collectives, body(): lax.all_to_all(low_parts, 'mp', split_axis=0, concat_axis=0, tiled=True)  10.8 us
    all_to_all x1, starting transfers between devices, body(): lax.all_to_all(back, 'dp', split_axis=0, concat_axis=0, tiled=True)  10.2 us
    ppermute x3, starting transfers between devices, neighbour(): return lax.ppermute(value, 'dp', pairs)  9.61 us
    pallas_call x1, Pallas kernels, body(): call(base_kernel, [jax.ShapeDtypeStruct((token_count, width), f32)] + [ja...  6.06 us
    all_to_all x1, waiting for transfers between devices, body(): lax.all_to_all(back, 'dp', split_axis=0, concat_axis=0, tiled=True)  5.7 us
  transfers between devices with their start and end apart: 12, of which 4 were waited for; matrix products, arithmetic and copies ran while one was open for 0% of the time, Pallas kernels for 8%

profile of v2, /device:TPU:1, one launch (start us, length us, event | category | flops | bytes accessed | tf_op | source)
XLA Modules:
  0.0 136.3 jit_solution(809821267125742772)
XLA Ops:
  0.6 3.2 %spread.1 = (bf16[128,2,3328]{2,1,0:T(2,128)(2,1)}, bf16[256,128]{1,0:T(8,128)(2,1)}) custom-call(s32[1,128]{1,0:T(1,128)} %bitcast.27, s32[1,128]{1,0:T(1,128)} %bitcast.28, bf16[128,2048]{1,0:T(8,128)(2,1)} %tokens_ref.1, bf16[128,256]{1,0:T(8,128)(2,1)} %own_ref.1, bf16[8,2048]{1,0:T(8,128)(2,1)} %bitcast.26), custom_call_target="tpu_custom_call" | custom-call | flops 218103808 | bytes 2555904 | tf_op jit(solution)/shard_map/spread/pallas_call | solution.py:283
  3.8 0.0 copy-start.11
  3.8 0.0 copy-start.1
  3.8 0.0 copy-start.7
  3.9 18.6 %all-to-all-start = ((bf16[128,2,3328]{2,1,0:T(2,128)(2,1)}), bf16[128,2,3328]{2,1,0:T(2,128)(2,1)S(1)}, u32[]{:S(2)}, u32[]{:S(2)}) async-start(bf16[128,2,3328]{2,1,0:T(2,128)(2,1)} %get-tuple-element.27), calls=%async_computation | async-start | bytes 3407872 | tf_op jit(solution)/shard_map/all_to_all | solution.py:310
  22.4 0.0 copy-done.11
  22.4 4.7 %collective-permute-start.1 = (bf16[128,256]{1,0:T(8,128)(2,1)S(1)}, bf16[128,256]{1,0:T(8,128)(2,1)S(1)}, u32[]{:S(2)}, u32[]{:S(2)}) collective-permute-start(bf16[128,256]{1,0:T(8,128)(2,1)S(1)} %copy-done.11), channel_id=1, source_target_pairs={{0,2},{1,3},{2,0},{3,1},{4,6},{5,7},{6,4},{7,5},{8,10},{9,11},{10,... | collective-permute-start | bytes 196616 | tf_op jit(solution)/shard_map/ppermute | solution.py:279
  27.1 2.2 %collective-permute-start = (bf16[128,256]{1,0:T(8,128)(2,1)S(1)}, bf16[128,256]{1,0:T(8,128)(2,1)S(1)}, u32[]{:S(2)}, u32[]{:S(2)}) collective-permute-start(bf16[128,256]{1,0:T(8,128)(2,1)S(1)} %copy-done.11), channel_id=1, source_target_pairs={{0,1},{1,2},{2,3},{3,0},{4,5},{5,6},{6,7},{7,4},{8,9},{9,10},{10,1... | collective-permute-start | bytes 196616 | tf_op jit(solution)/shard_map/ppermute | solution.py:279
  29.3 4.3 %collective-permute-start.2 = (bf16[128,256]{1,0:T(8,128)(2,1)S(1)}, bf16[128,256]{1,0:T(8,128)(2,1)S(1)}, u32[]{:S(2)}, u32[]{:S(2)}) collective-permute-start(bf16[128,256]{1,0:T(8,128)(2,1)S(1)} %copy-done.11), channel_id=1, source_target_pairs={{0,3},{1,0},{2,1},{3,2},{4,7},{5,4},{6,5},{7,6},{8,11},{9,8},{10,9... | collective-permute-start | bytes 196616 | tf_op jit(solution)/shard_map/ppermute | solution.py:279
  33.6 0.0 collective-permute-done.1.b_ref
  33.6 0.0 collective-permute-done.a_ref
  33.6 1.3 collective-permute-done.2.c_ref
  34.9 0.5 order.1.grads_ref
  35.4 0.0 copy-start.5
  35.4 0.7 copy-done.5
  36.1 30.0 %all-to-all-done.arrived_ref = bf16[128,2,3328]{2,1,0:T(2,128)(2,1)S(1)} async-done(((bf16[128,2,3328]{2,1,0:T(2,128)(2,1)}), bf16[128,2,3328]{2,1,0:T(2,128)(2,1)S(1)}, u32[]{:S(2)}, u32[]{:S(2)}) %all-to-all-start) | async-done | bytes 1703968 | tf_op jit(solution)/shard_map/all_to_all | solution.py:310
  66.1 0.0 copy-done.1
  66.1 0.0 copy-done.7
  66.1 1.3 low_rank.1
  67.5 4.3 %collective-permute-start.5 = (bf16[256,1024]{1,0:T(8,128)(2,1)}, bf16[256,1024]{1,0:T(8,128)(2,1)}, u32[]{:S(2)}, u32[]{:S(2)}) collective-permute-start(bf16[256,1024]{1,0:T(8,128)(2,1)} %get-tuple-element.34.refs_0_), channel_id=1, source_target_pairs={{0,8},{4,12},{8,16},{12,20},{16,24},{20,28},{24,32},{28,36},{32,40... | collective-permute-start | bytes 1572872 | tf_op jit(solution)/shard_map/ppermute | solution.py:238
  71.8 3.0 %collective-permute-start.4 = (bf16[256,1024]{1,0:T(8,128)(2,1)}, bf16[256,1024]{1,0:T(8,128)(2,1)}, u32[]{:S(2)}, u32[]{:S(2)}) collective-permute-start(bf16[256,1024]{1,0:T(8,128)(2,1)} %get-tuple-element.34.refs_0_), channel_id=1, source_target_pairs={{0,448},{4,452},{8,456},{12,460},{16,464},{20,468},{24,472},{28,47... | collective-permute-start | bytes 1572872 | tf_op jit(solution)/shard_map/ppermute | solution.py:238
  74.8 2.3 %collective-permute-start.3 = (bf16[256,1024]{1,0:T(8,128)(2,1)}, bf16[256,1024]{1,0:T(8,128)(2,1)}, u32[]{:S(2)}, u32[]{:S(2)}) collective-permute-start(bf16[256,1024]{1,0:T(8,128)(2,1)} %get-tuple-element.34.refs_0_), channel_id=1, source_target_pairs={{0,64},{4,68},{8,72},{12,76},{16,80},{20,84},{24,88},{28,92},{32,9... | collective-permute-start | bytes 1572872 | tf_op jit(solution)/shard_map/ppermute | solution.py:238
  77.1 10.8 %all_to_all.15.parts_ref = f32[4,256,128]{2,1,0:T(8,128)S(1)} all-to-all(f32[4,256,128]{2,1,0:T(8,128)S(1)} %get-tuple-element.30), channel_id=1, replica_groups=mesh['dp'=128,'mp'=4] {'mp'}, dimensions={0} | all-to-all | bytes 1048576 | tf_op jit(solution)/shard_map/all_to_all | solution.py:333
  87.9 0.5 back.1
  88.5 1.0 copy-done
  89.5 0.6 copy-done.8
  90.1 10.2 %all-to-all-start.2 = ((bf16[128,2,2304]{2,1,0:T(2,128)(2,1)}), bf16[128,2,2304]{2,1,0:T(2,128)(2,1)S(1)}, u32[]{:S(2)}, u32[]{:S(2)}) async-start(bf16[128,2,2304]{2,1,0:T(2,128)(2,1)} %copy-done), calls=%async_computation.2 | async-start | bytes 2359296 | tf_op jit(solution)/shard_map/all_to_all | solution.py:346
  100.4 0.0 copy-start.4
  100.4 0.0 collective-permute-done.5.refs_3_
  100.4 0.0 collective-permute-done.4.refs_2_
  100.4 0.0 collective-permute-done.3.refs_1_
  100.4 3.1 %stack.38.own_ref = bf16[4,256,1024]{2,1,0:T(8,128)(2,1)} custom-call(bf16[256,1024]{1,0:T(8,128)(2,1)} %get-tuple-element.34.refs_0_, bf16[256,1024]{1,0:T(8,128)(2,1)} %collective-permute-done.3.refs_1_, bf16[256,1024]{1,0:T(8,128)(2,1)} %collective-permute-done.4.refs_2_, bf16[256,1024]{1,0:T(8,128)(2,1)} %collective-permute-done.5.refs_3_), custom_call_target="tpu_custom_call" | custom-call | bytes 4194304 | tf_op jit(solution)/shard_map/stack/pallas_call | solution.py:360
  103.5 2.8 %collective-permute-start.6 = (bf16[4,256,1024]{2,1,0:T(8,128)(2,1)}, bf16[4,256,1024]{2,1,0:T(8,128)(2,1)}, u32[]{:S(2)}, u32[]{:S(2)}) collective-permute-start(bf16[4,256,1024]{2,1,0:T(8,128)(2,1)} %stack.38.own_ref), channel_id=1, source_target_pairs={{0,4},{4,0},{8,12},{12,8},{16,20},{20,16},{24,28},{28,24},{32,36},... | collective-permute-start | bytes 6291464 | tf_op jit(solution)/shard_map/ppermute | solution.py:242
  106.4 0.1 stack.37.order_ref
  106.5 3.9 %collective-permute-done.6.other_ref = bf16[4,256,1024]{2,1,0:T(8,128)(2,1)} collective-permute-done((bf16[4,256,1024]{2,1,0:T(8,128)(2,1)}, bf16[4,256,1024]{2,1,0:T(8,128)(2,1)}, u32[]{:S(2)}, u32[]{:S(2)}) %collective-permute-start.6) | collective-permute-done | bytes 2097184 | tf_op jit(solution)/shard_map/ppermute | solution.py:242
  110.4 0.9 copy-done.6
  111.3 6.1 %base.1 = (f32[128,2048]{1,0:T(8,128)S(1)}, f32[128,256]{1,0:T(8,128)S(1)}, f32[128,256]{1,0:T(8,128)}, f32[128,256]{1,0:T(8,128)}, f32[128,256]{1,0:T(8,128)}) custom-call(s32[9]{0:T(128)S(1)} %stack.37.order_ref, bf16[128,2048]{1,0:T(8,128)(2,1)S(1)} %copy-done.4, bf16[4,128,256]{2,1,0:T(8,128)(2,1)S(1)} %copy-done.6, ...), custom_call_target="tpu_custom_call" | custom-call | flops 1073741824 | bytes 4194304 | tf_op jit(solution)/shard_map/base/pallas_call | solution.py:373
  117.4 1.0 copy-done.2
  118.4 2.3 %collective-permute-start.7 = (f32[128,256]{1,0:T(8,128)}, f32[128,256]{1,0:T(8,128)S(1)}, u32[]{:S(2)}, u32[]{:S(2)}) collective-permute-start(f32[128,256]{1,0:T(8,128)} %get-tuple-element.40), channel_id=1, source_target_pairs={{0,1},{1,2},{2,3},{3,0},{4,5},{5,6},{6,7},{7,4},{8,9},{9,10},{10,1... | collective-permute-start | bytes 393224 | tf_op jit(solution)/shard_map/ppermute | solution.py:279
  120.7 3.7 %collective-permute-start.8 = (f32[128,256]{1,0:T(8,128)}, f32[128,256]{1,0:T(8,128)S(1)}, u32[]{:S(2)}, u32[]{:S(2)}) collective-permute-start(f32[128,256]{1,0:T(8,128)} %get-tuple-element.41), channel_id=1, source_target_pairs={{0,2},{1,3},{2,0},{3,1},{4,6},{5,7},{6,4},{7,5},{8,10},{9,11},{10,... | collective-permute-start | bytes 393224 | tf_op jit(solution)/shard_map/ppermute | solution.py:279
  124.4 2.5 %collective-permute-start.9 = (f32[128,256]{1,0:T(8,128)}, f32[128,256]{1,0:T(8,128)S(1)}, u32[]{:S(2)}, u32[]{:S(2)}) collective-permute-start(f32[128,256]{1,0:T(8,128)} %get-tuple-element.42), channel_id=1, source_target_pairs={{0,3},{1,0},{2,1},{3,2},{4,7},{5,4},{6,5},{7,6},{8,11},{9,8},{10,9... | collective-permute-start | bytes 393224 | tf_op jit(solution)/shard_map/ppermute | solution.py:279
  127.0 1.2 factor_gradients.1
  128.2 5.7 %all-to-all-done.2.returned_ref = bf16[128,2,2304]{2,1,0:T(2,128)(2,1)S(1)} async-done(((bf16[128,2,2304]{2,1,0:T(2,128)(2,1)}), bf16[128,2,2304]{2,1,0:T(2,128)(2,1)S(1)}, u32[]{:S(2)}, u32[]{:S(2)}) %all-to-all-start.2) | async-done | bytes 1179680 | tf_op jit(solution)/shard_map/all_to_all | solution.py:346
  133.9 0.0 collective-permute-done.7.a_ref
  133.9 0.0 collective-permute-done.8.b_ref
  133.9 0.0 collective-permute-done.9.c_ref
  133.9 1.2 copy-done.3
  135.1 1.2 finish.1
  (10 shorter events, 0.0 us)
Async XLA Ops:
  3.8 18.6 %copy-start.11 = (bf16[128,256]{1,0:T(8,128)(2,1)S(1)}, bf16[128,256]{1,0:T(8,128)(2,1)}, u32[]{:S(2)}) copy-start(bf16[128,256]{1,0:T(8,128)(2,1)} %own_ref.1) | copy-start | bytes 196612
  3.8 62.3 %copy-start.1 = (bf16[1,2048,64]{1,2,0:T(8,128)(2,1)S(1)}, bf16[1,2048,64]{1,2,0:T(8,128)(2,1)}, u32[]{:S(2)}) copy-start(bf16[1,2048,64]{1,2,0:T(8,128)(2,1)} %param.10) | copy-start | bytes 786436
  3.8 62.3 %copy-start.7 = (bf16[1,64,256]{2,1,0:T(8,128)(2,1)S(1)}, bf16[1,64,256]{2,1,0:T(8,128)(2,1)}, u32[]{:S(2)}) copy-start(bf16[1,64,256]{2,1,0:T(8,128)(2,1)} %param.11) | copy-start | bytes 98308
  3.9 62.3 %all-to-all-start = ((bf16[128,2,3328]{2,1,0:T(2,128)(2,1)}), bf16[128,2,3328]{2,1,0:T(2,128)(2,1)S(1)}, u32[]{:S(2)}, u32[]{:S(2)}) async-start(bf16[128,2,3328]{2,1,0:T(2,128)(2,1)} %get-tuple-element.27), calls=%async_computation | async-start | bytes 3407872 | tf_op jit(solution)/shard_map/all_to_all | solution.py:310
  22.4 11.2 %collective-permute-start.1 = (bf16[128,256]{1,0:T(8,128)(2,1)S(1)}, bf16[128,256]{1,0:T(8,128)(2,1)S(1)}, u32[]{:S(2)}, u32[]{:S(2)}) collective-permute-start(bf16[128,256]{1,0:T(8,128)(2,1)S(1)} %copy-done.11), channel_id=1, source_target_pairs={{0,2},{1,3},{2,0},{3,1},{4,6},{5,7},{6,4},{7,5},{8,10},{9,11},{10,... | collective-permute-start | bytes 196616 | tf_op jit(solution)/shard_map/ppermute | solution.py:279
  27.1 6.5 %collective-permute-start = (bf16[128,256]{1,0:T(8,128)(2,1)S(1)}, bf16[128,256]{1,0:T(8,128)(2,1)S(1)}, u32[]{:S(2)}, u32[]{:S(2)}) collective-permute-start(bf16[128,256]{1,0:T(8,128)(2,1)S(1)} %copy-done.11), channel_id=1, source_target_pairs={{0,1},{1,2},{2,3},{3,0},{4,5},{5,6},{6,7},{7,4},{8,9},{9,10},{10,1... | collective-permute-start | bytes 196616 | tf_op jit(solution)/shard_map/ppermute | solution.py:279
  29.3 5.6 %collective-permute-start.2 = (bf16[128,256]{1,0:T(8,128)(2,1)S(1)}, bf16[128,256]{1,0:T(8,128)(2,1)S(1)}, u32[]{:S(2)}, u32[]{:S(2)}) collective-permute-start(bf16[128,256]{1,0:T(8,128)(2,1)S(1)} %copy-done.11), channel_id=1, source_target_pairs={{0,3},{1,0},{2,1},{3,2},{4,7},{5,4},{6,5},{7,6},{8,11},{9,8},{10,9... | collective-permute-start | bytes 196616 | tf_op jit(solution)/shard_map/ppermute | solution.py:279
  35.4 0.7 copy-start.5
  67.5 33.0 %collective-permute-start.5 = (bf16[256,1024]{1,0:T(8,128)(2,1)}, bf16[256,1024]{1,0:T(8,128)(2,1)}, u32[]{:S(2)}, u32[]{:S(2)}) collective-permute-start(bf16[256,1024]{1,0:T(8,128)(2,1)} %get-tuple-element.34.refs_0_), channel_id=1, source_target_pairs={{0,8},{4,12},{8,16},{12,20},{16,24},{20,28},{24,32},{28,36},{32,40... | collective-permute-start | bytes 1572872 | tf_op jit(solution)/shard_map/ppermute | solution.py:238
  71.8 28.6 %collective-permute-start.4 = (bf16[256,1024]{1,0:T(8,128)(2,1)}, bf16[256,1024]{1,0:T(8,128)(2,1)}, u32[]{:S(2)}, u32[]{:S(2)}) collective-permute-start(bf16[256,1024]{1,0:T(8,128)(2,1)} %get-tuple-element.34.refs_0_), channel_id=1, source_target_pairs={{0,448},{4,452},{8,456},{12,460},{16,464},{20,468},{24,472},{28,47... | collective-permute-start | bytes 1572872 | tf_op jit(solution)/shard_map/ppermute | solution.py:238
  74.8 25.6 %collective-permute-start.3 = (bf16[256,1024]{1,0:T(8,128)(2,1)}, bf16[256,1024]{1,0:T(8,128)(2,1)}, u32[]{:S(2)}, u32[]{:S(2)}) collective-permute-start(bf16[256,1024]{1,0:T(8,128)(2,1)} %get-tuple-element.34.refs_0_), channel_id=1, source_target_pairs={{0,64},{4,68},{8,72},{12,76},{16,80},{20,84},{24,88},{28,92},{32,9... | collective-permute-start | bytes 1572872 | tf_op jit(solution)/shard_map/ppermute | solution.py:238
  88.5 1.1 copy-start
  89.5 0.6 copy-start.8
  90.1 43.7 %all-to-all-start.2 = ((bf16[128,2,2304]{2,1,0:T(2,128)(2,1)}), bf16[128,2,2304]{2,1,0:T(2,128)(2,1)S(1)}, u32[]{:S(2)}, u32[]{:S(2)}) async-start(bf16[128,2,2304]{2,1,0:T(2,128)(2,1)} %copy-done), calls=%async_computation.2 | async-start | bytes 2359296 | tf_op jit(solution)/shard_map/all_to_all | solution.py:346
  100.4 10.0 %copy-start.4 = (bf16[128,2048]{1,0:T(8,128)(2,1)S(1)}, bf16[128,2048]{1,0:T(8,128)(2,1)}, u32[]{:S(2)}) copy-start(bf16[128,2048]{1,0:T(8,128)(2,1)} %tokens_ref.1) | copy-start | bytes 1572868
  103.5 6.9 %collective-permute-start.6 = (bf16[4,256,1024]{2,1,0:T(8,128)(2,1)}, bf16[4,256,1024]{2,1,0:T(8,128)(2,1)}, u32[]{:S(2)}, u32[]{:S(2)}) collective-permute-start(bf16[4,256,1024]{2,1,0:T(8,128)(2,1)} %stack.38.own_ref), channel_id=1, source_target_pairs={{0,4},{4,0},{8,12},{12,8},{16,20},{20,16},{24,28},{28,24},{32,36},... | collective-permute-start | bytes 6291464 | tf_op jit(solution)/shard_map/ppermute | solution.py:242
  110.4 1.0 copy-start.6
  111.3 15.6 %copy-start.9 = (bf16[256,128]{1,0:T(8,128)(2,1)S(1)}, bf16[256,128]{1,0:T(8,128)(2,1)}, u32[]{:S(2)}) copy-start(bf16[256,128]{1,0:T(8,128)(2,1)} %copy-done.8) | copy-start | bytes 196612
  117.4 1.0 copy-start.2
  118.4 15.5 %copy-start.10 = (bf16[256,128]{1,0:T(8,128)(2,1)S(1)}, bf16[256,128]{1,0:T(8,128)(2,1)}, u32[]{:S(2)}) copy-start(bf16[256,128]{1,0:T(8,128)(2,1)} %get-tuple-element.26.picks_ref) | copy-start | bytes 196612
  118.4 15.5 %collective-permute-start.7 = (f32[128,256]{1,0:T(8,128)}, f32[128,256]{1,0:T(8,128)S(1)}, u32[]{:S(2)}, u32[]{:S(2)}) collective-permute-start(f32[128,256]{1,0:T(8,128)} %get-tuple-element.40), channel_id=1, source_target_pairs={{0,1},{1,2},{2,3},{3,0},{4,5},{5,6},{6,7},{7,4},{8,9},{9,10},{10,1... | collective-permute-start | bytes 393224 | tf_op jit(solution)/shard_map/ppermute | solution.py:279
  120.7 13.2 %collective-permute-start.8 = (f32[128,256]{1,0:T(8,128)}, f32[128,256]{1,0:T(8,128)S(1)}, u32[]{:S(2)}, u32[]{:S(2)}) collective-permute-start(f32[128,256]{1,0:T(8,128)} %get-tuple-element.41), channel_id=1, source_target_pairs={{0,2},{1,3},{2,0},{3,1},{4,6},{5,7},{6,4},{7,5},{8,10},{9,11},{10,... | collective-permute-start | bytes 393224 | tf_op jit(solution)/shard_map/ppermute | solution.py:279
  124.4 9.5 %collective-permute-start.9 = (f32[128,256]{1,0:T(8,128)}, f32[128,256]{1,0:T(8,128)S(1)}, u32[]{:S(2)}, u32[]{:S(2)}) collective-permute-start(f32[128,256]{1,0:T(8,128)} %get-tuple-element.42), channel_id=1, source_target_pairs={{0,3},{1,0},{2,1},{3,2},{4,7},{5,4},{6,5},{7,6},{8,11},{9,8},{10,9... | collective-permute-start | bytes 393224 | tf_op jit(solution)/shard_map/ppermute | solution.py:279
  133.9 1.2 copy-start.3

commit v3 on v2

--- a/solution.py
+++ b/solution.py
@@ -8,12 +8,14 @@
 adapter_scale = 0.5
 f32 = jnp.float32
 bf16 = jnp.bfloat16
-VMEM_LIMIT = 48 * 1024 * 1024
+VMEM_LIMIT = 16 * 1024 * 1024
 
 N_Z, N_Y, N_C = 8, 8, 2
 CLASSES = 4
 FOLD = 4
 CHUNK = 512
+WHOLE_VMEM = 62 * 1024 * 1024
+LONG = 100 * 1024 * 1024
 
 
 def chip_class(z, y):
@@ -51,6 +53,8 @@
     tokens_hbm,
     grads_hbm,
     weight_hbm,
+    out_hbm,
+    picks_hbm,
     out_ref,
     picks_ref,
     adapter_ref,
@@ -59,6 +63,7 @@
     grads_ref,
     weight_ref,
     sems,
+    out_sems,
 ):
     copies = [
         pltpu.make_async_copy(source, target, sems.at[at])
@@ -97,6 +102,14 @@
     place = jnp.bitwise_and(lax.broadcasted_iota(jnp.int32, (slots, token_count), 0), 1).astype(f32)
     picks = jnp.where(before == place, matches, 0.0).astype(bf16)
     picks_ref[...] = picks
+    stores = []
+
+    def store(source, target):
+        copy = pltpu.make_async_copy(source, target, out_sems.at[len(stores)])
+        copy.start()
+        stores.append(copy)
+
+    store(picks_ref, picks_hbm)
 
     copies[2].wait()
     stacked = jnp.concatenate(
@@ -114,12 +127,19 @@
         start = width + features + k * depth
         out_ref[:, :, start : start + depth] = paired(contract(chosen, stacked, 1, 0).astype(bf16))
 
+    at = pl.ds(width + features, out_ref.shape[2] - width - features)
+    store(out_ref.at[:, :, at], out_hbm.at[:, :, at])
     copies[3].wait()
     out_ref[:, :, width : width + features] = paired(contract(picks, grads_ref[...], 1, 0).astype(bf16))
     copies[4].wait()
     for start in range(0, width, CHUNK):
         at = pl.ds(start, CHUNK)
         out_ref[:, :, at] = paired(contract(picks, tokens_ref[:, at], 1, 0).astype(bf16))
+        if start + CHUNK == width:
+            at = pl.ds(start, CHUNK + features)
+        store(out_ref.at[:, :, at], out_hbm.at[:, :, at])
+    for copy in stores:
+        copy.wait()
 
 
 def order_kernel(across_ref, own_ref, a_ref, b_ref, c_ref, out_ref, canonical_ref):
@@ -137,10 +157,10 @@
         out_ref[k] = total.astype(bf16)
 
 
-def low_kernel(arrived_ref, down_ref, upper_ref, out_ref, weight_ref):
+def low_kernel(arrived_ref, down_ref, upper_ref, out_ref):
     width = down_ref.shape[1]
     features = upper_ref.shape[1]
-    hidden = jnp.zeros((weight_ref.shape[0], down_ref.shape[0]), f32)
+    hidden = jnp.zeros((out_ref.shape[1], down_ref.shape[0]), f32)
     for start in range(0, width, CHUNK):
         at = pl.ds(start, CHUNK)
         hidden += contract(flat(arrived_ref[:, :, at]), down_ref[:, at], 1, 1)
@@ -148,24 +168,35 @@
     low = jnp.concatenate([hidden, signal], axis=1)
     for part in range(out_ref.shape[0]):
         out_ref[part] = low
-    weight_ref[...] = flat(arrived_ref[:, :, width + features :])
-
-
-def back_kernel(parts_ref, down_ref, upper_ref, low_ref, out_ref):
+
+
+def weight_kernel(arrived_ref, out_ref):
+    out_ref[...] = flat(arrived_ref[:, :, arrived_ref.shape[2] - out_ref.shape[1] :])
+
+
+def back_kernel(parts_ref, down_ref, upper_ref, low_hbm, out_hbm, low_ref, out_ref, sems):
     rank, width = down_ref.shape
     total = parts_ref[0]
     for part in range(1, parts_ref.shape[0]):
         total = total + parts_ref[part]
     low = total.astype(bf16)
     low_ref[...] = low
+    stores = [pltpu.make_async_copy(low_ref, low_hbm, sems.at[0])]
+    stores[0].start()
     for start in range(0, width, CHUNK):
         at = pl.ds(start, CHUNK)
         out_ref[:, :, at] = paired(
             (adapter_scale * contract(low[:, rank:], down_ref[:, at], 1, 0)).astype(bf16)
         )
-    out_ref[:, :, width:] = paired(
-        (adapter_scale * contract(low[:, :rank], upper_ref[...], 1, 0)).astype(bf16)
-    )
+        if start + CHUNK == width:
+            at = pl.ds(start, out_ref.shape[2] - start)
+            out_ref[:, :, width:] = paired(
+                (adapter_scale * contract(low[:, :rank], upper_ref[...], 1, 0)).astype(bf16)
+            )
+        stores.append(pltpu.make_async_copy(out_ref.at[:, :, at], out_hbm.at[:, :, at], sems.at[len(stores)]))
+        stores[-1].start()
+    for store in stores:
+        store.wait()
 
 
 def factor_kernel(arrived_ref, low_ref, down_out_ref, upper_out_ref):
@@ -180,16 +211,47 @@
     )
 
 
-def finish_kernel(picks_ref, returned_ref, input_ref, own_ref, a_ref, b_ref, c_ref, out_ref, grad_ref):
-    width = input_ref.shape[1]
+def finish_kernel(order_ref, picks_hbm, returned_hbm, mine_hbm, other_hbm, *refs):
+    *part_hbm, out_hbm, grad_hbm = refs[:-8]
+    picks_ref, returned_ref, input_ref, part_ref, out_ref, grad_ref, in_sems, out_sems = refs[-8:]
+    classes, _, depth = mine_hbm.shape
+    width = grad_ref.shape[1]
+    sources = [(picks_hbm, picks_ref)]
+    for at in range(2 * classes):
+        half = mine_hbm if at < classes else other_hbm
+        sources.append((half.at[at % classes], input_ref.at[:, columns_of(order_ref, at, depth)]))
+    early = len(sources)
+    chunks = [pl.ds(start, CHUNK) for start in range(0, width, CHUNK)]
+    for columns in chunks + [pl.ds(width, returned_ref.shape[2] - width)]:
+        sources.append((returned_hbm.at[:, :, columns], returned_ref.at[:, :, columns]))
+    for at, source in enumerate(part_hbm):
+        sources.append((source, part_ref.at[at]))
+    copies = [
+        pltpu.make_async_copy(source, target, in_sems.at[at]) for at, (source, target) in enumerate(sources)
+    ]
+    for copy in copies:
+        copy.start()
+    for copy in copies[:early]:
+        copy.wait()
     picks = picks_ref[...]
-    for start in range(0, width, CHUNK):
-        at = pl.ds(start, CHUNK)
-        grad_ref[:, at] = (
-            input_ref[:, at] + contract(picks, flat(returned_ref[:, :, at]), 0, 0)
+    stores = []
+    for at, columns in enumerate(chunks):
+        copies[early + at].wait()
+        grad_ref[:, columns] = (
+            input_ref[:, columns] + contract(picks, flat(returned_ref[:, :, columns]), 0, 0)
         ).astype(bf16)
-    base = own_ref[...] + a_ref[...] + b_ref[...] + c_ref[...]
+        stores.append(pltpu.make_async_copy(grad_ref.at[:, columns], grad_hbm.at[:, columns], out_sems.at[at]))
+        stores[-1].start()
+    for copy in copies[early + len(chunks) :]:
+        copy.wait()
+    base = part_ref[0]
+    for at in range(1, len(part_hbm)):
+        base = base + part_ref[at]
     out_ref[...] = (base + contract(picks, flat(returned_ref[:, :, width:]), 0, 0)).astype(bf16)
+    stores.append(pltpu.make_async_copy(out_ref, out_hbm, out_sems.at[len(chunks)]))
+    stores[-1].start()
+    for store in stores:
+        store.wait()
 
 
 def stack_kernel(*refs):
@@ -197,35 +259,61 @@
         refs[-1][at] = ref[...]
 
 
-def base_kernel(order_ref, tokens_ref, grads_ref, own_ref, other_ref, *refs):
-    input_ref, *forward_refs, whole_ref = refs
+def columns_of(order_ref, at, depth):
+    return pl.ds(pl.multiple_of(order_ref[at] * depth, depth), depth)
+
+
+def forward_half(order_ref, first, tokens_ref, weight_ref):
+    classes, rows, carried = weight_ref.shape
+    depth = carried // FOLD
+    totals = [jnp.zeros((tokens_ref.shape[0], rows), f32) for _ in range(FOLD)]
+    for at in range(classes):
+        part = tokens_ref[:, columns_of(order_ref, first + at, depth)]
+        for k in range(FOLD):
+            totals[k] += contract(part, weight_ref[at, :, k * depth : (k + 1) * depth], 1, 1)
+    return totals
+
+
+def input_half(grads_ref, weight_ref, input_ref):
+    classes, _, carried = weight_ref.shape
+    depth = carried // FOLD
+    for at in range(classes):
+        total = contract(grads_ref[0], weight_ref[at, :, :depth], 1, 0)
+        for k in range(1, FOLD):
+            total += contract(grads_ref[k], weight_ref[at, :, k * depth : (k + 1) * depth], 1, 0)
+        input_ref[at] = total
+
+
+def own_kernel(order_ref, tokens_ref, grads_ref, weight_ref, totals_ref, input_ref):
+    for k, total in enumerate(forward_half(order_ref, 0, tokens_ref, weight_ref)):
+        totals_ref[k] = total
+    input_half(grads_ref, weight_ref, input_ref)
+
+
+def forward_kernel(order_ref, tokens_ref, totals_ref, weight_ref, *refs):
+    *forward_refs, whole_ref = refs
     parts, _, features = whole_ref.shape
-    rows, depth = own_ref.shape[1], own_ref.shape[2] // FOLD
-    totals = [jnp.zeros((tokens_ref.shape[0], rows), f32) for _ in range(FOLD)]
-    for step in range(2 * CLASSES):
-        weight_ref = own_ref if step < CLASSES else other_ref
-        at = pl.ds(pl.multiple_of(order_ref[step] * depth, depth), depth)
-        part = tokens_ref[:, at]
-        total = jnp.zeros((tokens_ref.shape[0], depth), f32)
-        for k in range(FOLD):
-            weight = weight_ref[step % CLASSES, :, k * depth : (k + 1) * depth]
-            totals[k] += contract(part, weight, 1, 1)
-            total += contract(grads_ref[k], weight, 1, 0)
-        input_ref[:, at] = total
+    totals = forward_half(order_ref, CLASSES, tokens_ref, weight_ref)
+    rows = totals[0].shape[1]
+    terms = []
+    for k in range(FOLD):
+        rest = totals[k] + totals_ref[k]
+        for _ in range(3):
+            terms.append((k, rest.astype(bf16)))
+            rest = rest - terms[-1][1].astype(f32)
     for block in range(parts):
+        at = lax.broadcasted_iota(jnp.int32, (rows, features), 1) + block * features
+        row = lax.broadcasted_iota(jnp.int32, (rows, features), 0)
         total = jnp.zeros(whole_ref.shape[1:], f32)
-        for k in range(FOLD):
-            at = lax.broadcasted_iota(jnp.int32, (rows, features), 1) + block * features
-            row = lax.broadcasted_iota(jnp.int32, (rows, features), 0)
-            chosen = (at == FOLD * row + k).astype(f32).astype(bf16)
-            rest = totals[k]
-            for _ in range(3):
-                term = rest.astype(bf16)
-                total += contract(term, chosen, 1, 0)
-                rest = rest - term.astype(f32)
+        for k, term in terms:
+            total += contract(term, (at == FOLD * row + k).astype(f32).astype(bf16), 1, 0)
         whole_ref[block] = total
     for shift, forward_ref in enumerate(forward_refs):
         forward_ref[...] = whole_ref[lax.rem(order_ref[2 * CLASSES] + shift, parts)]
+
+
+def input_kernel(grads_ref, weight_ref, input_ref):
+    input_half(grads_ref, weight_ref, input_ref)
 
 
 def neighbour(value, dz, dy):
@@ -289,16 +377,19 @@
         "spread",
         2 * slots * token_count * columns,
         2 * (slots + token_count) * columns,
-        limit=62 * 1024 * 1024,
+        limit=WHOLE_VMEM,
         in_specs=[hbm] * 5,
-        out_specs=(vmem, vmem),
+        out_specs=(hbm, hbm),
         scratch_shapes=[
+            pltpu.VMEM((owners, capacity, columns), bf16),
+            pltpu.VMEM((slots, token_count), bf16),
             pltpu.VMEM((1, token_count), jnp.int32),
             pltpu.VMEM((1, adapters), jnp.int32),
             pltpu.VMEM(tokens.shape, bf16),
             pltpu.VMEM(output_gradient.shape, bf16),
             pltpu.VMEM((own_features, width), bf16),
             pltpu.SemaphoreType.DMA((5,)),
+            pltpu.SemaphoreType.DMA((2 + width // CHUNK,)),
         ],
     )(
         adapter_per_token.reshape(1, token_count),
@@ -320,17 +411,22 @@
     )(across.reshape(1).astype(jnp.int32), *grads)
     down, upper, whole_gradient = lax.optimization_barrier((down, upper, whole_gradient))
 
-    low_parts, weight = call(
+    low_parts = call(
         low_kernel,
-        (
-            jax.ShapeDtypeStruct((parts, slots, 2 * rank), f32),
-            jax.ShapeDtypeStruct((slots, carried), bf16),
-        ),
+        jax.ShapeDtypeStruct((parts, slots, 2 * rank), f32),
         "low_rank",
         2 * slots * rank * (width + features),
         2 * slots * columns,
     )(arrived, down, upper)
+    after_low = lax.optimization_barrier((low_parts, arrived))[1]
     low_parts = lax.all_to_all(low_parts, "mp", split_axis=0, concat_axis=0, tiled=True)
+    weight = call(
+        weight_kernel,
+        jax.ShapeDtypeStruct((slots, carried), bf16),
+        "weight",
+        0,
+        2 * slots * columns,
+    )(after_low)
     near = (weight, neighbour(weight, 1, 0), neighbour(weight, -1, 0), neighbour(weight, 0, 1))
 
     low, back = call(
@@ -340,8 +436,14 @@
             jax.ShapeDtypeStruct((owners, capacity, width + features), bf16),
         ),
         "back",
-        2 * slots * rank * (width + features),
-        2 * slots * (width + features),
+        LONG * 400,
+        LONG,
+        out_specs=(hbm, hbm),
+        scratch_shapes=[
+            pltpu.VMEM((slots, 2 * rank), bf16),
+            pltpu.VMEM((owners, capacity, width + features), bf16),
+            pltpu.SemaphoreType.DMA((1 + width // CHUNK,)),
+        ],
     )(low_parts, down, upper)
     returned = lax.all_to_all(back, "dp", split_axis=0, concat_axis=0, tiled=True)
 
@@ -352,11 +454,11 @@
             jax.ShapeDtypeStruct((rank, features), f32),
         ),
         "factor_gradients",
-        2 * slots * rank * (width + features),
-        6 * slots * (width + features),
+        LONG * 400,
+        LONG,
     )(arrived, low)
 
-    near = lax.optimization_barrier((back, near))[1]
+    near = lax.optimization_barrier((down_out, near))[1]
     gathered = call(
         stack_kernel,
         jax.ShapeDtypeStruct((CLASSES, slots, carried), bf16),
@@ -370,17 +472,34 @@
     order = [(((mine + offset) % CLASSES) * N_C + core) for offset in offsets]
     order += [(((mine + offset) % CLASSES) * N_C + 1 - core) for offset in offsets]
     order = jnp.stack(order + [across]).astype(jnp.int32)
-    plain_input, *forward = call(
-        base_kernel,
-        [jax.ShapeDtypeStruct((token_count, width), f32)]
-        + [jax.ShapeDtypeStruct((token_count, features), f32)] * parts,
-        "base",
-        4 * token_count * width * all_features,
-        2 * width * all_features,
-        in_specs=[smem] + [vmem] * 4,
-        out_specs=[vmem] * (parts + 1),
+    half_work = 2 * token_count * width * all_features // 2
+    by_class = jax.ShapeDtypeStruct((CLASSES, token_count, depth), f32)
+    totals, own_input = call(
+        own_kernel,
+        (jax.ShapeDtypeStruct((FOLD, token_count, slots), f32), by_class),
+        "base_own",
+        2 * half_work,
+        width * all_features,
+        in_specs=[smem] + [vmem] * 3,
+        out_specs=(vmem, vmem),
+    )(order, tokens, whole_gradient, gathered)
+    forward = call(
+        forward_kernel,
+        [jax.ShapeDtypeStruct((token_count, features), f32)] * parts,
+        "base_forward",
+        half_work,
+        width * all_features,
+        in_specs=[smem] + [vmem] * 3,
+        out_specs=[vmem] * parts,
         scratch_shapes=[pltpu.VMEM((parts, token_count, features), f32)],
-    )(order, tokens, whole_gradient, gathered, swapped)
+    )(order, tokens, totals, swapped)
+    other_input = call(
+        input_kernel,
+        by_class,
+        "base_input",
+        half_work,
+        width * all_features,
+    )(whole_gradient, swapped)
     sums = [forward[0]] + [around(forward[shift], shift) for shift in range(1, parts)]
 
     projected, activation_gradient = call(
@@ -392,7 +511,20 @@
         "finish",
         2 * slots * token_count * (width + features),
         2 * slots * (width + features),
-    )(picks, returned, plain_input, *sums)
+        limit=WHOLE_VMEM,
+        in_specs=[smem] + [hbm] * (4 + parts),
+        out_specs=(hbm, hbm),
+        scratch_shapes=[
+            pltpu.VMEM(picks.shape, bf16),
+            pltpu.VMEM(returned.shape, bf16),
+            pltpu.VMEM((token_count, width), f32),
+            pltpu.VMEM((parts, token_count, features), f32),
+            pltpu.VMEM((token_count, features), bf16),
+            pltpu.VMEM((token_count, width), bf16),
+            pltpu.SemaphoreType.DMA((1 + 2 * CLASSES + width // CHUNK + 1 + parts,)),
+            pltpu.SemaphoreType.DMA((width // CHUNK + 1,)),
+        ],
+    )(order, picks, returned, own_input, other_input, *sums)
     return (projected, activation_gradient, down_out.T[None], upper_out[None])
 
 

time: 137 us -> 132 us (0.964)
  blocking collectives: 10.8 us -> 0 us
  starting transfers between devices: 60.9 us -> 66.3 us
  Pallas kernels: 17 us -> 20.4 us
  local copies, waits for them, and re-layouts: 5.64 us -> 3.28 us
    all_to_all x1 -> x0, blocking collectives: 10.8 us -> none  [body(): lax.all_to_all(low_parts, 'mp', split_axis=0, concat_axis=0, tiled=True)]
    all_to_all x0 -> x1, starting transfers between devices: none -> 4.02 us  [body(): lax.all_to_all(low_parts, 'mp', split_axis=0, concat_axis=0, tiled=True)]
    ppermute x1, waiting for transfers between devices: 3.9 us -> 1.04 us  [other_core(): lax.ppermute(value, 'dp', [(i, i ^ 1) for i in range(N_Z * N_Y * N_C)])]
    pallas_call x1, Pallas kernels: 1.15 us -> 3.89 us  [body(): call(finish_kernel, (jax.ShapeDtypeStruct((token_count, features), bf16),...]
    unnamed x24, local copies, waits for them, and re-layouts: 5.56 us -> 3.2 us
    all_to_all x1, starting transfers between devices: 10.2 us -> 8.4 us  [body(): lax.all_to_all(back, 'dp', split_axis=0, concat_axis=0, tiled=True)]
    ppermute x6, starting transfers between devices: 19.7 us -> 21.3 us  [around(): lax.ppermute(value, 'mp', [(i, (i + shift) % parts) for i in range(parts)])]
    pallas_call x2 -> x5, Pallas kernels: 7.37 us -> 7.71 us  [the longest x1 3.18 us: body(): call(forward_kernel, [jax.ShapeDtypeStruct((token_count, features), f32)]...]
  transfers between devices with their start and end apart: 12 -> 13, of which waited for: 4 -> 4; matrix products, arithmetic and copies ran while one was open for 0% -> 0% of each run, Pallas kernels for 8% -> 9%
where the time goes in v3:
time: 132 us; the launch traced here: 131 us
  starting transfers between devices  66.3 us (50%)
  waiting for transfers between devices  39.8 us (30%)
  Pallas kernels  20.4 us (15%)
  local copies, waits for them, and re-layouts  3.28 us (2%)
    all_to_all x1, waiting for transfers between devices, body(): lax.all_to_all(outgoing, 'dp', split_axis=0, concat_axis=0, tiled=True)  30.4 us
    ppermute x6, starting transfers between devices, around(): lax.ppermute(value, 'mp', [(i, (i + shift) % parts) for i in range(parts)])  21.3 us
    all_to_all x1, starting transfers between devices, body(): lax.all_to_all(outgoing, 'dp', split_axis=0, concat_axis=0, tiled=True)  18.6 us
    ppermute x3, starting transfers between devices, neighbour(): return lax.ppermute(value, 'dp', pairs)  10.8 us
    all_to_all x1, starting transfers between devices, body(): lax.all_to_all(back, 'dp', split_axis=0, concat_axis=0, tiled=True)  8.4 us
    all_to_all x1, waiting for transfers between devices, body(): lax.all_to_all(back, 'dp', split_axis=0, concat_axis=0, tiled=True)  6.06 us
    all_to_all x1, starting transfers between devices, body(): lax.all_to_all(low_parts, 'mp', split_axis=0, concat_axis=0, tiled=True)  4.02 us
    pallas_call x1, Pallas kernels, body(): call(finish_kernel, (jax.ShapeDtypeStruct((token_count, features), bf16),...  3.89 us
  transfers between devices with their start and end apart: 13, of which 4 were waited for; matrix products, arithmetic and copies ran while one was open for 0% of the time, Pallas kernels for 9%

profile of v3, /device:TPU:1, one launch (start us, length us, event | category | flops | bytes accessed | tf_op | source)
XLA Modules:
  0.0 130.8 jit_solution(1213800549741095890)
XLA Ops:
  0.6 2.8 %spread.1 = (bf16[128,2,3328]{2,1,0:T(2,128)(2,1)}, bf16[256,128]{1,0:T(8,128)(2,1)}) custom-call(s32[1,128]{1,0:T(1,128)} %bitcast.25, s32[1,128]{1,0:T(1,128)} %bitcast.26, bf16[128,2048]{1,0:T(8,128)(2,1)} %tokens_ref.3, bf16[128,256]{1,0:T(8,128)(2,1)} %own_ref.1, bf16[8,2048]{1,0:T(8,128)(2,1)} %bitcast.24), custom_call_target="tpu_custom_call" | custom-call | flops 218103808 | bytes 2555904 | tf_op jit(solution)/shard_map/spread/pallas_call | solution.py:371
  3.5 0.0 copy-start.8
  3.5 0.0 copy-start.4
  3.5 0.0 copy-start.6
  3.5 18.6 %all-to-all-start = ((bf16[128,2,3328]{2,1,0:T(2,128)(2,1)}), bf16[128,2,3328]{2,1,0:T(2,128)(2,1)S(1)}, u32[]{:S(2)}, u32[]{:S(2)}) async-start(bf16[128,2,3328]{2,1,0:T(2,128)(2,1)} %get-tuple-element.27), calls=%async_computation | async-start | bytes 3407872 | tf_op jit(solution)/shard_map/all_to_all | solution.py:401
  22.1 3.1 %collective-permute-start = (bf16[128,256]{1,0:T(8,128)(2,1)S(1)}, bf16[128,256]{1,0:T(8,128)(2,1)S(1)}, u32[]{:S(2)}, u32[]{:S(2)}) collective-permute-start(bf16[128,256]{1,0:T(8,128)(2,1)S(1)} %copy-done.8), channel_id=1, source_target_pairs={{0,1},{1,2},{2,3},{3,0},{4,5},{5,6},{6,7},{7,4},{8,9},{9,10},{10,1... | collective-permute-start | bytes 196616 | tf_op jit(solution)/shard_map/ppermute | solution.py:367
  25.2 4.4 %collective-permute-start.1 = (bf16[128,256]{1,0:T(8,128)(2,1)S(1)}, bf16[128,256]{1,0:T(8,128)(2,1)S(1)}, u32[]{:S(2)}, u32[]{:S(2)}) collective-permute-start(bf16[128,256]{1,0:T(8,128)(2,1)S(1)} %copy-done.8), channel_id=1, source_target_pairs={{0,2},{1,3},{2,0},{3,1},{4,6},{5,7},{6,4},{7,5},{8,10},{9,11},{10,... | collective-permute-start | bytes 196616 | tf_op jit(solution)/shard_map/ppermute | solution.py:367
  29.6 3.1 %collective-permute-start.2 = (bf16[128,256]{1,0:T(8,128)(2,1)S(1)}, bf16[128,256]{1,0:T(8,128)(2,1)S(1)}, u32[]{:S(2)}, u32[]{:S(2)}) collective-permute-start(bf16[128,256]{1,0:T(8,128)(2,1)S(1)} %copy-done.8), channel_id=1, source_target_pairs={{0,3},{1,0},{2,1},{3,2},{4,7},{5,4},{6,5},{7,6},{8,11},{9,8},{10,9... | collective-permute-start | bytes 196616 | tf_op jit(solution)/shard_map/ppermute | solution.py:367
  32.7 0.0 collective-permute-done.a_ref
  32.7 0.0 collective-permute-done.1.b_ref
  32.7 2.2 %collective-permute-done.2.c_ref = bf16[128,256]{1,0:T(8,128)(2,1)S(1)} collective-permute-done((bf16[128,256]{1,0:T(8,128)(2,1)S(1)}, bf16[128,256]{1,0:T(8,128)(2,1)S(1)}, u32[]{:S(2)}, u32[]{:S(2)}) %collective-permute-start.2) | collective-permute-done | bytes 65568 | tf_op jit(solution)/shard_map/ppermute | solution.py:367
  34.9 0.5 order.1.grads_ref
  35.4 30.4 %all-to-all-done.arrived_ref = bf16[128,2,3328]{2,1,0:T(2,128)(2,1)S(1)} async-done(((bf16[128,2,3328]{2,1,0:T(2,128)(2,1)}), bf16[128,2,3328]{2,1,0:T(2,128)(2,1)S(1)}, u32[]{:S(2)}, u32[]{:S(2)}) %all-to-all-start) | async-done | bytes 1703968 | tf_op jit(solution)/shard_map/all_to_all | solution.py:401
  65.8 1.3 %low_rank.1 = f32[4,256,128]{2,1,0:T(8,128)} custom-call(bf16[128,2,3328]{2,1,0:T(2,128)(2,1)S(1)} %all-to-all-done.arrived_ref, bf16[64,2048]{1,0:T(8,128)(2,1)S(1)} %bitcast.20, bf16[64,256]{1,0:T(8,128)(2,1)S(1)} %bitcast.22), custom_call_target="tpu_custom_call" | custom-call | flops 75497472 | bytes 1703936 | tf_op jit(solution)/shard_map/low_rank/pallas_call | solution.py:414
  67.1 4.0 %all-to-all-start.1 = ((f32[4,256,128]{2,1,0:T(8,128)}), f32[4,256,128]{2,1,0:T(8,128)S(1)}, u32[]{:S(2)}, u32[]{:S(2)}) async-start(f32[4,256,128]{2,1,0:T(8,128)} %low_rank.1), calls=%async_computation.1 | async-start | bytes 1048576 | tf_op jit(solution)/shard_map/all_to_all | solution.py:422
  71.2 0.1 weight.1.refs_0_
  71.2 2.3 %collective-permute-start.3 = (bf16[256,1024]{1,0:T(8,128)(2,1)S(1)}, bf16[256,1024]{1,0:T(8,128)(2,1)}, u32[]{:S(2)}, u32[]{:S(2)}) collective-permute-start(bf16[256,1024]{1,0:T(8,128)(2,1)S(1)} %weight.1.refs_0_), channel_id=1, source_target_pairs={{0,64},{4,68},{8,72},{12,76},{16,80},{20,84},{24,88},{28,92},{32,9... | collective-permute-start | bytes 1572872 | tf_op jit(solution)/shard_map/ppermute | solution.py:326
  73.5 4.2 %collective-permute-start.4 = (bf16[256,1024]{1,0:T(8,128)(2,1)S(1)}, bf16[256,1024]{1,0:T(8,128)(2,1)}, u32[]{:S(2)}, u32[]{:S(2)}) collective-permute-start(bf16[256,1024]{1,0:T(8,128)(2,1)S(1)} %weight.1.refs_0_), channel_id=1, source_target_pairs={{0,448},{4,452},{8,456},{12,460},{16,464},{20,468},{24,472},{28,47... | collective-permute-start | bytes 1572872 | tf_op jit(solution)/shard_map/ppermute | solution.py:326
  77.7 4.3 %collective-permute-start.5 = (bf16[256,1024]{1,0:T(8,128)(2,1)S(1)}, bf16[256,1024]{1,0:T(8,128)(2,1)}, u32[]{:S(2)}, u32[]{:S(2)}) collective-permute-start(bf16[256,1024]{1,0:T(8,128)(2,1)S(1)} %weight.1.refs_0_), channel_id=1, source_target_pairs={{0,8},{4,12},{8,16},{12,20},{16,24},{20,28},{24,32},{28,36},{32,40... | collective-permute-start | bytes 1572872 | tf_op jit(solution)/shard_map/ppermute | solution.py:326
  82.1 0.0 all-to-all-done.1.parts_ref
  82.1 1.4 %back.1 = (bf16[256,128]{1,0:T(8,128)(2,1)S(1)}, bf16[128,2,2304]{2,1,0:T(2,128)(2,1)S(1)}) custom-call(f32[4,256,128]{2,1,0:T(8,128)S(1)} %all-to-all-done.1.parts_ref, bf16[64,2048]{1,0:T(8,128)(2,1)S(1)} %bitcast.21, bf16[64,256]{1,0:T(8,128)(2,1)S(1)} %bitcast.23), custom_call_target="tpu_custom_call" | custom-call | flops 41943040000 | bytes 104857600 | tf_op jit(solution)/shard_map/back/pallas_call | solution.py:432
  83.5 1.0 copy-done.2
  84.5 8.4 %all-to-all-start.2 = ((bf16[128,2,2304]{2,1,0:T(2,128)(2,1)}), bf16[128,2,2304]{2,1,0:T(2,128)(2,1)}, u32[]{:S(2)}, u32[]{:S(2)}) async-start(bf16[128,2,2304]{2,1,0:T(2,128)(2,1)} %copy-done.2), calls=%async_computation.2 | async-start | bytes 2359296 | tf_op jit(solution)/shard_map/all_to_all | solution.py:448
  92.9 1.2 factor_gradients.1
  94.1 0.0 collective-permute-done.3.refs_1_
  94.1 0.0 collective-permute-done.4.refs_2_
  94.1 0.0 collective-permute-done.5.refs_3_
  94.1 0.0 copy-start
  94.1 2.9 %stack.41.weight_ref = bf16[4,256,1024]{2,1,0:T(8,128)(2,1)} custom-call(bf16[256,1024]{1,0:T(8,128)(2,1)S(1)} %weight.1.refs_0_, bf16[256,1024]{1,0:T(8,128)(2,1)} %collective-permute-done.3.refs_1_, bf16[256,1024]{1,0:T(8,128)(2,1)} %collective-permute-done.4.refs_2_, bf16[256,1024]{1,0:T(8,128)(2,1)} %collective-permute-done.5.refs_3_), custom_call_target="tpu_custom_call" | custom-call | bytes 4194304 | tf_op jit(solution)/shard_map/stack/pallas_call | solution.py:462
  97.0 3.2 %collective-permute-start.6 = (bf16[4,256,1024]{2,1,0:T(8,128)(2,1)}, bf16[4,256,1024]{2,1,0:T(8,128)(2,1)S(1)}, u32[]{:S(2)}, u32[]{:S(2)}) collective-permute-start(bf16[4,256,1024]{2,1,0:T(8,128)(2,1)} %stack.41.weight_ref), channel_id=1, source_target_pairs={{0,4},{4,0},{8,12},{12,8},{16,20},{20,16},{24,28},{28,24},{32,36},... | collective-permute-start | bytes 6291464 | tf_op jit(solution)/shard_map/ppermute | solution.py:330
  100.4 0.1 stack.40.order_ref
  100.5 2.7 %base_own.1 = (f32[4,128,256]{2,1,0:T(8,128)S(1)}, f32[4,128,256]{2,1,0:T(8,128)S(1)}) custom-call(s32[9]{0:T(128)S(1)} %stack.40.order_ref, bf16[128,2048]{1,0:T(8,128)(2,1)S(1)} %copy-done, bf16[4,128,256]{2,1,0:T(8,128)(2,1)S(1)} %order.1.grads_ref, bf16[4,256,1024]{2,1,0:T(8,128)(2,1)} %stack.41.weight_ref), custom_call_target="tpu_custom_call" | custom-call | flops 536870912 | bytes 2097152 | tf_op jit(solution)/shard_map/base_own/pallas_call | solution.py:477
  103.2 1.0 collective-permute-done.6.weight_ref
  104.2 3.2 %base_forward.1 = (f32[128,256]{1,0:T(8,128)S(1)}, f32[128,256]{1,0:T(8,128)}, f32[128,256]{1,0:T(8,128)}, f32[128,256]{1,0:T(8,128)S(1)}) custom-call(s32[9]{0:T(128)S(1)} %stack.40.order_ref, bf16[128,2048]{1,0:T(8,128)(2,1)S(1)} %copy-done, f32[4,128,256]{2,1,0:T(8,128)S(1)} %get-tuple-element.40.totals_ref, ...), custom_call_target="tpu_custom_call" | custom-call | flops 268435456 | bytes 2097152 | tf_op jit(solution)/shard_map/base_forward/pallas_call | solution.py:486
  107.4 0.6 copy-done.5
  108.1 3.4 %collective-permute-start.7 = (f32[128,256]{1,0:T(8,128)}, f32[128,256]{1,0:T(8,128)S(1)}, u32[]{:S(2)}, u32[]{:S(2)}) collective-permute-start(f32[128,256]{1,0:T(8,128)} %get-tuple-element.42), channel_id=1, source_target_pairs={{0,1},{1,2},{2,3},{3,0},{4,5},{5,6},{6,7},{7,4},{8,9},{9,10},{10,1... | collective-permute-start | bytes 393224 | tf_op jit(solution)/shard_map/ppermute | solution.py:367
  111.4 4.3 %collective-permute-start.8 = (f32[128,256]{1,0:T(8,128)}, f32[128,256]{1,0:T(8,128)S(1)}, u32[]{:S(2)}, u32[]{:S(2)}) collective-permute-start(f32[128,256]{1,0:T(8,128)} %get-tuple-element.43), channel_id=1, source_target_pairs={{0,2},{1,3},{2,0},{3,1},{4,6},{5,7},{6,4},{7,5},{8,10},{9,11},{10,... | collective-permute-start | bytes 393224 | tf_op jit(solution)/shard_map/ppermute | solution.py:367
  115.7 3.1 %collective-permute-start.9 = (f32[128,256]{1,0:T(8,128)S(1)}, f32[128,256]{1,0:T(8,128)S(1)}, u32[]{:S(2)}, u32[]{:S(2)}) collective-permute-start(f32[128,256]{1,0:T(8,128)S(1)} %get-tuple-element.44), channel_id=1, source_target_pairs={{0,3},{1,0},{2,1},{3,2},{4,7},{5,4},{6,5},{7,6},{8,11},{9,8},{10,9... | collective-permute-start | bytes 393224 | tf_op jit(solution)/shard_map/ppermute | solution.py:367
  118.8 0.4 base_input.1.other_hbm
  119.3 0.8 copy-done.1
  120.1 6.1 %all-to-all-done.2.returned_hbm = bf16[128,2,2304]{2,1,0:T(2,128)(2,1)} async-done(((bf16[128,2,2304]{2,1,0:T(2,128)(2,1)}), bf16[128,2,2304]{2,1,0:T(2,128)(2,1)}, u32[]{:S(2)}, u32[]{:S(2)}) %all-to-all-start.2) | async-done | bytes 1179680 | tf_op jit(solution)/shard_map/all_to_all | solution.py:448
  126.2 0.0 collective-permute-done.7.refs_1_
  126.2 0.0 collective-permute-done.8.refs_2_
  126.2 0.0 collective-permute-done.9.refs_3_
  126.2 0.6 copy-done.9
  126.8 0.1 copy-done.10
  126.9 0.1 copy-done.11
  126.9 3.9 %finish.1 = (bf16[128,256]{1,0:T(8,128)(2,1)}, bf16[128,2048]{1,0:T(8,128)(2,1)}) custom-call(s32[9]{0:T(128)} %copy-done.7, bf16[256,128]{1,0:T(8,128)(2,1)} %get-tuple-element.26.picks_hbm, bf16[128,2,2304]{2,1,0:T(2,128)(2,1)} %all-to-all-done.2.returned_hbm, f32[4,128,256]{2,1,0:T(8,128)} %copy-done.3, f32[4,128,256]{2,1,0:T(8,128)} %copy-done.1, ...), custom_call_target="tpu_custom_call" | custom-call | flops 150994944 | bytes 1179648 | tf_op jit(solution)/shard_map/finish/pallas_call | solution.py:505
  (14 shorter events, 0.0 us)
Async XLA Ops:
  3.5 18.6 %copy-start.8 = (bf16[128,256]{1,0:T(8,128)(2,1)S(1)}, bf16[128,256]{1,0:T(8,128)(2,1)}, u32[]{:S(2)}) copy-start(bf16[128,256]{1,0:T(8,128)(2,1)} %own_ref.1) | copy-start | bytes 196612
  3.5 62.3 %copy-start.4 = (bf16[1,2048,64]{1,2,0:T(8,128)(2,1)S(1)}, bf16[1,2048,64]{1,2,0:T(8,128)(2,1)}, u32[]{:S(2)}) copy-start(bf16[1,2048,64]{1,2,0:T(8,128)(2,1)} %param.10) | copy-start | bytes 786436
  3.5 62.3 %copy-start.6 = (bf16[1,64,256]{2,1,0:T(8,128)(2,1)S(1)}, bf16[1,64,256]{2,1,0:T(8,128)(2,1)}, u32[]{:S(2)}) copy-start(bf16[1,64,256]{2,1,0:T(8,128)(2,1)} %param.11) | copy-start | bytes 98308
  3.5 62.3 %all-to-all-start = ((bf16[128,2,3328]{2,1,0:T(2,128)(2,1)}), bf16[128,2,3328]{2,1,0:T(2,128)(2,1)S(1)}, u32[]{:S(2)}, u32[]{:S(2)}) async-start(bf16[128,2,3328]{2,1,0:T(2,128)(2,1)} %get-tuple-element.27), calls=%async_computation | async-start | bytes 3407872 | tf_op jit(solution)/shard_map/all_to_all | solution.py:401
  22.1 10.6 %collective-permute-start = (bf16[128,256]{1,0:T(8,128)(2,1)S(1)}, bf16[128,256]{1,0:T(8,128)(2,1)S(1)}, u32[]{:S(2)}, u32[]{:S(2)}) collective-permute-start(bf16[128,256]{1,0:T(8,128)(2,1)S(1)} %copy-done.8), channel_id=1, source_target_pairs={{0,1},{1,2},{2,3},{3,0},{4,5},{5,6},{6,7},{7,4},{8,9},{9,10},{10,1... | collective-permute-start | bytes 196616 | tf_op jit(solution)/shard_map/ppermute | solution.py:367
  25.2 7.5 %collective-permute-start.1 = (bf16[128,256]{1,0:T(8,128)(2,1)S(1)}, bf16[128,256]{1,0:T(8,128)(2,1)S(1)}, u32[]{:S(2)}, u32[]{:S(2)}) collective-permute-start(bf16[128,256]{1,0:T(8,128)(2,1)S(1)} %copy-done.8), channel_id=1, source_target_pairs={{0,2},{1,3},{2,0},{3,1},{4,6},{5,7},{6,4},{7,5},{8,10},{9,11},{10,... | collective-permute-start | bytes 196616 | tf_op jit(solution)/shard_map/ppermute | solution.py:367
  29.6 5.3 %collective-permute-start.2 = (bf16[128,256]{1,0:T(8,128)(2,1)S(1)}, bf16[128,256]{1,0:T(8,128)(2,1)S(1)}, u32[]{:S(2)}, u32[]{:S(2)}) collective-permute-start(bf16[128,256]{1,0:T(8,128)(2,1)S(1)} %copy-done.8), channel_id=1, source_target_pairs={{0,3},{1,0},{2,1},{3,2},{4,7},{5,4},{6,5},{7,6},{8,11},{9,8},{10,9... | collective-permute-start | bytes 196616 | tf_op jit(solution)/shard_map/ppermute | solution.py:367
  67.1 14.9 %all-to-all-start.1 = ((f32[4,256,128]{2,1,0:T(8,128)}), f32[4,256,128]{2,1,0:T(8,128)S(1)}, u32[]{:S(2)}, u32[]{:S(2)}) async-start(f32[4,256,128]{2,1,0:T(8,128)} %low_rank.1), calls=%async_computation.1 | async-start | bytes 1048576 | tf_op jit(solution)/shard_map/all_to_all | solution.py:422
  71.2 22.9 %collective-permute-start.3 = (bf16[256,1024]{1,0:T(8,128)(2,1)S(1)}, bf16[256,1024]{1,0:T(8,128)(2,1)}, u32[]{:S(2)}, u32[]{:S(2)}) collective-permute-start(bf16[256,1024]{1,0:T(8,128)(2,1)S(1)} %weight.1.refs_0_), channel_id=1, source_target_pairs={{0,64},{4,68},{8,72},{12,76},{16,80},{20,84},{24,88},{28,92},{32,9... | collective-permute-start | bytes 1572872 | tf_op jit(solution)/shard_map/ppermute | solution.py:326
  73.5 20.6 %collective-permute-start.4 = (bf16[256,1024]{1,0:T(8,128)(2,1)S(1)}, bf16[256,1024]{1,0:T(8,128)(2,1)}, u32[]{:S(2)}, u32[]{:S(2)}) collective-permute-start(bf16[256,1024]{1,0:T(8,128)(2,1)S(1)} %weight.1.refs_0_), channel_id=1, source_target_pairs={{0,448},{4,452},{8,456},{12,460},{16,464},{20,468},{24,472},{28,47... | collective-permute-start | bytes 1572872 | tf_op jit(solution)/shard_map/ppermute | solution.py:326
  77.7 16.4 %collective-permute-start.5 = (bf16[256,1024]{1,0:T(8,128)(2,1)S(1)}, bf16[256,1024]{1,0:T(8,128)(2,1)}, u32[]{:S(2)}, u32[]{:S(2)}) collective-permute-start(bf16[256,1024]{1,0:T(8,128)(2,1)S(1)} %weight.1.refs_0_), channel_id=1, source_target_pairs={{0,8},{4,12},{8,16},{12,20},{16,24},{20,28},{24,32},{28,36},{32,40... | collective-permute-start | bytes 1572872 | tf_op jit(solution)/shard_map/ppermute | solution.py:326
  83.4 1.0 copy-start.2
  84.5 41.7 %all-to-all-start.2 = ((bf16[128,2,2304]{2,1,0:T(2,128)(2,1)}), bf16[128,2,2304]{2,1,0:T(2,128)(2,1)}, u32[]{:S(2)}, u32[]{:S(2)}) async-start(bf16[128,2,2304]{2,1,0:T(2,128)(2,1)} %copy-done.2), calls=%async_computation.2 | async-start | bytes 2359296 | tf_op jit(solution)/shard_map/all_to_all | solution.py:448
  94.1 6.4 %copy-start = (bf16[128,2048]{1,0:T(8,128)(2,1)S(1)}, bf16[128,2048]{1,0:T(8,128)(2,1)}, u32[]{:S(2)}) copy-start(bf16[128,2048]{1,0:T(8,128)(2,1)} %tokens_ref.3) | copy-start | bytes 1572868
  97.0 7.2 %collective-permute-start.6 = (bf16[4,256,1024]{2,1,0:T(8,128)(2,1)}, bf16[4,256,1024]{2,1,0:T(8,128)(2,1)S(1)}, u32[]{:S(2)}, u32[]{:S(2)}) collective-permute-start(bf16[4,256,1024]{2,1,0:T(8,128)(2,1)} %stack.41.weight_ref), channel_id=1, source_target_pairs={{0,4},{4,0},{8,12},{12,8},{16,20},{20,16},{24,28},{28,24},{32,36},... | collective-permute-start | bytes 6291464 | tf_op jit(solution)/shard_map/ppermute | solution.py:330
  100.5 7.0 %copy-start.7 = (s32[9]{0:T(128)}, s32[9]{0:T(128)S(1)}, u32[]{:S(2)}) copy-start(s32[9]{0:T(128)S(1)} %stack.40.order_ref) | copy-start | bytes 112
  103.2 16.1 %copy-start.3 = (f32[4,128,256]{2,1,0:T(8,128)}, f32[4,128,256]{2,1,0:T(8,128)S(1)}, u32[]{:S(2)}) copy-start(f32[4,128,256]{2,1,0:T(8,128)S(1)} %get-tuple-element.39.mine_hbm) | copy-start | bytes 1572868
  107.4 0.6 copy-start.5
  108.1 18.1 %collective-permute-start.7 = (f32[128,256]{1,0:T(8,128)}, f32[128,256]{1,0:T(8,128)S(1)}, u32[]{:S(2)}, u32[]{:S(2)}) collective-permute-start(f32[128,256]{1,0:T(8,128)} %get-tuple-element.42), channel_id=1, source_target_pairs={{0,1},{1,2},{2,3},{3,0},{4,5},{5,6},{6,7},{7,4},{8,9},{9,10},{10,1... | collective-permute-start | bytes 393224 | tf_op jit(solution)/shard_map/ppermute | solution.py:367
  111.4 14.7 %collective-permute-start.8 = (f32[128,256]{1,0:T(8,128)}, f32[128,256]{1,0:T(8,128)S(1)}, u32[]{:S(2)}, u32[]{:S(2)}) collective-permute-start(f32[128,256]{1,0:T(8,128)} %get-tuple-element.43), channel_id=1, source_target_pairs={{0,2},{1,3},{2,0},{3,1},{4,6},{5,7},{6,4},{7,5},{8,10},{9,11},{10,... | collective-permute-start | bytes 393224 | tf_op jit(solution)/shard_map/ppermute | solution.py:367
  115.7 10.4 %collective-permute-start.9 = (f32[128,256]{1,0:T(8,128)S(1)}, f32[128,256]{1,0:T(8,128)S(1)}, u32[]{:S(2)}, u32[]{:S(2)}) collective-permute-start(f32[128,256]{1,0:T(8,128)S(1)} %get-tuple-element.44), channel_id=1, source_target_pairs={{0,3},{1,0},{2,1},{3,2},{4,7},{5,4},{6,5},{7,6},{8,11},{9,8},{10,9... | collective-permute-start | bytes 393224 | tf_op jit(solution)/shard_map/ppermute | solution.py:367
  119.3 0.8 copy-start.1
  126.2 0.6 copy-start.9
  126.2 0.7 copy-start.10
  126.2 0.7 copy-start.11

commit v4 on v3

--- a/solution.py
+++ b/solution.py
@@ -174,29 +174,24 @@
     out_ref[...] = flat(arrived_ref[:, :, arrived_ref.shape[2] - out_ref.shape[1] :])
 
 
-def back_kernel(parts_ref, down_ref, upper_ref, low_hbm, out_hbm, low_ref, out_ref, sems):
+def back_kernel(parts_ref, down_ref, upper_ref, low_hbm, out_ref, low_ref, sem):
     rank, width = down_ref.shape
     total = parts_ref[0]
     for part in range(1, parts_ref.shape[0]):
         total = total + parts_ref[part]
     low = total.astype(bf16)
     low_ref[...] = low
-    stores = [pltpu.make_async_copy(low_ref, low_hbm, sems.at[0])]
-    stores[0].start()
+    store = pltpu.make_async_copy(low_ref, low_hbm, sem)
+    store.start()
     for start in range(0, width, CHUNK):
         at = pl.ds(start, CHUNK)
         out_ref[:, :, at] = paired(
             (adapter_scale * contract(low[:, rank:], down_ref[:, at], 1, 0)).astype(bf16)
         )
-        if start + CHUNK == width:
-            at = pl.ds(start, out_ref.shape[2] - start)
-            out_ref[:, :, width:] = paired(
-                (adapter_scale * contract(low[:, :rank], upper_ref[...], 1, 0)).astype(bf16)
-            )
-        stores.append(pltpu.make_async_copy(out_ref.at[:, :, at], out_hbm.at[:, :, at], sems.at[len(stores)]))
-        stores[-1].start()
-    for store in stores:
-        store.wait()
+    out_ref[:, :, width:] = paired(
+        (adapter_scale * contract(low[:, :rank], upper_ref[...], 1, 0)).astype(bf16)
+    )
+    store.wait()
 
 
 def factor_kernel(arrived_ref, low_ref, down_out_ref, upper_out_ref):
@@ -211,47 +206,22 @@
     )
 
 
-def finish_kernel(order_ref, picks_hbm, returned_hbm, mine_hbm, other_hbm, *refs):
-    *part_hbm, out_hbm, grad_hbm = refs[:-8]
-    picks_ref, returned_ref, input_ref, part_ref, out_ref, grad_ref, in_sems, out_sems = refs[-8:]
-    classes, _, depth = mine_hbm.shape
-    width = grad_ref.shape[1]
-    sources = [(picks_hbm, picks_ref)]
-    for at in range(2 * classes):
-        half = mine_hbm if at < classes else other_hbm
-        sources.append((half.at[at % classes], input_ref.at[:, columns_of(order_ref, at, depth)]))
-    early = len(sources)
-    chunks = [pl.ds(start, CHUNK) for start in range(0, width, CHUNK)]
-    for columns in chunks + [pl.ds(width, returned_ref.shape[2] - width)]:
-        sources.append((returned_hbm.at[:, :, columns], returned_ref.at[:, :, columns]))
-    for at, source in enumerate(part_hbm):
-        sources.append((source, part_ref.at[at]))
-    copies = [
-        pltpu.make_async_copy(source, target, in_sems.at[at]) for at, (source, target) in enumerate(sources)
-    ]
-    for copy in copies:
-        copy.start()
-    for copy in copies[:early]:
-        copy.wait()
+def sum_kernel(*refs):
+    total = refs[0][...]
+    for ref in refs[1:-1]:
+        total = total + ref[...]
+    refs[-1][...] = total
+
+
+def finish_kernel(picks_ref, returned_ref, input_ref, base_ref, out_ref, grad_ref):
+    width = input_ref.shape[1]
     picks = picks_ref[...]
-    stores = []
-    for at, columns in enumerate(chunks):
-        copies[early + at].wait()
-        grad_ref[:, columns] = (
-            input_ref[:, columns] + contract(picks, flat(returned_ref[:, :, columns]), 0, 0)
+    for start in range(0, width, CHUNK):
+        at = pl.ds(start, CHUNK)
+        grad_ref[:, at] = (
+            input_ref[:, at] + contract(picks, flat(returned_ref[:, :, at]), 0, 0)
         ).astype(bf16)
-        stores.append(pltpu.make_async_copy(grad_ref.at[:, columns], grad_hbm.at[:, columns], out_sems.at[at]))
-        stores[-1].start()
-    for copy in copies[early + len(chunks) :]:
-        copy.wait()
-    base = part_ref[0]
-    for at in range(1, len(part_hbm)):
-        base = base + part_ref[at]
-    out_ref[...] = (base + contract(picks, flat(returned_ref[:, :, width:]), 0, 0)).astype(bf16)
-    stores.append(pltpu.make_async_copy(out_ref, out_hbm, out_sems.at[len(chunks)]))
-    stores[-1].start()
-    for store in stores:
-        store.wait()
+    out_ref[...] = (base_ref[...] + contract(picks, flat(returned_ref[:, :, width:]), 0, 0)).astype(bf16)
 
 
 def stack_kernel(*refs):
@@ -312,8 +282,12 @@
         forward_ref[...] = whole_ref[lax.rem(order_ref[2 * CLASSES] + shift, parts)]
 
 
-def input_kernel(grads_ref, weight_ref, input_ref):
+def input_kernel(order_ref, grads_ref, weight_ref, own_ref, out_ref, input_ref):
     input_half(grads_ref, weight_ref, input_ref)
+    depth = own_ref.shape[2]
+    for at in range(CLASSES):
+        out_ref[:, columns_of(order_ref, at, depth)] = own_ref[at]
+        out_ref[:, columns_of(order_ref, CLASSES + at, depth)] = input_ref[at]
 
 
 def neighbour(value, dz, dy):
@@ -438,12 +412,8 @@
         "back",
         LONG * 400,
         LONG,
-        out_specs=(hbm, hbm),
-        scratch_shapes=[
-            pltpu.VMEM((slots, 2 * rank), bf16),
-            pltpu.VMEM((owners, capacity, width + features), bf16),
-            pltpu.SemaphoreType.DMA((1 + width // CHUNK,)),
-        ],
+        out_specs=(hbm, vmem),
+        scratch_shapes=[pltpu.VMEM((slots, 2 * rank), bf16), pltpu.SemaphoreType.DMA],
     )(low_parts, down, upper)
     returned = lax.all_to_all(back, "dp", split_axis=0, concat_axis=0, tiled=True)
 
@@ -493,14 +463,25 @@
         out_specs=[vmem] * parts,
         scratch_shapes=[pltpu.VMEM((parts, token_count, features), f32)],
     )(order, tokens, totals, swapped)
-    other_input = call(
+    plain_input = call(
         input_kernel,
-        by_class,
+        jax.ShapeDtypeStruct((token_count, width), f32),
         "base_input",
         half_work,
         width * all_features,
-    )(whole_gradient, swapped)
+        in_specs=[smem] + [vmem] * 3,
+        out_specs=vmem,
+        scratch_shapes=[pltpu.VMEM((CLASSES, token_count, depth), f32)],
+    )(order, whole_gradient, swapped, own_input)
     sums = [forward[0]] + [around(forward[shift], shift) for shift in range(1, parts)]
+
+    plain_output = call(
+        sum_kernel,
+        jax.ShapeDtypeStruct((token_count, features), f32),
+        "sum",
+        0,
+        4 * (parts + 1) * token_count * features,
+    )(*sums)
 
     projected, activation_gradient = call(
         finish_kernel,
@@ -512,19 +493,7 @@
         2 * slots * token_count * (width + features),
         2 * slots * (width + features),
         limit=WHOLE_VMEM,
-        in_specs=[smem] + [hbm] * (4 + parts),
-        out_specs=(hbm, hbm),
-        scratch_shapes=[
-            pltpu.VMEM(picks.shape, bf16),
-            pltpu.VMEM(returned.shape, bf16),
-            pltpu.VMEM((token_count, width), f32),
-            pltpu.VMEM((parts, token_count, features), f32),
-            pltpu.VMEM((token_count, features), bf16),
-            pltpu.VMEM((token_count, width), bf16),
-            pltpu.SemaphoreType.DMA((1 + 2 * CLASSES + width // CHUNK + 1 + parts,)),
-            pltpu.SemaphoreType.DMA((width // CHUNK + 1,)),
-        ],
-    )(order, picks, returned, own_input, other_input, *sums)
+    )(picks, returned, plain_input, plain_output)
     return (projected, activation_gradient, down_out.T[None], upper_out[None])
 
 

time: 132 us -> 129 us (0.977)
  starting transfers between devices: 66.3 us -> 69 us
  waiting for transfers between devices: 39.8 us -> 37.1 us
  Pallas kernels: 20.4 us -> 18.4 us
    all_to_all x1, waiting for transfers between devices: 6.06 us -> 2.38 us  [body(): lax.all_to_all(back, 'dp', split_axis=0, concat_axis=0, tiled=True)]
    ppermute x1, starting transfers between devices: 3.24 us -> 6.67 us  [other_core(): lax.ppermute(value, 'dp', [(i, i ^ 1) for i in range(N_Z * N_Y * N_C)])]
    unnamed x24 -> x14, local copies, waits for them, and re-layouts: 3.2 us -> 2.69 us
  transfers between devices with their start and end apart: 13 -> 13, of which waited for: 4 -> 5; matrix products, arithmetic and copies ran while one was open for 0% -> 0% of each run, Pallas kernels for 9% -> 9%
where the time goes in v4:
time: 129 us; the launch traced here: 128 us
  starting transfers between devices  69 us (53%)
  waiting for transfers between devices  37.1 us (29%)
  Pallas kernels  18.4 us (14%)
  local copies, waits for them, and re-layouts  2.77 us (2%)
    all_to_all x1, waiting for transfers between devices, body(): lax.all_to_all(outgoing, 'dp', split_axis=0, concat_axis=0, tiled=True)  30.4 us
    ppermute x6, starting transfers between devices, around(): lax.ppermute(value, 'mp', [(i, (i + shift) % parts) for i in range(parts)])  20.5 us
    all_to_all x1, starting transfers between devices, body(): lax.all_to_all(outgoing, 'dp', split_axis=0, concat_axis=0, tiled=True)  18.6 us
    ppermute x3, starting transfers between devices, neighbour(): return lax.ppermute(value, 'dp', pairs)  10.8 us
    all_to_all x1, starting transfers between devices, body(): lax.all_to_all(back, 'dp', split_axis=0, concat_axis=0, tiled=True)  8.4 us
    ppermute x1, starting transfers between devices, other_core(): lax.ppermute(value, 'dp', [(i, i ^ 1) for i in range(N_Z * N_Y * N_C)])  6.67 us
    all_to_all x1, starting transfers between devices, body(): lax.all_to_all(low_parts, 'mp', split_axis=0, concat_axis=0, tiled=True)  4.02 us
    ppermute x6, waiting for transfers between devices, around(): lax.ppermute(value, 'mp', [(i, (i + shift) % parts) for i in range(parts)])  3.2 us
  transfers between devices with their start and end apart: 13, of which 5 were waited for; matrix products, arithmetic and copies ran while one was open for 0% of the time, Pallas kernels for 9%

profile of v4, /device:TPU:1, one launch (start us, length us, event | category | flops | bytes accessed | tf_op | source)
XLA Modules:
  0.0 128.3 jit_solution(10828318827975608447)
XLA Ops:
  0.6 2.9 %spread.1 = (bf16[128,2,3328]{2,1,0:T(2,128)(2,1)}, bf16[256,128]{1,0:T(8,128)(2,1)}) custom-call(s32[1,128]{1,0:T(1,128)} %bitcast.25, s32[1,128]{1,0:T(1,128)} %bitcast.26, bf16[128,2048]{1,0:T(8,128)(2,1)} %tokens_ref.3, bf16[128,256]{1,0:T(8,128)(2,1)} %own_ref.1, bf16[8,2048]{1,0:T(8,128)(2,1)} %bitcast.24), custom_call_target="tpu_custom_call" | custom-call | flops 218103808 | bytes 2555904 | tf_op jit(solution)/shard_map/spread/pallas_call | solution.py:345
  3.5 0.0 copy-start.6
  3.5 0.0 copy-start.4
  3.5 0.0 copy-start.5
  3.6 18.6 %all-to-all-start = ((bf16[128,2,3328]{2,1,0:T(2,128)(2,1)}), bf16[128,2,3328]{2,1,0:T(2,128)(2,1)S(1)}, u32[]{:S(2)}, u32[]{:S(2)}) async-start(bf16[128,2,3328]{2,1,0:T(2,128)(2,1)} %get-tuple-element.27), calls=%async_computation | async-start | bytes 3407872 | tf_op jit(solution)/shard_map/all_to_all | solution.py:375
  22.1 0.0 copy-done.6
  22.1 3.1 %collective-permute-start = (bf16[128,256]{1,0:T(8,128)(2,1)S(1)}, bf16[128,256]{1,0:T(8,128)(2,1)S(1)}, u32[]{:S(2)}, u32[]{:S(2)}) collective-permute-start(bf16[128,256]{1,0:T(8,128)(2,1)S(1)} %copy-done.6), channel_id=1, source_target_pairs={{0,1},{1,2},{2,3},{3,0},{4,5},{5,6},{6,7},{7,4},{8,9},{9,10},{10,1... | collective-permute-start | bytes 196616 | tf_op jit(solution)/shard_map/ppermute | solution.py:341
  25.3 4.4 %collective-permute-start.1 = (bf16[128,256]{1,0:T(8,128)(2,1)S(1)}, bf16[128,256]{1,0:T(8,128)(2,1)S(1)}, u32[]{:S(2)}, u32[]{:S(2)}) collective-permute-start(bf16[128,256]{1,0:T(8,128)(2,1)S(1)} %copy-done.6), channel_id=1, source_target_pairs={{0,2},{1,3},{2,0},{3,1},{4,6},{5,7},{6,4},{7,5},{8,10},{9,11},{10,... | collective-permute-start | bytes 196616 | tf_op jit(solution)/shard_map/ppermute | solution.py:341
  29.6 3.1 %collective-permute-start.2 = (bf16[128,256]{1,0:T(8,128)(2,1)S(1)}, bf16[128,256]{1,0:T(8,128)(2,1)S(1)}, u32[]{:S(2)}, u32[]{:S(2)}) collective-permute-start(bf16[128,256]{1,0:T(8,128)(2,1)S(1)} %copy-done.6), channel_id=1, source_target_pairs={{0,3},{1,0},{2,1},{3,2},{4,7},{5,4},{6,5},{7,6},{8,11},{9,8},{10,9... | collective-permute-start | bytes 196616 | tf_op jit(solution)/shard_map/ppermute | solution.py:341
  32.7 0.0 collective-permute-done.a_ref
  32.7 0.0 collective-permute-done.1.b_ref
  32.7 2.2 %collective-permute-done.2.c_ref = bf16[128,256]{1,0:T(8,128)(2,1)S(1)} collective-permute-done((bf16[128,256]{1,0:T(8,128)(2,1)S(1)}, bf16[128,256]{1,0:T(8,128)(2,1)S(1)}, u32[]{:S(2)}, u32[]{:S(2)}) %collective-permute-start.2) | collective-permute-done | bytes 65568 | tf_op jit(solution)/shard_map/ppermute | solution.py:341
  34.9 0.5 order.1.grads_ref
  35.4 30.4 %all-to-all-done.arrived_ref = bf16[128,2,3328]{2,1,0:T(2,128)(2,1)S(1)} async-done(((bf16[128,2,3328]{2,1,0:T(2,128)(2,1)}), bf16[128,2,3328]{2,1,0:T(2,128)(2,1)S(1)}, u32[]{:S(2)}, u32[]{:S(2)}) %all-to-all-start) | async-done | bytes 1703968 | tf_op jit(solution)/shard_map/all_to_all | solution.py:375
  65.8 0.0 copy-done.4
  65.8 1.3 %low_rank.1 = f32[4,256,128]{2,1,0:T(8,128)} custom-call(bf16[128,2,3328]{2,1,0:T(2,128)(2,1)S(1)} %all-to-all-done.arrived_ref, bf16[64,2048]{1,0:T(8,128)(2,1)S(1)} %bitcast.20, bf16[64,256]{1,0:T(8,128)(2,1)S(1)} %bitcast.22), custom_call_target="tpu_custom_call" | custom-call | flops 75497472 | bytes 1703936 | tf_op jit(solution)/shard_map/low_rank/pallas_call | solution.py:388
  67.2 4.0 %all-to-all-start.1 = ((f32[4,256,128]{2,1,0:T(8,128)}), f32[4,256,128]{2,1,0:T(8,128)S(1)}, u32[]{:S(2)}, u32[]{:S(2)}) async-start(f32[4,256,128]{2,1,0:T(8,128)} %low_rank.1), calls=%async_computation.1 | async-start | bytes 1048576 | tf_op jit(solution)/shard_map/all_to_all | solution.py:396
  71.2 0.1 weight.1.refs_0_
  71.2 2.3 %collective-permute-start.3 = (bf16[256,1024]{1,0:T(8,128)(2,1)S(1)}, bf16[256,1024]{1,0:T(8,128)(2,1)}, u32[]{:S(2)}, u32[]{:S(2)}) collective-permute-start(bf16[256,1024]{1,0:T(8,128)(2,1)S(1)} %weight.1.refs_0_), channel_id=1, source_target_pairs={{0,64},{4,68},{8,72},{12,76},{16,80},{20,84},{24,88},{28,92},{32,9... | collective-permute-start | bytes 1572872 | tf_op jit(solution)/shard_map/ppermute | solution.py:300
  73.6 4.2 %collective-permute-start.4 = (bf16[256,1024]{1,0:T(8,128)(2,1)S(1)}, bf16[256,1024]{1,0:T(8,128)(2,1)}, u32[]{:S(2)}, u32[]{:S(2)}) collective-permute-start(bf16[256,1024]{1,0:T(8,128)(2,1)S(1)} %weight.1.refs_0_), channel_id=1, source_target_pairs={{0,448},{4,452},{8,456},{12,460},{16,464},{20,468},{24,472},{28,47... | collective-permute-start | bytes 1572872 | tf_op jit(solution)/shard_map/ppermute | solution.py:300
  77.8 4.3 %collective-permute-start.5 = (bf16[256,1024]{1,0:T(8,128)(2,1)S(1)}, bf16[256,1024]{1,0:T(8,128)(2,1)}, u32[]{:S(2)}, u32[]{:S(2)}) collective-permute-start(bf16[256,1024]{1,0:T(8,128)(2,1)S(1)} %weight.1.refs_0_), channel_id=1, source_target_pairs={{0,8},{4,12},{8,16},{12,20},{16,24},{20,28},{24,32},{28,36},{32,40... | collective-permute-start | bytes 1572872 | tf_op jit(solution)/shard_map/ppermute | solution.py:300
  82.1 0.0 all-to-all-done.1.parts_ref
  82.1 0.7 back.1
  82.8 1.0 copy-done.2
  83.8 8.4 %all-to-all-start.2 = ((bf16[128,2,2304]{2,1,0:T(2,128)(2,1)}), bf16[128,2,2304]{2,1,0:T(2,128)(2,1)}, u32[]{:S(2)}, u32[]{:S(2)}) async-start(bf16[128,2,2304]{2,1,0:T(2,128)(2,1)} %copy-done.2), calls=%async_computation.2 | async-start | bytes 2359296 | tf_op jit(solution)/shard_map/all_to_all | solution.py:418
  92.2 1.2 factor_gradients.1
  93.4 0.0 collective-permute-done.3.refs_1_
  93.4 0.0 collective-permute-done.4.refs_2_
  93.4 0.0 collective-permute-done.5.refs_3_
  93.4 0.0 copy-start.1
  93.4 2.9 %stack.38.weight_ref = bf16[4,256,1024]{2,1,0:T(8,128)(2,1)} custom-call(bf16[256,1024]{1,0:T(8,128)(2,1)S(1)} %weight.1.refs_0_, bf16[256,1024]{1,0:T(8,128)(2,1)} %collective-permute-done.3.refs_1_, bf16[256,1024]{1,0:T(8,128)(2,1)} %collective-permute-done.4.refs_2_, bf16[256,1024]{1,0:T(8,128)(2,1)} %collective-permute-done.5.refs_3_), custom_call_target="tpu_custom_call" | custom-call | bytes 4194304 | tf_op jit(solution)/shard_map/stack/pallas_call | solution.py:432
  96.3 6.7 %collective-permute-start.6 = (bf16[4,256,1024]{2,1,0:T(8,128)(2,1)}, bf16[4,256,1024]{2,1,0:T(8,128)(2,1)S(1)}, u32[]{:S(2)}, u32[]{:S(2)}) collective-permute-start(bf16[4,256,1024]{2,1,0:T(8,128)(2,1)} %stack.38.weight_ref), channel_id=1, source_target_pairs={{0,4},{4,0},{8,12},{12,8},{16,20},{20,16},{24,28},{28,24},{32,36},... | collective-permute-start | bytes 6291464 | tf_op jit(solution)/shard_map/ppermute | solution.py:304
  103.1 0.1 stack.37.order_ref
  103.2 2.7 %base_own.1 = (f32[4,128,256]{2,1,0:T(8,128)S(1)}, f32[4,128,256]{2,1,0:T(8,128)S(1)}) custom-call(s32[9]{0:T(128)S(1)} %stack.37.order_ref, bf16[128,2048]{1,0:T(8,128)(2,1)S(1)} %copy-done.1, bf16[4,128,256]{2,1,0:T(8,128)(2,1)S(1)} %order.1.grads_ref, bf16[4,256,1024]{2,1,0:T(8,128)(2,1)} %stack.38.weight_ref), custom_call_target="tpu_custom_call" | custom-call | flops 536870912 | bytes 2097152 | tf_op jit(solution)/shard_map/base_own/pallas_call | solution.py:447
  105.9 1.1 collective-permute-done.6.weight_ref
  107.0 2.5 %base_forward.1 = (f32[128,256]{1,0:T(8,128)S(1)}, f32[128,256]{1,0:T(8,128)S(1)}, f32[128,256]{1,0:T(8,128)S(1)}, f32[128,256]{1,0:T(8,128)S(1)}) custom-call(s32[9]{0:T(128)S(1)} %stack.37.order_ref, bf16[128,2048]{1,0:T(8,128)(2,1)S(1)} %copy-done.1, f32[4,128,256]{2,1,0:T(8,128)S(1)} %get-tuple-element.40.totals_ref, ...), custom_call_target="tpu_custom_call" | custom-call | flops 268435456 | bytes 2097152 | tf_op jit(solution)/shard_map/base_forward/pallas_call | solution.py:456
  109.5 2.5 %collective-permute-start.7 = (f32[128,256]{1,0:T(8,128)S(1)}, f32[128,256]{1,0:T(8,128)S(1)}, u32[]{:S(2)}, u32[]{:S(2)}) collective-permute-start(f32[128,256]{1,0:T(8,128)S(1)} %get-tuple-element.42), channel_id=1, source_target_pairs={{0,1},{1,2},{2,3},{3,0},{4,5},{5,6},{6,7},{7,4},{8,9},{9,10},{10,1... | collective-permute-start | bytes 393224 | tf_op jit(solution)/shard_map/ppermute | solution.py:341
  112.0 4.3 %collective-permute-start.8 = (f32[128,256]{1,0:T(8,128)S(1)}, f32[128,256]{1,0:T(8,128)S(1)}, u32[]{:S(2)}, u32[]{:S(2)}) collective-permute-start(f32[128,256]{1,0:T(8,128)S(1)} %get-tuple-element.43), channel_id=1, source_target_pairs={{0,2},{1,3},{2,0},{3,1},{4,6},{5,7},{6,4},{7,5},{8,10},{9,11},{10,... | collective-permute-start | bytes 393224 | tf_op jit(solution)/shard_map/ppermute | solution.py:341
  116.3 3.1 %collective-permute-start.9 = (f32[128,256]{1,0:T(8,128)S(1)}, f32[128,256]{1,0:T(8,128)S(1)}, u32[]{:S(2)}, u32[]{:S(2)}) collective-permute-start(f32[128,256]{1,0:T(8,128)S(1)} %get-tuple-element.44), channel_id=1, source_target_pairs={{0,3},{1,0},{2,1},{3,2},{4,7},{5,4},{6,5},{7,6},{8,11},{9,8},{10,9... | collective-permute-start | bytes 393224 | tf_op jit(solution)/shard_map/ppermute | solution.py:341
  119.4 1.0 base_input.1.input_ref
  120.4 0.0 copy-start
  120.5 1.0 copy-done
  121.5 0.0 collective-permute-done.7.refs_1_
  121.5 0.0 collective-permute-done.8.refs_2_
  121.5 1.0 collective-permute-done.9.refs_3_
  122.5 0.6 copy-done.3
  123.1 2.4 %all-to-all-done.2.returned_ref = bf16[128,2,2304]{2,1,0:T(2,128)(2,1)} async-done(((bf16[128,2,2304]{2,1,0:T(2,128)(2,1)}), bf16[128,2,2304]{2,1,0:T(2,128)(2,1)}, u32[]{:S(2)}, u32[]{:S(2)}) %all-to-all-start.2) | async-done | bytes 1179680 | tf_op jit(solution)/shard_map/all_to_all | solution.py:418
  125.5 2.8 %finish.1 = (bf16[128,256]{1,0:T(8,128)(2,1)}, bf16[128,2048]{1,0:T(8,128)(2,1)}) custom-call(bf16[256,128]{1,0:T(8,128)(2,1)} %get-tuple-element.26.picks_ref, bf16[128,2,2304]{2,1,0:T(2,128)(2,1)} %all-to-all-done.2.returned_ref, f32[128,2048]{1,0:T(8,128)} %copy-done, f32[128,256]{1,0:T(8,128)} %copy-done.3), custom_call_target="tpu_custom_call" | custom-call | flops 150994944 | bytes 1179648 | tf_op jit(solution)/shard_map/finish/pallas_call | solution.py:486
  (5 shorter events, 0.0 us)
Async XLA Ops:
  3.5 18.6 %copy-start.6 = (bf16[128,256]{1,0:T(8,128)(2,1)S(1)}, bf16[128,256]{1,0:T(8,128)(2,1)}, u32[]{:S(2)}) copy-start(bf16[128,256]{1,0:T(8,128)(2,1)} %own_ref.1) | copy-start | bytes 196612
  3.5 62.3 %copy-start.4 = (bf16[1,2048,64]{1,2,0:T(8,128)(2,1)S(1)}, bf16[1,2048,64]{1,2,0:T(8,128)(2,1)}, u32[]{:S(2)}) copy-start(bf16[1,2048,64]{1,2,0:T(8,128)(2,1)} %param.10) | copy-start | bytes 786436
  3.5 62.3 %copy-start.5 = (bf16[1,64,256]{2,1,0:T(8,128)(2,1)S(1)}, bf16[1,64,256]{2,1,0:T(8,128)(2,1)}, u32[]{:S(2)}) copy-start(bf16[1,64,256]{2,1,0:T(8,128)(2,1)} %param.11) | copy-start | bytes 98308
  3.6 62.3 %all-to-all-start = ((bf16[128,2,3328]{2,1,0:T(2,128)(2,1)}), bf16[128,2,3328]{2,1,0:T(2,128)(2,1)S(1)}, u32[]{:S(2)}, u32[]{:S(2)}) async-start(bf16[128,2,3328]{2,1,0:T(2,128)(2,1)} %get-tuple-element.27), calls=%async_computation | async-start | bytes 3407872 | tf_op jit(solution)/shard_map/all_to_all | solution.py:375
  22.1 10.6 %collective-permute-start = (bf16[128,256]{1,0:T(8,128)(2,1)S(1)}, bf16[128,256]{1,0:T(8,128)(2,1)S(1)}, u32[]{:S(2)}, u32[]{:S(2)}) collective-permute-start(bf16[128,256]{1,0:T(8,128)(2,1)S(1)} %copy-done.6), channel_id=1, source_target_pairs={{0,1},{1,2},{2,3},{3,0},{4,5},{5,6},{6,7},{7,4},{8,9},{9,10},{10,1... | collective-permute-start | bytes 196616 | tf_op jit(solution)/shard_map/ppermute | solution.py:341
  25.3 7.5 %collective-permute-start.1 = (bf16[128,256]{1,0:T(8,128)(2,1)S(1)}, bf16[128,256]{1,0:T(8,128)(2,1)S(1)}, u32[]{:S(2)}, u32[]{:S(2)}) collective-permute-start(bf16[128,256]{1,0:T(8,128)(2,1)S(1)} %copy-done.6), channel_id=1, source_target_pairs={{0,2},{1,3},{2,0},{3,1},{4,6},{5,7},{6,4},{7,5},{8,10},{9,11},{10,... | collective-permute-start | bytes 196616 | tf_op jit(solution)/shard_map/ppermute | solution.py:341
  29.6 5.3 %collective-permute-start.2 = (bf16[128,256]{1,0:T(8,128)(2,1)S(1)}, bf16[128,256]{1,0:T(8,128)(2,1)S(1)}, u32[]{:S(2)}, u32[]{:S(2)}) collective-permute-start(bf16[128,256]{1,0:T(8,128)(2,1)S(1)} %copy-done.6), channel_id=1, source_target_pairs={{0,3},{1,0},{2,1},{3,2},{4,7},{5,4},{6,5},{7,6},{8,11},{9,8},{10,9... | collective-permute-start | bytes 196616 | tf_op jit(solution)/shard_map/ppermute | solution.py:341
  67.2 14.9 %all-to-all-start.1 = ((f32[4,256,128]{2,1,0:T(8,128)}), f32[4,256,128]{2,1,0:T(8,128)S(1)}, u32[]{:S(2)}, u32[]{:S(2)}) async-start(f32[4,256,128]{2,1,0:T(8,128)} %low_rank.1), calls=%async_computation.1 | async-start | bytes 1048576 | tf_op jit(solution)/shard_map/all_to_all | solution.py:396
  71.2 22.2 %collective-permute-start.3 = (bf16[256,1024]{1,0:T(8,128)(2,1)S(1)}, bf16[256,1024]{1,0:T(8,128)(2,1)}, u32[]{:S(2)}, u32[]{:S(2)}) collective-permute-start(bf16[256,1024]{1,0:T(8,128)(2,1)S(1)} %weight.1.refs_0_), channel_id=1, source_target_pairs={{0,64},{4,68},{8,72},{12,76},{16,80},{20,84},{24,88},{28,92},{32,9... | collective-permute-start | bytes 1572872 | tf_op jit(solution)/shard_map/ppermute | solution.py:300
  73.6 19.9 %collective-permute-start.4 = (bf16[256,1024]{1,0:T(8,128)(2,1)S(1)}, bf16[256,1024]{1,0:T(8,128)(2,1)}, u32[]{:S(2)}, u32[]{:S(2)}) collective-permute-start(bf16[256,1024]{1,0:T(8,128)(2,1)S(1)} %weight.1.refs_0_), channel_id=1, source_target_pairs={{0,448},{4,452},{8,456},{12,460},{16,464},{20,468},{24,472},{28,47... | collective-permute-start | bytes 1572872 | tf_op jit(solution)/shard_map/ppermute | solution.py:300
  77.8 15.7 %collective-permute-start.5 = (bf16[256,1024]{1,0:T(8,128)(2,1)S(1)}, bf16[256,1024]{1,0:T(8,128)(2,1)}, u32[]{:S(2)}, u32[]{:S(2)}) collective-permute-start(bf16[256,1024]{1,0:T(8,128)(2,1)S(1)} %weight.1.refs_0_), channel_id=1, source_target_pairs={{0,8},{4,12},{8,16},{12,20},{16,24},{20,28},{24,32},{28,36},{32,40... | collective-permute-start | bytes 1572872 | tf_op jit(solution)/shard_map/ppermute | solution.py:300
  82.8 1.0 copy-start.2
  83.8 41.7 %all-to-all-start.2 = ((bf16[128,2,2304]{2,1,0:T(2,128)(2,1)}), bf16[128,2,2304]{2,1,0:T(2,128)(2,1)}, u32[]{:S(2)}, u32[]{:S(2)}) async-start(bf16[128,2,2304]{2,1,0:T(2,128)(2,1)} %copy-done.2), calls=%async_computation.2 | async-start | bytes 2359296 | tf_op jit(solution)/shard_map/all_to_all | solution.py:418
  93.4 9.8 %copy-start.1 = (bf16[128,2048]{1,0:T(8,128)(2,1)S(1)}, bf16[128,2048]{1,0:T(8,128)(2,1)}, u32[]{:S(2)}) copy-start(bf16[128,2048]{1,0:T(8,128)(2,1)} %tokens_ref.3) | copy-start | bytes 1572868
  96.3 10.7 %collective-permute-start.6 = (bf16[4,256,1024]{2,1,0:T(8,128)(2,1)}, bf16[4,256,1024]{2,1,0:T(8,128)(2,1)S(1)}, u32[]{:S(2)}, u32[]{:S(2)}) collective-permute-start(bf16[4,256,1024]{2,1,0:T(8,128)(2,1)} %stack.38.weight_ref), channel_id=1, source_target_pairs={{0,4},{4,0},{8,12},{12,8},{16,20},{20,16},{24,28},{28,24},{32,36},... | collective-permute-start | bytes 6291464 | tf_op jit(solution)/shard_map/ppermute | solution.py:304
  109.5 12.0 %collective-permute-start.7 = (f32[128,256]{1,0:T(8,128)S(1)}, f32[128,256]{1,0:T(8,128)S(1)}, u32[]{:S(2)}, u32[]{:S(2)}) collective-permute-start(f32[128,256]{1,0:T(8,128)S(1)} %get-tuple-element.42), channel_id=1, source_target_pairs={{0,1},{1,2},{2,3},{3,0},{4,5},{5,6},{6,7},{7,4},{8,9},{9,10},{10,1... | collective-permute-start | bytes 393224 | tf_op jit(solution)/shard_map/ppermute | solution.py:341
  112.0 9.4 %collective-permute-start.8 = (f32[128,256]{1,0:T(8,128)S(1)}, f32[128,256]{1,0:T(8,128)S(1)}, u32[]{:S(2)}, u32[]{:S(2)}) collective-permute-start(f32[128,256]{1,0:T(8,128)S(1)} %get-tuple-element.43), channel_id=1, source_target_pairs={{0,2},{1,3},{2,0},{3,1},{4,6},{5,7},{6,4},{7,5},{8,10},{9,11},{10,... | collective-permute-start | bytes 393224 | tf_op jit(solution)/shard_map/ppermute | solution.py:341
  116.3 6.1 %collective-permute-start.9 = (f32[128,256]{1,0:T(8,128)S(1)}, f32[128,256]{1,0:T(8,128)S(1)}, u32[]{:S(2)}, u32[]{:S(2)}) collective-permute-start(f32[128,256]{1,0:T(8,128)S(1)} %get-tuple-element.44), channel_id=1, source_target_pairs={{0,3},{1,0},{2,1},{3,2},{4,7},{5,4},{6,5},{7,6},{8,11},{9,8},{10,9... | collective-permute-start | bytes 393224 | tf_op jit(solution)/shard_map/ppermute | solution.py:341
  120.4 1.0 copy-start
  122.5 0.6 copy-start.3

commit v5 on v4

--- a/solution.py
+++ b/solution.py
@@ -174,15 +174,16 @@
     out_ref[...] = flat(arrived_ref[:, :, arrived_ref.shape[2] - out_ref.shape[1] :])
 
 
-def back_kernel(parts_ref, down_ref, upper_ref, low_hbm, out_ref, low_ref, sem):
-    rank, width = down_ref.shape
+def summed(parts_ref):
     total = parts_ref[0]
     for part in range(1, parts_ref.shape[0]):
         total = total + parts_ref[part]
-    low = total.astype(bf16)
-    low_ref[...] = low
-    store = pltpu.make_async_copy(low_ref, low_hbm, sem)
-    store.start()
+    return total.astype(bf16)
+
+
+def back_kernel(parts_ref, down_ref, upper_ref, out_ref):
+    rank, width = down_ref.shape
+    low = summed(parts_ref)
     for start in range(0, width, CHUNK):
         at = pl.ds(start, CHUNK)
         out_ref[:, :, at] = paired(
@@ -191,13 +192,12 @@
     out_ref[:, :, width:] = paired(
         (adapter_scale * contract(low[:, :rank], upper_ref[...], 1, 0)).astype(bf16)
     )
-    store.wait()
-
-
-def factor_kernel(arrived_ref, low_ref, down_out_ref, upper_out_ref):
+
+
+def factor_kernel(arrived_ref, parts_ref, down_out_ref, upper_out_ref):
     rank, width = down_out_ref.shape
     features = upper_out_ref.shape[1]
-    low = low_ref[...]
+    low = summed(parts_ref)
     for start in range(0, width, CHUNK):
         at = pl.ds(start, CHUNK)
         down_out_ref[:, at] = adapter_scale * contract(low[:, rank:], flat(arrived_ref[:, :, at]), 0, 0)
@@ -206,22 +206,24 @@
     )
 
 
-def sum_kernel(*refs):
-    total = refs[0][...]
-    for ref in refs[1:-1]:
-        total = total + ref[...]
-    refs[-1][...] = total
-
-
-def finish_kernel(picks_ref, returned_ref, input_ref, base_ref, out_ref, grad_ref):
-    width = input_ref.shape[1]
-    picks = picks_ref[...]
+def finish_kernel(returned_ref, ready_ref, out_ref, grad_ref):
+    token_count, width = grad_ref.shape
+    features = out_ref.shape[1]
+    start = width + features
+    picks = jnp.concatenate(
+        [
+            ready_ref[:, start + half * token_count : start + (half + 1) * token_count].astype(bf16)
+            for half in range(2)
+        ],
+        axis=0,
+    )
     for start in range(0, width, CHUNK):
         at = pl.ds(start, CHUNK)
         grad_ref[:, at] = (
-            input_ref[:, at] + contract(picks, flat(returned_ref[:, :, at]), 0, 0)
+            ready_ref[:, at] + contract(picks, flat(returned_ref[:, :, at]), 0, 0)
         ).astype(bf16)
-    out_ref[...] = (base_ref[...] + contract(picks, flat(returned_ref[:, :, width:]), 0, 0)).astype(bf16)
+    at = pl.ds(width, features)
+    out_ref[...] = (ready_ref[:, at] + contract(picks, flat(returned_ref[:, :, at]), 0, 0)).astype(bf16)
 
 
 def stack_kernel(*refs):
@@ -282,12 +284,22 @@
         forward_ref[...] = whole_ref[lax.rem(order_ref[2 * CLASSES] + shift, parts)]
 
 
-def input_kernel(order_ref, grads_ref, weight_ref, own_ref, out_ref, input_ref):
+def ready_kernel(order_ref, grads_ref, weight_ref, own_ref, picks_ref, *refs):
+    *part_refs, out_ref, input_ref = refs
     input_half(grads_ref, weight_ref, input_ref)
-    depth = own_ref.shape[2]
-    for at in range(CLASSES):
+    classes, token_count, depth = own_ref.shape
+    for at in range(classes):
         out_ref[:, columns_of(order_ref, at, depth)] = own_ref[at]
-        out_ref[:, columns_of(order_ref, CLASSES + at, depth)] = input_ref[at]
+        out_ref[:, columns_of(order_ref, classes + at, depth)] = input_ref[at]
+    total = part_refs[0][...]
+    for ref in part_refs[1:]:
+        total = total + ref[...]
+    start = 2 * classes * depth
+    out_ref[:, start : start + total.shape[1]] = total
+    start += total.shape[1]
+    for half in range(2):
+        rows = picks_ref[half * token_count : (half + 1) * token_count]
+        out_ref[:, start + half * token_count : start + (half + 1) * token_count] = rows.astype(f32)
 
 
 def neighbour(value, dz, dy):
@@ -403,17 +415,12 @@
     )(after_low)
     near = (weight, neighbour(weight, 1, 0), neighbour(weight, -1, 0), neighbour(weight, 0, 1))
 
-    low, back = call(
+    back = call(
         back_kernel,
-        (
-            jax.ShapeDtypeStruct((slots, 2 * rank), bf16),
-            jax.ShapeDtypeStruct((owners, capacity, width + features), bf16),
-        ),
+        jax.ShapeDtypeStruct((owners, capacity, width + features), bf16),
         "back",
         LONG * 400,
         LONG,
-        out_specs=(hbm, vmem),
-        scratch_shapes=[pltpu.VMEM((slots, 2 * rank), bf16), pltpu.SemaphoreType.DMA],
     )(low_parts, down, upper)
     returned = lax.all_to_all(back, "dp", split_axis=0, concat_axis=0, tiled=True)
 
@@ -426,7 +433,7 @@
         "factor_gradients",
         LONG * 400,
         LONG,
-    )(arrived, low)
+    )(arrived, low_parts)
 
     near = lax.optimization_barrier((down_out, near))[1]
     gathered = call(
@@ -463,25 +470,17 @@
         out_specs=[vmem] * parts,
         scratch_shapes=[pltpu.VMEM((parts, token_count, features), f32)],
     )(order, tokens, totals, swapped)
-    plain_input = call(
-        input_kernel,
-        jax.ShapeDtypeStruct((token_count, width), f32),
-        "base_input",
+    sums = [forward[0]] + [around(forward[shift], shift) for shift in range(1, parts)]
+    ready = call(
+        ready_kernel,
+        jax.ShapeDtypeStruct((token_count, width + features + slots), f32),
+        "ready",
         half_work,
         width * all_features,
-        in_specs=[smem] + [vmem] * 3,
+        in_specs=[smem] + [vmem] * (4 + parts),
         out_specs=vmem,
         scratch_shapes=[pltpu.VMEM((CLASSES, token_count, depth), f32)],
-    )(order, whole_gradient, swapped, own_input)
-    sums = [forward[0]] + [around(forward[shift], shift) for shift in range(1, parts)]
-
-    plain_output = call(
-        sum_kernel,
-        jax.ShapeDtypeStruct((token_count, features), f32),
-        "sum",
-        0,
-        4 * (parts + 1) * token_count * features,
-    )(*sums)
+    )(order, whole_gradient, swapped, own_input, picks, *sums)
 
     projected, activation_gradient = call(
         finish_kernel,
@@ -492,8 +491,7 @@
         "finish",
         2 * slots * token_count * (width + features),
         2 * slots * (width + features),
-        limit=WHOLE_VMEM,
-    )(picks, returned, plain_input, plain_output)
+    )(returned, ready)
     return (projected, activation_gradient, down_out.T[None], upper_out[None])
 
 

time: 129 us -> 129 us (level)
  local copies, waits for them, and re-layouts: 2.77 us -> 1.15 us
    ppermute x6, waiting for transfers between devices: 3.2 us -> 5.22 us  [around(): lax.ppermute(value, 'mp', [(i, (i + shift) % parts) for i in range(parts)])]
    unnamed x14 -> x16, local copies, waits for them, and re-layouts: 2.69 us -> 1.06 us
  transfers between devices with their start and end apart: 13 -> 13, of which waited for: 5 -> 6; matrix products, arithmetic and copies ran while one was open for 0% -> 0% of each run, Pallas kernels for 9% -> 9%
where the time goes in v5:
time: 129 us; the launch traced here: 128 us
  starting transfers between devices  69.3 us (54%)
  waiting for transfers between devices  38.3 us (30%)
  Pallas kernels  18 us (14%)
    all_to_all x1, waiting for transfers between devices, body(): lax.all_to_all(outgoing, 'dp', split_axis=0, concat_axis=0, tiled=True)  30.4 us
    ppermute x6, starting transfers between devices, around(): lax.ppermute(value, 'mp', [(i, (i + shift) % parts) for i in range(parts)])  20.4 us
    all_to_all x1, starting transfers between devices, body(): lax.all_to_all(outgoing, 'dp', split_axis=0, concat_axis=0, tiled=True)  18.6 us
    ppermute x3, starting transfers between devices, neighbour(): return lax.ppermute(value, 'dp', pairs)  10.8 us
    all_to_all x1, starting transfers between devices, body(): lax.all_to_all(back, 'dp', split_axis=0, concat_axis=0, tiled=True)  8.4 us
    ppermute x1, starting transfers between devices, other_core(): lax.ppermute(value, 'dp', [(i, i ^ 1) for i in range(N_Z * N_Y * N_C)])  7.14 us
    ppermute x6, waiting for transfers between devices, around(): lax.ppermute(value, 'mp', [(i, (i + shift) % parts) for i in range(parts)])  5.22 us
    all_to_all x1, starting transfers between devices, body(): lax.all_to_all(low_parts, 'mp', split_axis=0, concat_axis=0, tiled=True)  4.02 us
  transfers between devices with their start and end apart: 13, of which 6 were waited for; matrix products, arithmetic and copies ran while one was open for 0% of the time, Pallas kernels for 9%

profile of v5, /device:TPU:1, one launch (start us, length us, event | category | flops | bytes accessed | tf_op | source)
XLA Modules:
  0.0 127.8 jit_solution(4207459147299823949)
XLA Ops:
  0.6 2.9 %spread.1 = (bf16[128,2,3328]{2,1,0:T(2,128)(2,1)}, bf16[256,128]{1,0:T(8,128)(2,1)}) custom-call(s32[1,128]{1,0:T(1,128)} %bitcast.25, s32[1,128]{1,0:T(1,128)} %bitcast.26, bf16[128,2048]{1,0:T(8,128)(2,1)} %tokens_ref.3, bf16[128,256]{1,0:T(8,128)(2,1)} %own_ref.1, bf16[8,2048]{1,0:T(8,128)(2,1)} %bitcast.24), custom_call_target="tpu_custom_call" | custom-call | flops 218103808 | bytes 2555904 | tf_op jit(solution)/shard_map/spread/pallas_call | solution.py:357
  3.5 0.0 copy-start.7
  3.5 0.0 copy-start.4
  3.5 0.0 copy-start.6
  3.5 18.6 %all-to-all-start = ((bf16[128,2,3328]{2,1,0:T(2,128)(2,1)}), bf16[128,2,3328]{2,1,0:T(2,128)(2,1)S(1)}, u32[]{:S(2)}, u32[]{:S(2)}) async-start(bf16[128,2,3328]{2,1,0:T(2,128)(2,1)} %get-tuple-element.24), calls=%async_computation | async-start | bytes 3407872 | tf_op jit(solution)/shard_map/all_to_all | solution.py:387
  22.1 3.1 %collective-permute-start = (bf16[128,256]{1,0:T(8,128)(2,1)S(1)}, bf16[128,256]{1,0:T(8,128)(2,1)S(1)}, u32[]{:S(2)}, u32[]{:S(2)}) collective-permute-start(bf16[128,256]{1,0:T(8,128)(2,1)S(1)} %copy-done.7), channel_id=1, source_target_pairs={{0,1},{1,2},{2,3},{3,0},{4,5},{5,6},{6,7},{7,4},{8,9},{9,10},{10,1... | collective-permute-start | bytes 196616 | tf_op jit(solution)/shard_map/ppermute | solution.py:353
  25.2 4.4 %collective-permute-start.1 = (bf16[128,256]{1,0:T(8,128)(2,1)S(1)}, bf16[128,256]{1,0:T(8,128)(2,1)S(1)}, u32[]{:S(2)}, u32[]{:S(2)}) collective-permute-start(bf16[128,256]{1,0:T(8,128)(2,1)S(1)} %copy-done.7), channel_id=1, source_target_pairs={{0,2},{1,3},{2,0},{3,1},{4,6},{5,7},{6,4},{7,5},{8,10},{9,11},{10,... | collective-permute-start | bytes 196616 | tf_op jit(solution)/shard_map/ppermute | solution.py:353
  29.6 3.1 %collective-permute-start.2 = (bf16[128,256]{1,0:T(8,128)(2,1)S(1)}, bf16[128,256]{1,0:T(8,128)(2,1)S(1)}, u32[]{:S(2)}, u32[]{:S(2)}) collective-permute-start(bf16[128,256]{1,0:T(8,128)(2,1)S(1)} %copy-done.7), channel_id=1, source_target_pairs={{0,3},{1,0},{2,1},{3,2},{4,7},{5,4},{6,5},{7,6},{8,11},{9,8},{10,9... | collective-permute-start | bytes 196616 | tf_op jit(solution)/shard_map/ppermute | solution.py:353
  32.7 0.0 collective-permute-done.a_ref
  32.7 0.0 collective-permute-done.1.b_ref
  32.7 2.2 %collective-permute-done.2.c_ref = bf16[128,256]{1,0:T(8,128)(2,1)S(1)} collective-permute-done((bf16[128,256]{1,0:T(8,128)(2,1)S(1)}, bf16[128,256]{1,0:T(8,128)(2,1)S(1)}, u32[]{:S(2)}, u32[]{:S(2)}) %collective-permute-start.2) | collective-permute-done | bytes 65568 | tf_op jit(solution)/shard_map/ppermute | solution.py:353
  34.9 0.5 order.1.grads_ref
  35.4 0.0 copy-start.2
  35.4 30.4 %all-to-all-done.arrived_ref = bf16[128,2,3328]{2,1,0:T(2,128)(2,1)S(1)} async-done(((bf16[128,2,3328]{2,1,0:T(2,128)(2,1)}), bf16[128,2,3328]{2,1,0:T(2,128)(2,1)S(1)}, u32[]{:S(2)}, u32[]{:S(2)}) %all-to-all-start) | async-done | bytes 1703968 | tf_op jit(solution)/shard_map/all_to_all | solution.py:387
  65.8 1.3 %low_rank.1 = f32[4,256,128]{2,1,0:T(8,128)} custom-call(bf16[128,2,3328]{2,1,0:T(2,128)(2,1)S(1)} %all-to-all-done.arrived_ref, bf16[64,2048]{1,0:T(8,128)(2,1)S(1)} %bitcast.20, bf16[64,256]{1,0:T(8,128)(2,1)S(1)} %bitcast.22), custom_call_target="tpu_custom_call" | custom-call | flops 75497472 | bytes 1703936 | tf_op jit(solution)/shard_map/low_rank/pallas_call | solution.py:400
  67.1 4.0 %all-to-all-start.1 = ((f32[4,256,128]{2,1,0:T(8,128)}), f32[4,256,128]{2,1,0:T(8,128)S(1)}, u32[]{:S(2)}, u32[]{:S(2)}) async-start(f32[4,256,128]{2,1,0:T(8,128)} %low_rank.1), calls=%async_computation.1 | async-start | bytes 1048576 | tf_op jit(solution)/shard_map/all_to_all | solution.py:408
  71.2 0.1 weight.1.refs_0_
  71.2 2.3 %collective-permute-start.3 = (bf16[256,1024]{1,0:T(8,128)(2,1)S(1)}, bf16[256,1024]{1,0:T(8,128)(2,1)}, u32[]{:S(2)}, u32[]{:S(2)}) collective-permute-start(bf16[256,1024]{1,0:T(8,128)(2,1)S(1)} %weight.1.refs_0_), channel_id=1, source_target_pairs={{0,64},{4,68},{8,72},{12,76},{16,80},{20,84},{24,88},{28,92},{32,9... | collective-permute-start | bytes 1572872 | tf_op jit(solution)/shard_map/ppermute | solution.py:312
  73.5 4.2 %collective-permute-start.4 = (bf16[256,1024]{1,0:T(8,128)(2,1)S(1)}, bf16[256,1024]{1,0:T(8,128)(2,1)}, u32[]{:S(2)}, u32[]{:S(2)}) collective-permute-start(bf16[256,1024]{1,0:T(8,128)(2,1)S(1)} %weight.1.refs_0_), channel_id=1, source_target_pairs={{0,448},{4,452},{8,456},{12,460},{16,464},{20,468},{24,472},{28,47... | collective-permute-start | bytes 1572872 | tf_op jit(solution)/shard_map/ppermute | solution.py:312
  77.7 4.3 %collective-permute-start.5 = (bf16[256,1024]{1,0:T(8,128)(2,1)S(1)}, bf16[256,1024]{1,0:T(8,128)(2,1)}, u32[]{:S(2)}, u32[]{:S(2)}) collective-permute-start(bf16[256,1024]{1,0:T(8,128)(2,1)S(1)} %weight.1.refs_0_), channel_id=1, source_target_pairs={{0,8},{4,12},{8,16},{12,20},{16,24},{20,28},{24,32},{28,36},{32,40... | collective-permute-start | bytes 1572872 | tf_op jit(solution)/shard_map/ppermute | solution.py:312
  82.1 0.0 all-to-all-done.1.parts_ref
  82.1 0.5 back.1
  82.6 0.0 copy-start.1
  82.6 1.0 copy-done.1
  83.7 8.4 %all-to-all-start.2 = ((bf16[128,2,2304]{2,1,0:T(2,128)(2,1)}), bf16[128,2,2304]{2,1,0:T(2,128)(2,1)}, u32[]{:S(2)}, u32[]{:S(2)}) async-start(bf16[128,2,2304]{2,1,0:T(2,128)(2,1)} %copy-done.1), calls=%async_computation.2 | async-start | bytes 2359296 | tf_op jit(solution)/shard_map/all_to_all | solution.py:425
  92.1 1.2 factor_gradients.1
  93.3 0.0 collective-permute-done.3.refs_1_
  93.3 0.0 collective-permute-done.4.refs_2_
  93.3 0.0 collective-permute-done.5.refs_3_
  93.3 0.0 copy-start
  93.3 2.9 %stack.38.weight_ref = bf16[4,256,1024]{2,1,0:T(8,128)(2,1)} custom-call(bf16[256,1024]{1,0:T(8,128)(2,1)S(1)} %weight.1.refs_0_, bf16[256,1024]{1,0:T(8,128)(2,1)} %collective-permute-done.3.refs_1_, bf16[256,1024]{1,0:T(8,128)(2,1)} %collective-permute-done.4.refs_2_, bf16[256,1024]{1,0:T(8,128)(2,1)} %collective-permute-done.5.refs_3_), custom_call_target="tpu_custom_call" | custom-call | bytes 4194304 | tf_op jit(solution)/shard_map/stack/pallas_call | solution.py:439
  96.2 7.1 %collective-permute-start.6 = (bf16[4,256,1024]{2,1,0:T(8,128)(2,1)}, bf16[4,256,1024]{2,1,0:T(8,128)(2,1)S(1)}, u32[]{:S(2)}, u32[]{:S(2)}) collective-permute-start(bf16[4,256,1024]{2,1,0:T(8,128)(2,1)} %stack.38.weight_ref), channel_id=1, source_target_pairs={{0,4},{4,0},{8,12},{12,8},{16,20},{20,16},{24,28},{28,24},{32,36},... | collective-permute-start | bytes 6291464 | tf_op jit(solution)/shard_map/ppermute | solution.py:316
  103.5 0.1 stack.37.order_ref
  103.6 0.0 copy-done
  103.6 2.7 %base_own.1 = (f32[4,128,256]{2,1,0:T(8,128)S(1)}, f32[4,128,256]{2,1,0:T(8,128)S(1)}) custom-call(s32[9]{0:T(128)S(1)} %stack.37.order_ref, bf16[128,2048]{1,0:T(8,128)(2,1)S(1)} %copy-done, bf16[4,128,256]{2,1,0:T(8,128)(2,1)S(1)} %order.1.grads_ref, bf16[4,256,1024]{2,1,0:T(8,128)(2,1)} %stack.38.weight_ref), custom_call_target="tpu_custom_call" | custom-call | flops 536870912 | bytes 2097152 | tf_op jit(solution)/shard_map/base_own/pallas_call | solution.py:454
  106.3 0.0 copy-start.3
  106.3 0.0 copy-start.5
  106.3 1.0 collective-permute-done.6.weight_ref
  107.3 2.5 %base_forward.1 = (f32[128,256]{1,0:T(8,128)S(1)}, f32[128,256]{1,0:T(8,128)S(1)}, f32[128,256]{1,0:T(8,128)S(1)}, f32[128,256]{1,0:T(8,128)S(1)}) custom-call(s32[9]{0:T(128)S(1)} %stack.37.order_ref, bf16[128,2048]{1,0:T(8,128)(2,1)S(1)} %copy-done, f32[4,128,256]{2,1,0:T(8,128)S(1)} %get-tuple-element.36.totals_ref, ...), custom_call_target="tpu_custom_call" | custom-call | flops 268435456 | bytes 2097152 | tf_op jit(solution)/shard_map/base_forward/pallas_call | solution.py:463
  109.8 2.4 %collective-permute-start.7 = (f32[128,256]{1,0:T(8,128)S(1)}, f32[128,256]{1,0:T(8,128)S(1)}, u32[]{:S(2)}, u32[]{:S(2)}) collective-permute-start(f32[128,256]{1,0:T(8,128)S(1)} %get-tuple-element.38), channel_id=1, source_target_pairs={{0,1},{1,2},{2,3},{3,0},{4,5},{5,6},{6,7},{7,4},{8,9},{9,10},{10,1... | collective-permute-start | bytes 393224 | tf_op jit(solution)/shard_map/ppermute | solution.py:353
  112.2 4.3 %collective-permute-start.8 = (f32[128,256]{1,0:T(8,128)S(1)}, f32[128,256]{1,0:T(8,128)S(1)}, u32[]{:S(2)}, u32[]{:S(2)}) collective-permute-start(f32[128,256]{1,0:T(8,128)S(1)} %get-tuple-element.39), channel_id=1, source_target_pairs={{0,2},{1,3},{2,0},{3,1},{4,6},{5,7},{6,4},{7,5},{8,10},{9,11},{10,... | collective-permute-start | bytes 393224 | tf_op jit(solution)/shard_map/ppermute | solution.py:353
  116.5 3.1 %collective-permute-start.9 = (f32[128,256]{1,0:T(8,128)S(1)}, f32[128,256]{1,0:T(8,128)S(1)}, u32[]{:S(2)}, u32[]{:S(2)}) collective-permute-start(f32[128,256]{1,0:T(8,128)S(1)} %get-tuple-element.40), channel_id=1, source_target_pairs={{0,3},{1,0},{2,1},{3,2},{4,7},{5,4},{6,5},{7,6},{8,11},{9,8},{10,9... | collective-permute-start | bytes 393224 | tf_op jit(solution)/shard_map/ppermute | solution.py:353
  119.6 0.0 collective-permute-done.7.refs_1_
  119.7 1.1 collective-permute-done.8.refs_2_
  120.8 1.9 %collective-permute-done.9.refs_3_ = f32[128,256]{1,0:T(8,128)S(1)} collective-permute-done((f32[128,256]{1,0:T(8,128)S(1)}, f32[128,256]{1,0:T(8,128)S(1)}, u32[]{:S(2)}, u32[]{:S(2)}) %collective-permute-start.9) | collective-permute-done | bytes 131104 | tf_op jit(solution)/shard_map/ppermute | solution.py:353
  122.7 1.0 ready.1.ready_ref
  123.7 1.6 %all-to-all-done.2.returned_ref = bf16[128,2,2304]{2,1,0:T(2,128)(2,1)} async-done(((bf16[128,2,2304]{2,1,0:T(2,128)(2,1)}), bf16[128,2,2304]{2,1,0:T(2,128)(2,1)}, u32[]{:S(2)}, u32[]{:S(2)}) %all-to-all-start.2) | async-done | bytes 1179680 | tf_op jit(solution)/shard_map/all_to_all | solution.py:425
  125.3 2.4 %finish.1 = (bf16[128,256]{1,0:T(8,128)(2,1)}, bf16[128,2048]{1,0:T(8,128)(2,1)}) custom-call(bf16[128,2,2304]{2,1,0:T(2,128)(2,1)} %all-to-all-done.2.returned_ref, f32[128,2560]{1,0:T(8,128)S(1)} %ready.1.ready_ref), custom_call_target="tpu_custom_call" | custom-call | flops 150994944 | bytes 1179648 | tf_op jit(solution)/shard_map/finish/pallas_call | solution.py:485
  (6 shorter events, 0.0 us)
Async XLA Ops:
  3.5 18.6 %copy-start.7 = (bf16[128,256]{1,0:T(8,128)(2,1)S(1)}, bf16[128,256]{1,0:T(8,128)(2,1)}, u32[]{:S(2)}) copy-start(bf16[128,256]{1,0:T(8,128)(2,1)} %own_ref.1) | copy-start | bytes 196612
  3.5 62.3 %copy-start.4 = (bf16[1,2048,64]{1,2,0:T(8,128)(2,1)S(1)}, bf16[1,2048,64]{1,2,0:T(8,128)(2,1)}, u32[]{:S(2)}) copy-start(bf16[1,2048,64]{1,2,0:T(8,128)(2,1)} %param.10) | copy-start | bytes 786436
  3.5 62.3 %copy-start.6 = (bf16[1,64,256]{2,1,0:T(8,128)(2,1)S(1)}, bf16[1,64,256]{2,1,0:T(8,128)(2,1)}, u32[]{:S(2)}) copy-start(bf16[1,64,256]{2,1,0:T(8,128)(2,1)} %param.11) | copy-start | bytes 98308
  3.5 62.3 %all-to-all-start = ((bf16[128,2,3328]{2,1,0:T(2,128)(2,1)}), bf16[128,2,3328]{2,1,0:T(2,128)(2,1)S(1)}, u32[]{:S(2)}, u32[]{:S(2)}) async-start(bf16[128,2,3328]{2,1,0:T(2,128)(2,1)} %get-tuple-element.24), calls=%async_computation | async-start | bytes 3407872 | tf_op jit(solution)/shard_map/all_to_all | solution.py:387
  22.1 10.6 %collective-permute-start = (bf16[128,256]{1,0:T(8,128)(2,1)S(1)}, bf16[128,256]{1,0:T(8,128)(2,1)S(1)}, u32[]{:S(2)}, u32[]{:S(2)}) collective-permute-start(bf16[128,256]{1,0:T(8,128)(2,1)S(1)} %copy-done.7), channel_id=1, source_target_pairs={{0,1},{1,2},{2,3},{3,0},{4,5},{5,6},{6,7},{7,4},{8,9},{9,10},{10,1... | collective-permute-start | bytes 196616 | tf_op jit(solution)/shard_map/ppermute | solution.py:353
  25.2 7.5 %collective-permute-start.1 = (bf16[128,256]{1,0:T(8,128)(2,1)S(1)}, bf16[128,256]{1,0:T(8,128)(2,1)S(1)}, u32[]{:S(2)}, u32[]{:S(2)}) collective-permute-start(bf16[128,256]{1,0:T(8,128)(2,1)S(1)} %copy-done.7), channel_id=1, source_target_pairs={{0,2},{1,3},{2,0},{3,1},{4,6},{5,7},{6,4},{7,5},{8,10},{9,11},{10,... | collective-permute-start | bytes 196616 | tf_op jit(solution)/shard_map/ppermute | solution.py:353
  29.6 5.3 %collective-permute-start.2 = (bf16[128,256]{1,0:T(8,128)(2,1)S(1)}, bf16[128,256]{1,0:T(8,128)(2,1)S(1)}, u32[]{:S(2)}, u32[]{:S(2)}) collective-permute-start(bf16[128,256]{1,0:T(8,128)(2,1)S(1)} %copy-done.7), channel_id=1, source_target_pairs={{0,3},{1,0},{2,1},{3,2},{4,7},{5,4},{6,5},{7,6},{8,11},{9,8},{10,9... | collective-permute-start | bytes 196616 | tf_op jit(solution)/shard_map/ppermute | solution.py:353
  35.4 68.2 %copy-start.2 = (bf16[4,128,256]{2,1,0:T(8,128)(2,1)}, bf16[4,128,256]{2,1,0:T(8,128)(2,1)S(1)}, u32[]{:S(2)}) copy-start(bf16[4,128,256]{2,1,0:T(8,128)(2,1)S(1)} %order.1.grads_ref) | copy-start | bytes 786436
  67.1 14.9 %all-to-all-start.1 = ((f32[4,256,128]{2,1,0:T(8,128)}), f32[4,256,128]{2,1,0:T(8,128)S(1)}, u32[]{:S(2)}, u32[]{:S(2)}) async-start(f32[4,256,128]{2,1,0:T(8,128)} %low_rank.1), calls=%async_computation.1 | async-start | bytes 1048576 | tf_op jit(solution)/shard_map/all_to_all | solution.py:408
  71.2 22.1 %collective-permute-start.3 = (bf16[256,1024]{1,0:T(8,128)(2,1)S(1)}, bf16[256,1024]{1,0:T(8,128)(2,1)}, u32[]{:S(2)}, u32[]{:S(2)}) collective-permute-start(bf16[256,1024]{1,0:T(8,128)(2,1)S(1)} %weight.1.refs_0_), channel_id=1, source_target_pairs={{0,64},{4,68},{8,72},{12,76},{16,80},{20,84},{24,88},{28,92},{32,9... | collective-permute-start | bytes 1572872 | tf_op jit(solution)/shard_map/ppermute | solution.py:312
  73.5 19.7 %collective-permute-start.4 = (bf16[256,1024]{1,0:T(8,128)(2,1)S(1)}, bf16[256,1024]{1,0:T(8,128)(2,1)}, u32[]{:S(2)}, u32[]{:S(2)}) collective-permute-start(bf16[256,1024]{1,0:T(8,128)(2,1)S(1)} %weight.1.refs_0_), channel_id=1, source_target_pairs={{0,448},{4,452},{8,456},{12,460},{16,464},{20,468},{24,472},{28,47... | collective-permute-start | bytes 1572872 | tf_op jit(solution)/shard_map/ppermute | solution.py:312
  77.7 15.6 %collective-permute-start.5 = (bf16[256,1024]{1,0:T(8,128)(2,1)S(1)}, bf16[256,1024]{1,0:T(8,128)(2,1)}, u32[]{:S(2)}, u32[]{:S(2)}) collective-permute-start(bf16[256,1024]{1,0:T(8,128)(2,1)S(1)} %weight.1.refs_0_), channel_id=1, source_target_pairs={{0,8},{4,12},{8,16},{12,20},{16,24},{20,28},{24,32},{28,36},{32,40... | collective-permute-start | bytes 1572872 | tf_op jit(solution)/shard_map/ppermute | solution.py:312
  82.6 1.0 copy-start.1
  83.7 41.7 %all-to-all-start.2 = ((bf16[128,2,2304]{2,1,0:T(2,128)(2,1)}), bf16[128,2,2304]{2,1,0:T(2,128)(2,1)}, u32[]{:S(2)}, u32[]{:S(2)}) async-start(bf16[128,2,2304]{2,1,0:T(2,128)(2,1)} %copy-done.1), calls=%async_computation.2 | async-start | bytes 2359296 | tf_op jit(solution)/shard_map/all_to_all | solution.py:425
  93.3 10.3 %copy-start = (bf16[128,2048]{1,0:T(8,128)(2,1)S(1)}, bf16[128,2048]{1,0:T(8,128)(2,1)}, u32[]{:S(2)}) copy-start(bf16[128,2048]{1,0:T(8,128)(2,1)} %tokens_ref.3) | copy-start | bytes 1572868
  96.2 11.1 %collective-permute-start.6 = (bf16[4,256,1024]{2,1,0:T(8,128)(2,1)}, bf16[4,256,1024]{2,1,0:T(8,128)(2,1)S(1)}, u32[]{:S(2)}, u32[]{:S(2)}) collective-permute-start(bf16[4,256,1024]{2,1,0:T(8,128)(2,1)} %stack.38.weight_ref), channel_id=1, source_target_pairs={{0,4},{4,0},{8,12},{12,8},{16,20},{20,16},{24,28},{28,24},{32,36},... | collective-permute-start | bytes 6291464 | tf_op jit(solution)/shard_map/ppermute | solution.py:316
  106.3 16.4 %copy-start.3 = (bf16[4,128,256]{2,1,0:T(8,128)(2,1)S(1)}, bf16[4,128,256]{2,1,0:T(8,128)(2,1)}, u32[]{:S(2)}) copy-start(bf16[4,128,256]{2,1,0:T(8,128)(2,1)} %copy-done.2) | copy-start | bytes 786436
  106.3 16.4 %copy-start.5 = (bf16[256,128]{1,0:T(8,128)(2,1)S(1)}, bf16[256,128]{1,0:T(8,128)(2,1)}, u32[]{:S(2)}) copy-start(bf16[256,128]{1,0:T(8,128)(2,1)} %get-tuple-element.35.picks_ref) | copy-start | bytes 196612
  109.8 9.8 %collective-permute-start.7 = (f32[128,256]{1,0:T(8,128)S(1)}, f32[128,256]{1,0:T(8,128)S(1)}, u32[]{:S(2)}, u32[]{:S(2)}) collective-permute-start(f32[128,256]{1,0:T(8,128)S(1)} %get-tuple-element.38), channel_id=1, source_target_pairs={{0,1},{1,2},{2,3},{3,0},{4,5},{5,6},{6,7},{7,4},{8,9},{9,10},{10,1... | collective-permute-start | bytes 393224 | tf_op jit(solution)/shard_map/ppermute | solution.py:353
  112.2 8.5 %collective-permute-start.8 = (f32[128,256]{1,0:T(8,128)S(1)}, f32[128,256]{1,0:T(8,128)S(1)}, u32[]{:S(2)}, u32[]{:S(2)}) collective-permute-start(f32[128,256]{1,0:T(8,128)S(1)} %get-tuple-element.39), channel_id=1, source_target_pairs={{0,2},{1,3},{2,0},{3,1},{4,6},{5,7},{6,4},{7,5},{8,10},{9,11},{10,... | collective-permute-start | bytes 393224 | tf_op jit(solution)/shard_map/ppermute | solution.py:353
  116.5 6.1 %collective-permute-start.9 = (f32[128,256]{1,0:T(8,128)S(1)}, f32[128,256]{1,0:T(8,128)S(1)}, u32[]{:S(2)}, u32[]{:S(2)}) collective-permute-start(f32[128,256]{1,0:T(8,128)S(1)} %get-tuple-element.40), channel_id=1, source_target_pairs={{0,3},{1,0},{2,1},{3,2},{4,7},{5,4},{6,5},{7,6},{8,11},{9,8},{10,9... | collective-permute-start | bytes 393224 | tf_op jit(solution)/shard_map/ppermute | solution.py:353

commit v6 on v5

--- a/solution.py
+++ b/solution.py
@@ -302,11 +302,12 @@
         out_ref[:, start + half * token_count : start + (half + 1) * token_count] = rows.astype(f32)
 
 
-def neighbour(value, dz, dy):
+def neighbour(value, *steps):
     pairs = []
     for z in range(N_Z):
         for y in range(N_Y):
             for core in range(N_C):
+                dz, dy = steps[core]
                 target = ((z + dz) % N_Z) * N_Y + (y + dy) % N_Y
                 pairs.append(((z * N_Y + y) * N_C + core, target * N_C + core))
     return lax.ppermute(value, "dp", pairs)
@@ -413,7 +414,12 @@
         0,
         2 * slots * columns,
     )(after_low)
-    near = (weight, neighbour(weight, 1, 0), neighbour(weight, -1, 0), neighbour(weight, 0, 1))
+    near = (
+        weight,
+        neighbour(weight, (1, 0), (1, 0)),
+        neighbour(weight, (-1, 0), (-1, 0)),
+        neighbour(weight, (0, 1), (0, -1)),
+    )
 
     back = call(
         back_kernel,

time: 129 us -> 129 us (level)
  waiting for transfers between devices: 38.3 us -> 41.3 us
  starting transfers between devices: 69.3 us -> 66.4 us
    ppermute x1, starting transfers between devices: 7.14 us -> 2.97 us  [other_core(): lax.ppermute(value, 'dp', [(i, i ^ 1) for i in range(N_Z * N_Y * N_C)])]
    all_to_all x1, waiting for transfers between devices: 1.64 us -> 4.6 us  [body(): lax.all_to_all(back, 'dp', split_axis=0, concat_axis=0, tiled=True)]
    all_to_all x1, starting transfers between devices: 8.4 us -> 9.8 us  [body(): lax.all_to_all(back, 'dp', split_axis=0, concat_axis=0, tiled=True)]
    ppermute x3, starting transfers between devices: 10.8 us -> 9.43 us  [neighbour(): return lax.ppermute(value, 'dp', pairs)]
where the time goes in v6:
time: 129 us; the launch traced here: 128 us
  starting transfers between devices  66.4 us (51%)
  waiting for transfers between devices  41.3 us (32%)
  Pallas kernels  18 us (14%)
    all_to_all x1, waiting for transfers between devices, body(): lax.all_to_all(outgoing, 'dp', split_axis=0, concat_axis=0, tiled=True)  30.4 us
    ppermute x6, starting transfers between devices, around(): lax.ppermute(value, 'mp', [(i, (i + shift) % parts) for i in range(parts)])  21.6 us
    all_to_all x1, starting transfers between devices, body(): lax.all_to_all(outgoing, 'dp', split_axis=0, concat_axis=0, tiled=True)  18.6 us
    all_to_all x1, starting transfers between devices, body(): lax.all_to_all(back, 'dp', split_axis=0, concat_axis=0, tiled=True)  9.8 us
    ppermute x3, starting transfers between devices, neighbour(): return lax.ppermute(value, 'dp', pairs)  9.43 us
    ppermute x6, waiting for transfers between devices, around(): lax.ppermute(value, 'mp', [(i, (i + shift) % parts) for i in range(parts)])  5.22 us
    all_to_all x1, waiting for transfers between devices, body(): lax.all_to_all(back, 'dp', split_axis=0, concat_axis=0, tiled=True)  4.6 us
    all_to_all x1, starting transfers between devices, body(): lax.all_to_all(low_parts, 'mp', split_axis=0, concat_axis=0, tiled=True)  4.02 us
  transfers between devices with their start and end apart: 13, of which 6 were waited for; matrix products, arithmetic and copies ran while one was open for 0% of the time, Pallas kernels for 9%

profile of v6, /device:TPU:1, one launch (start us, length us, event | category | flops | bytes accessed | tf_op | source)
XLA Modules:
  0.0 127.8 jit_solution(14156746675967030642)
XLA Ops:
  0.6 2.9 %spread.1 = (bf16[128,2,3328]{2,1,0:T(2,128)(2,1)}, bf16[256,128]{1,0:T(8,128)(2,1)}) custom-call(s32[1,128]{1,0:T(1,128)} %bitcast.25, s32[1,128]{1,0:T(1,128)} %bitcast.26, bf16[128,2048]{1,0:T(8,128)(2,1)} %tokens_ref.3, bf16[128,256]{1,0:T(8,128)(2,1)} %own_ref.1, bf16[8,2048]{1,0:T(8,128)(2,1)} %bitcast.24), custom_call_target="tpu_custom_call" | custom-call | flops 218103808 | bytes 2555904 | tf_op jit(solution)/shard_map/spread/pallas_call | solution.py:358
  3.5 0.0 copy-start.7
  3.5 0.0 copy-start.4
  3.5 0.0 copy-start.6
  3.5 18.6 %all-to-all-start = ((bf16[128,2,3328]{2,1,0:T(2,128)(2,1)}), bf16[128,2,3328]{2,1,0:T(2,128)(2,1)S(1)}, u32[]{:S(2)}, u32[]{:S(2)}) async-start(bf16[128,2,3328]{2,1,0:T(2,128)(2,1)} %get-tuple-element.24), calls=%async_computation | async-start | bytes 3407872 | tf_op jit(solution)/shard_map/all_to_all | solution.py:388
  22.1 3.1 %collective-permute-start = (bf16[128,256]{1,0:T(8,128)(2,1)S(1)}, bf16[128,256]{1,0:T(8,128)(2,1)S(1)}, u32[]{:S(2)}, u32[]{:S(2)}) collective-permute-start(bf16[128,256]{1,0:T(8,128)(2,1)S(1)} %copy-done.7), channel_id=1, source_target_pairs={{0,1},{1,2},{2,3},{3,0},{4,5},{5,6},{6,7},{7,4},{8,9},{9,10},{10,1... | collective-permute-start | bytes 196616 | tf_op jit(solution)/shard_map/ppermute | solution.py:354
  25.2 4.4 %collective-permute-start.1 = (bf16[128,256]{1,0:T(8,128)(2,1)S(1)}, bf16[128,256]{1,0:T(8,128)(2,1)S(1)}, u32[]{:S(2)}, u32[]{:S(2)}) collective-permute-start(bf16[128,256]{1,0:T(8,128)(2,1)S(1)} %copy-done.7), channel_id=1, source_target_pairs={{0,2},{1,3},{2,0},{3,1},{4,6},{5,7},{6,4},{7,5},{8,10},{9,11},{10,... | collective-permute-start | bytes 196616 | tf_op jit(solution)/shard_map/ppermute | solution.py:354
  29.6 3.1 %collective-permute-start.2 = (bf16[128,256]{1,0:T(8,128)(2,1)S(1)}, bf16[128,256]{1,0:T(8,128)(2,1)S(1)}, u32[]{:S(2)}, u32[]{:S(2)}) collective-permute-start(bf16[128,256]{1,0:T(8,128)(2,1)S(1)} %copy-done.7), channel_id=1, source_target_pairs={{0,3},{1,0},{2,1},{3,2},{4,7},{5,4},{6,5},{7,6},{8,11},{9,8},{10,9... | collective-permute-start | bytes 196616 | tf_op jit(solution)/shard_map/ppermute | solution.py:354
  32.7 0.0 collective-permute-done.a_ref
  32.7 0.0 collective-permute-done.1.b_ref
  32.7 2.2 %collective-permute-done.2.c_ref = bf16[128,256]{1,0:T(8,128)(2,1)S(1)} collective-permute-done((bf16[128,256]{1,0:T(8,128)(2,1)S(1)}, bf16[128,256]{1,0:T(8,128)(2,1)S(1)}, u32[]{:S(2)}, u32[]{:S(2)}) %collective-permute-start.2) | collective-permute-done | bytes 65568 | tf_op jit(solution)/shard_map/ppermute | solution.py:354
  34.9 0.5 order.1.grads_ref
  35.4 0.0 copy-start.2
  35.4 30.4 %all-to-all-done.arrived_ref = bf16[128,2,3328]{2,1,0:T(2,128)(2,1)S(1)} async-done(((bf16[128,2,3328]{2,1,0:T(2,128)(2,1)}), bf16[128,2,3328]{2,1,0:T(2,128)(2,1)S(1)}, u32[]{:S(2)}, u32[]{:S(2)}) %all-to-all-start) | async-done | bytes 1703968 | tf_op jit(solution)/shard_map/all_to_all | solution.py:388
  65.8 1.3 %low_rank.1 = f32[4,256,128]{2,1,0:T(8,128)} custom-call(bf16[128,2,3328]{2,1,0:T(2,128)(2,1)S(1)} %all-to-all-done.arrived_ref, bf16[64,2048]{1,0:T(8,128)(2,1)S(1)} %bitcast.20, bf16[64,256]{1,0:T(8,128)(2,1)S(1)} %bitcast.22), custom_call_target="tpu_custom_call" | custom-call | flops 75497472 | bytes 1703936 | tf_op jit(solution)/shard_map/low_rank/pallas_call | solution.py:401
  67.1 4.0 %all-to-all-start.1 = ((f32[4,256,128]{2,1,0:T(8,128)}), f32[4,256,128]{2,1,0:T(8,128)S(1)}, u32[]{:S(2)}, u32[]{:S(2)}) async-start(f32[4,256,128]{2,1,0:T(8,128)} %low_rank.1), calls=%async_computation.1 | async-start | bytes 1048576 | tf_op jit(solution)/shard_map/all_to_all | solution.py:409
  71.2 0.1 weight.1.refs_0_
  71.2 2.3 %collective-permute-start.3 = (bf16[256,1024]{1,0:T(8,128)(2,1)S(1)}, bf16[256,1024]{1,0:T(8,128)(2,1)}, u32[]{:S(2)}, u32[]{:S(2)}) collective-permute-start(bf16[256,1024]{1,0:T(8,128)(2,1)S(1)} %weight.1.refs_0_), channel_id=1, source_target_pairs={{0,64},{4,68},{8,72},{12,76},{16,80},{20,84},{24,88},{28,92},{32,9... | collective-permute-start | bytes 1572872 | tf_op jit(solution)/shard_map/ppermute | solution.py:313
  73.5 4.2 %collective-permute-start.4 = (bf16[256,1024]{1,0:T(8,128)(2,1)S(1)}, bf16[256,1024]{1,0:T(8,128)(2,1)}, u32[]{:S(2)}, u32[]{:S(2)}) collective-permute-start(bf16[256,1024]{1,0:T(8,128)(2,1)S(1)} %weight.1.refs_0_), channel_id=1, source_target_pairs={{0,448},{4,452},{8,456},{12,460},{16,464},{20,468},{24,472},{28,47... | collective-permute-start | bytes 1572872 | tf_op jit(solution)/shard_map/ppermute | solution.py:313
  77.7 2.9 %collective-permute-start.5 = (bf16[256,1024]{1,0:T(8,128)(2,1)S(1)}, bf16[256,1024]{1,0:T(8,128)(2,1)}, u32[]{:S(2)}, u32[]{:S(2)}) collective-permute-start(bf16[256,1024]{1,0:T(8,128)(2,1)S(1)} %weight.1.refs_0_), channel_id=1, source_target_pairs={{0,8},{4,60},{8,16},{12,4},{16,24},{20,12},{24,32},{28,20},{32,40}... | collective-permute-start | bytes 1572872 | tf_op jit(solution)/shard_map/ppermute | solution.py:313
  80.7 0.0 all-to-all-done.1.parts_ref
  80.7 0.5 back.1
  81.2 0.0 copy-start.1
  81.2 1.0 copy-done.1
  82.3 9.8 %all-to-all-start.2 = ((bf16[128,2,2304]{2,1,0:T(2,128)(2,1)}), bf16[128,2,2304]{2,1,0:T(2,128)(2,1)}, u32[]{:S(2)}, u32[]{:S(2)}) async-start(bf16[128,2,2304]{2,1,0:T(2,128)(2,1)} %copy-done.1), calls=%async_computation.2 | async-start | bytes 2359296 | tf_op jit(solution)/shard_map/all_to_all | solution.py:431
  92.1 1.2 factor_gradients.1
  93.3 0.0 collective-permute-done.3.refs_1_
  93.3 0.0 collective-permute-done.4.refs_2_
  93.3 0.0 collective-permute-done.5.refs_3_
  93.3 0.0 copy-start
  93.3 2.9 %stack.38.weight_ref = bf16[4,256,1024]{2,1,0:T(8,128)(2,1)} custom-call(bf16[256,1024]{1,0:T(8,128)(2,1)S(1)} %weight.1.refs_0_, bf16[256,1024]{1,0:T(8,128)(2,1)} %collective-permute-done.3.refs_1_, bf16[256,1024]{1,0:T(8,128)(2,1)} %collective-permute-done.4.refs_2_, bf16[256,1024]{1,0:T(8,128)(2,1)} %collective-permute-done.5.refs_3_), custom_call_target="tpu_custom_call" | custom-call | bytes 4194304 | tf_op jit(solution)/shard_map/stack/pallas_call | solution.py:445
  96.2 3.0 %collective-permute-start.6 = (bf16[4,256,1024]{2,1,0:T(8,128)(2,1)}, bf16[4,256,1024]{2,1,0:T(8,128)(2,1)S(1)}, u32[]{:S(2)}, u32[]{:S(2)}) collective-permute-start(bf16[4,256,1024]{2,1,0:T(8,128)(2,1)} %stack.38.weight_ref), channel_id=1, source_target_pairs={{0,4},{4,0},{8,12},{12,8},{16,20},{20,16},{24,28},{28,24},{32,36},... | collective-permute-start | bytes 6291464 | tf_op jit(solution)/shard_map/ppermute | solution.py:317
  99.3 0.1 stack.37.order_ref
  99.4 0.0 copy-done
  99.4 2.7 %base_own.1 = (f32[4,128,256]{2,1,0:T(8,128)S(1)}, f32[4,128,256]{2,1,0:T(8,128)S(1)}) custom-call(s32[9]{0:T(128)S(1)} %stack.37.order_ref, bf16[128,2048]{1,0:T(8,128)(2,1)S(1)} %copy-done, bf16[4,128,256]{2,1,0:T(8,128)(2,1)S(1)} %order.1.grads_ref, bf16[4,256,1024]{2,1,0:T(8,128)(2,1)} %stack.38.weight_ref), custom_call_target="tpu_custom_call" | custom-call | flops 536870912 | bytes 2097152 | tf_op jit(solution)/shard_map/base_own/pallas_call | solution.py:460
  102.1 0.0 copy-start.3
  102.1 0.0 copy-start.5
  102.1 1.0 collective-permute-done.6.weight_ref
  103.1 2.5 %base_forward.1 = (f32[128,256]{1,0:T(8,128)S(1)}, f32[128,256]{1,0:T(8,128)S(1)}, f32[128,256]{1,0:T(8,128)S(1)}, f32[128,256]{1,0:T(8,128)S(1)}) custom-call(s32[9]{0:T(128)S(1)} %stack.37.order_ref, bf16[128,2048]{1,0:T(8,128)(2,1)S(1)} %copy-done, f32[4,128,256]{2,1,0:T(8,128)S(1)} %get-tuple-element.36.totals_ref, ...), custom_call_target="tpu_custom_call" | custom-call | flops 268435456 | bytes 2097152 | tf_op jit(solution)/shard_map/base_forward/pallas_call | solution.py:469
  105.6 3.6 %collective-permute-start.7 = (f32[128,256]{1,0:T(8,128)S(1)}, f32[128,256]{1,0:T(8,128)S(1)}, u32[]{:S(2)}, u32[]{:S(2)}) collective-permute-start(f32[128,256]{1,0:T(8,128)S(1)} %get-tuple-element.38), channel_id=1, source_target_pairs={{0,1},{1,2},{2,3},{3,0},{4,5},{5,6},{6,7},{7,4},{8,9},{9,10},{10,1... | collective-permute-start | bytes 393224 | tf_op jit(solution)/shard_map/ppermute | solution.py:354
  109.3 4.3 %collective-permute-start.8 = (f32[128,256]{1,0:T(8,128)S(1)}, f32[128,256]{1,0:T(8,128)S(1)}, u32[]{:S(2)}, u32[]{:S(2)}) collective-permute-start(f32[128,256]{1,0:T(8,128)S(1)} %get-tuple-element.39), channel_id=1, source_target_pairs={{0,2},{1,3},{2,0},{3,1},{4,6},{5,7},{6,4},{7,5},{8,10},{9,11},{10,... | collective-permute-start | bytes 393224 | tf_op jit(solution)/shard_map/ppermute | solution.py:354
  113.6 3.1 %collective-permute-start.9 = (f32[128,256]{1,0:T(8,128)S(1)}, f32[128,256]{1,0:T(8,128)S(1)}, u32[]{:S(2)}, u32[]{:S(2)}) collective-permute-start(f32[128,256]{1,0:T(8,128)S(1)} %get-tuple-element.40), channel_id=1, source_target_pairs={{0,3},{1,0},{2,1},{3,2},{4,7},{5,4},{6,5},{7,6},{8,11},{9,8},{10,9... | collective-permute-start | bytes 393224 | tf_op jit(solution)/shard_map/ppermute | solution.py:354
  116.7 0.0 collective-permute-done.7.refs_1_
  116.7 1.1 collective-permute-done.8.refs_2_
  117.8 1.9 %collective-permute-done.9.refs_3_ = f32[128,256]{1,0:T(8,128)S(1)} collective-permute-done((f32[128,256]{1,0:T(8,128)S(1)}, f32[128,256]{1,0:T(8,128)S(1)}, u32[]{:S(2)}, u32[]{:S(2)}) %collective-permute-start.9) | collective-permute-done | bytes 131104 | tf_op jit(solution)/shard_map/ppermute | solution.py:354
  119.7 1.0 ready.1.ready_ref
  120.8 4.6 %all-to-all-done.2.returned_ref = bf16[128,2,2304]{2,1,0:T(2,128)(2,1)} async-done(((bf16[128,2,2304]{2,1,0:T(2,128)(2,1)}), bf16[128,2,2304]{2,1,0:T(2,128)(2,1)}, u32[]{:S(2)}, u32[]{:S(2)}) %all-to-all-start.2) | async-done | bytes 1179680 | tf_op jit(solution)/shard_map/all_to_all | solution.py:431
  125.3 2.4 %finish.1 = (bf16[128,256]{1,0:T(8,128)(2,1)}, bf16[128,2048]{1,0:T(8,128)(2,1)}) custom-call(bf16[128,2,2304]{2,1,0:T(2,128)(2,1)} %all-to-all-done.2.returned_ref, f32[128,2560]{1,0:T(8,128)S(1)} %ready.1.ready_ref), custom_call_target="tpu_custom_call" | custom-call | flops 150994944 | bytes 1179648 | tf_op jit(solution)/shard_map/finish/pallas_call | solution.py:491
  (6 shorter events, 0.0 us)
Async XLA Ops:
  3.5 18.6 %copy-start.7 = (bf16[128,256]{1,0:T(8,128)(2,1)S(1)}, bf16[128,256]{1,0:T(8,128)(2,1)}, u32[]{:S(2)}) copy-start(bf16[128,256]{1,0:T(8,128)(2,1)} %own_ref.1) | copy-start | bytes 196612
  3.5 62.3 %copy-start.4 = (bf16[1,2048,64]{1,2,0:T(8,128)(2,1)S(1)}, bf16[1,2048,64]{1,2,0:T(8,128)(2,1)}, u32[]{:S(2)}) copy-start(bf16[1,2048,64]{1,2,0:T(8,128)(2,1)} %param.10) | copy-start | bytes 786436
  3.5 62.3 %copy-start.6 = (bf16[1,64,256]{2,1,0:T(8,128)(2,1)S(1)}, bf16[1,64,256]{2,1,0:T(8,128)(2,1)}, u32[]{:S(2)}) copy-start(bf16[1,64,256]{2,1,0:T(8,128)(2,1)} %param.11) | copy-start | bytes 98308
  3.5 62.3 %all-to-all-start = ((bf16[128,2,3328]{2,1,0:T(2,128)(2,1)}), bf16[128,2,3328]{2,1,0:T(2,128)(2,1)S(1)}, u32[]{:S(2)}, u32[]{:S(2)}) async-start(bf16[128,2,3328]{2,1,0:T(2,128)(2,1)} %get-tuple-element.24), calls=%async_computation | async-start | bytes 3407872 | tf_op jit(solution)/shard_map/all_to_all | solution.py:388
  22.1 10.6 %collective-permute-start = (bf16[128,256]{1,0:T(8,128)(2,1)S(1)}, bf16[128,256]{1,0:T(8,128)(2,1)S(1)}, u32[]{:S(2)}, u32[]{:S(2)}) collective-permute-start(bf16[128,256]{1,0:T(8,128)(2,1)S(1)} %copy-done.7), channel_id=1, source_target_pairs={{0,1},{1,2},{2,3},{3,0},{4,5},{5,6},{6,7},{7,4},{8,9},{9,10},{10,1... | collective-permute-start | bytes 196616 | tf_op jit(solution)/shard_map/ppermute | solution.py:354
  25.2 7.5 %collective-permute-start.1 = (bf16[128,256]{1,0:T(8,128)(2,1)S(1)}, bf16[128,256]{1,0:T(8,128)(2,1)S(1)}, u32[]{:S(2)}, u32[]{:S(2)}) collective-permute-start(bf16[128,256]{1,0:T(8,128)(2,1)S(1)} %copy-done.7), channel_id=1, source_target_pairs={{0,2},{1,3},{2,0},{3,1},{4,6},{5,7},{6,4},{7,5},{8,10},{9,11},{10,... | collective-permute-start | bytes 196616 | tf_op jit(solution)/shard_map/ppermute | solution.py:354
  29.6 5.3 %collective-permute-start.2 = (bf16[128,256]{1,0:T(8,128)(2,1)S(1)}, bf16[128,256]{1,0:T(8,128)(2,1)S(1)}, u32[]{:S(2)}, u32[]{:S(2)}) collective-permute-start(bf16[128,256]{1,0:T(8,128)(2,1)S(1)} %copy-done.7), channel_id=1, source_target_pairs={{0,3},{1,0},{2,1},{3,2},{4,7},{5,4},{6,5},{7,6},{8,11},{9,8},{10,9... | collective-permute-start | bytes 196616 | tf_op jit(solution)/shard_map/ppermute | solution.py:354
  35.4 64.0 %copy-start.2 = (bf16[4,128,256]{2,1,0:T(8,128)(2,1)}, bf16[4,128,256]{2,1,0:T(8,128)(2,1)S(1)}, u32[]{:S(2)}) copy-start(bf16[4,128,256]{2,1,0:T(8,128)(2,1)S(1)} %order.1.grads_ref) | copy-start | bytes 786436
  67.1 13.5 %all-to-all-start.1 = ((f32[4,256,128]{2,1,0:T(8,128)}), f32[4,256,128]{2,1,0:T(8,128)S(1)}, u32[]{:S(2)}, u32[]{:S(2)}) async-start(f32[4,256,128]{2,1,0:T(8,128)} %low_rank.1), calls=%async_computation.1 | async-start | bytes 1048576 | tf_op jit(solution)/shard_map/all_to_all | solution.py:409
  71.2 22.1 %collective-permute-start.3 = (bf16[256,1024]{1,0:T(8,128)(2,1)S(1)}, bf16[256,1024]{1,0:T(8,128)(2,1)}, u32[]{:S(2)}, u32[]{:S(2)}) collective-permute-start(bf16[256,1024]{1,0:T(8,128)(2,1)S(1)} %weight.1.refs_0_), channel_id=1, source_target_pairs={{0,64},{4,68},{8,72},{12,76},{16,80},{20,84},{24,88},{28,92},{32,9... | collective-permute-start | bytes 1572872 | tf_op jit(solution)/shard_map/ppermute | solution.py:313
  73.5 19.7 %collective-permute-start.4 = (bf16[256,1024]{1,0:T(8,128)(2,1)S(1)}, bf16[256,1024]{1,0:T(8,128)(2,1)}, u32[]{:S(2)}, u32[]{:S(2)}) collective-permute-start(bf16[256,1024]{1,0:T(8,128)(2,1)S(1)} %weight.1.refs_0_), channel_id=1, source_target_pairs={{0,448},{4,452},{8,456},{12,460},{16,464},{20,468},{24,472},{28,47... | collective-permute-start | bytes 1572872 | tf_op jit(solution)/shard_map/ppermute | solution.py:313
  77.7 15.6 %collective-permute-start.5 = (bf16[256,1024]{1,0:T(8,128)(2,1)S(1)}, bf16[256,1024]{1,0:T(8,128)(2,1)}, u32[]{:S(2)}, u32[]{:S(2)}) collective-permute-start(bf16[256,1024]{1,0:T(8,128)(2,1)S(1)} %weight.1.refs_0_), channel_id=1, source_target_pairs={{0,8},{4,60},{8,16},{12,4},{16,24},{20,12},{24,32},{28,20},{32,40}... | collective-permute-start | bytes 1572872 | tf_op jit(solution)/shard_map/ppermute | solution.py:313
  81.2 1.0 copy-start.1
  82.3 43.1 %all-to-all-start.2 = ((bf16[128,2,2304]{2,1,0:T(2,128)(2,1)}), bf16[128,2,2304]{2,1,0:T(2,128)(2,1)}, u32[]{:S(2)}, u32[]{:S(2)}) async-start(bf16[128,2,2304]{2,1,0:T(2,128)(2,1)} %copy-done.1), calls=%async_computation.2 | async-start | bytes 2359296 | tf_op jit(solution)/shard_map/all_to_all | solution.py:431
  93.3 6.1 %copy-start = (bf16[128,2048]{1,0:T(8,128)(2,1)S(1)}, bf16[128,2048]{1,0:T(8,128)(2,1)}, u32[]{:S(2)}) copy-start(bf16[128,2048]{1,0:T(8,128)(2,1)} %tokens_ref.3) | copy-start | bytes 1572868
  96.2 6.9 %collective-permute-start.6 = (bf16[4,256,1024]{2,1,0:T(8,128)(2,1)}, bf16[4,256,1024]{2,1,0:T(8,128)(2,1)S(1)}, u32[]{:S(2)}, u32[]{:S(2)}) collective-permute-start(bf16[4,256,1024]{2,1,0:T(8,128)(2,1)} %stack.38.weight_ref), channel_id=1, source_target_pairs={{0,4},{4,0},{8,12},{12,8},{16,20},{20,16},{24,28},{28,24},{32,36},... | collective-permute-start | bytes 6291464 | tf_op jit(solution)/shard_map/ppermute | solution.py:317
  102.1 17.6 %copy-start.3 = (bf16[4,128,256]{2,1,0:T(8,128)(2,1)S(1)}, bf16[4,128,256]{2,1,0:T(8,128)(2,1)}, u32[]{:S(2)}) copy-start(bf16[4,128,256]{2,1,0:T(8,128)(2,1)} %copy-done.2) | copy-start | bytes 786436
  102.1 17.6 %copy-start.5 = (bf16[256,128]{1,0:T(8,128)(2,1)S(1)}, bf16[256,128]{1,0:T(8,128)(2,1)}, u32[]{:S(2)}) copy-start(bf16[256,128]{1,0:T(8,128)(2,1)} %get-tuple-element.35.picks_ref) | copy-start | bytes 196612
  105.6 11.1 %collective-permute-start.7 = (f32[128,256]{1,0:T(8,128)S(1)}, f32[128,256]{1,0:T(8,128)S(1)}, u32[]{:S(2)}, u32[]{:S(2)}) collective-permute-start(f32[128,256]{1,0:T(8,128)S(1)} %get-tuple-element.38), channel_id=1, source_target_pairs={{0,1},{1,2},{2,3},{3,0},{4,5},{5,6},{6,7},{7,4},{8,9},{9,10},{10,1... | collective-permute-start | bytes 393224 | tf_op jit(solution)/shard_map/ppermute | solution.py:354
  109.3 8.5 %collective-permute-start.8 = (f32[128,256]{1,0:T(8,128)S(1)}, f32[128,256]{1,0:T(8,128)S(1)}, u32[]{:S(2)}, u32[]{:S(2)}) collective-permute-start(f32[128,256]{1,0:T(8,128)S(1)} %get-tuple-element.39), channel_id=1, source_target_pairs={{0,2},{1,3},{2,0},{3,1},{4,6},{5,7},{6,4},{7,5},{8,10},{9,11},{10,... | collective-permute-start | bytes 393224 | tf_op jit(solution)/shard_map/ppermute | solution.py:354
  113.6 6.1 %collective-permute-start.9 = (f32[128,256]{1,0:T(8,128)S(1)}, f32[128,256]{1,0:T(8,128)S(1)}, u32[]{:S(2)}, u32[]{:S(2)}) collective-permute-start(f32[128,256]{1,0:T(8,128)S(1)} %get-tuple-element.40), channel_id=1, source_target_pairs={{0,3},{1,0},{2,1},{3,2},{4,7},{5,4},{6,5},{7,6},{8,11},{9,8},{10,9... | collective-permute-start | bytes 393224 | tf_op jit(solution)/shard_map/ppermute | solution.py:354

commit v7 on v6

--- a/solution.py
+++ b/solution.py
@@ -416,9 +416,9 @@
     )(after_low)
     near = (
         weight,
+        neighbour(weight, (0, 1), (0, -1)),
+        neighbour(weight, (-1, 0), (-1, 0)),
         neighbour(weight, (1, 0), (1, 0)),
-        neighbour(weight, (-1, 0), (-1, 0)),
-        neighbour(weight, (0, 1), (0, -1)),
     )
 
     back = call(
@@ -451,7 +451,7 @@
     )(*near)
     swapped = other_core(gathered)
     mine = chip_class(z, y)
-    offsets = [0, CLASSES - 1, 1, 2]
+    offsets = [0, 2, 1, CLASSES - 1]
     order = [(((mine + offset) % CLASSES) * N_C + core) for offset in offsets]
     order += [(((mine + offset) % CLASSES) * N_C + 1 - core) for offset in offsets]
     order = jnp.stack(order + [across]).astype(jnp.int32)

time: 129 us -> 128 us (level)
  no operation moved by 1% of the time
where the time goes in v7:
time: 128 us; the launch traced here: 127 us
  starting transfers between devices  66.3 us (52%)
  waiting for transfers between devices  40.4 us (32%)
  Pallas kernels  18 us (14%)
    all_to_all x1, waiting for transfers between devices, body(): lax.all_to_all(outgoing, 'dp', split_axis=0, concat_axis=0, tiled=True)  30.4 us
    ppermute x6, starting transfers between devices, around(): lax.ppermute(value, 'mp', [(i, (i + shift) % parts) for i in range(parts)])  21.3 us
    all_to_all x1, starting transfers between devices, body(): lax.all_to_all(outgoing, 'dp', split_axis=0, concat_axis=0, tiled=True)  18.6 us
    all_to_all x1, starting transfers between devices, body(): lax.all_to_all(back, 'dp', split_axis=0, concat_axis=0, tiled=True)  10.2 us
    ppermute x3, starting transfers between devices, neighbour(): return lax.ppermute(value, 'dp', pairs)  8.22 us
    ppermute x6, waiting for transfers between devices, around(): lax.ppermute(value, 'mp', [(i, (i + shift) % parts) for i in range(parts)])  5.22 us
    all_to_all x1, starting transfers between devices, body(): lax.all_to_all(low_parts, 'mp', split_axis=0, concat_axis=0, tiled=True)  4.02 us
    ppermute x1, starting transfers between devices, other_core(): lax.ppermute(value, 'dp', [(i, i ^ 1) for i in range(N_Z * N_Y * N_C)])  3.99 us
  transfers between devices with their start and end apart: 13, of which 6 were waited for; matrix products, arithmetic and copies ran while one was open for 0% of the time, Pallas kernels for 9%

profile of v7, /device:TPU:1, one launch (start us, length us, event | category | flops | bytes accessed | tf_op | source)
XLA Modules:
  0.0 126.8 jit_solution(13655415188920117839)
XLA Ops:
  0.6 2.9 %spread.1 = (bf16[128,2,3328]{2,1,0:T(2,128)(2,1)}, bf16[256,128]{1,0:T(8,128)(2,1)}) custom-call(s32[1,128]{1,0:T(1,128)} %bitcast.25, s32[1,128]{1,0:T(1,128)} %bitcast.26, bf16[128,2048]{1,0:T(8,128)(2,1)} %tokens_ref.3, bf16[128,256]{1,0:T(8,128)(2,1)} %own_ref.1, bf16[8,2048]{1,0:T(8,128)(2,1)} %bitcast.24), custom_call_target="tpu_custom_call" | custom-call | flops 218103808 | bytes 2555904 | tf_op jit(solution)/shard_map/spread/pallas_call | solution.py:358
  3.5 0.0 copy-start.7
  3.5 0.0 copy-start.4
  3.5 0.0 copy-start.6
  3.5 18.6 %all-to-all-start = ((bf16[128,2,3328]{2,1,0:T(2,128)(2,1)}), bf16[128,2,3328]{2,1,0:T(2,128)(2,1)S(1)}, u32[]{:S(2)}, u32[]{:S(2)}) async-start(bf16[128,2,3328]{2,1,0:T(2,128)(2,1)} %get-tuple-element.24), calls=%async_computation | async-start | bytes 3407872 | tf_op jit(solution)/shard_map/all_to_all | solution.py:388
  22.1 3.1 %collective-permute-start = (bf16[128,256]{1,0:T(8,128)(2,1)S(1)}, bf16[128,256]{1,0:T(8,128)(2,1)S(1)}, u32[]{:S(2)}, u32[]{:S(2)}) collective-permute-start(bf16[128,256]{1,0:T(8,128)(2,1)S(1)} %copy-done.7), channel_id=1, source_target_pairs={{0,1},{1,2},{2,3},{3,0},{4,5},{5,6},{6,7},{7,4},{8,9},{9,10},{10,1... | collective-permute-start | bytes 196616 | tf_op jit(solution)/shard_map/ppermute | solution.py:354
  25.2 4.4 %collective-permute-start.1 = (bf16[128,256]{1,0:T(8,128)(2,1)S(1)}, bf16[128,256]{1,0:T(8,128)(2,1)S(1)}, u32[]{:S(2)}, u32[]{:S(2)}) collective-permute-start(bf16[128,256]{1,0:T(8,128)(2,1)S(1)} %copy-done.7), channel_id=1, source_target_pairs={{0,2},{1,3},{2,0},{3,1},{4,6},{5,7},{6,4},{7,5},{8,10},{9,11},{10,... | collective-permute-start | bytes 196616 | tf_op jit(solution)/shard_map/ppermute | solution.py:354
  29.6 3.1 %collective-permute-start.2 = (bf16[128,256]{1,0:T(8,128)(2,1)S(1)}, bf16[128,256]{1,0:T(8,128)(2,1)S(1)}, u32[]{:S(2)}, u32[]{:S(2)}) collective-permute-start(bf16[128,256]{1,0:T(8,128)(2,1)S(1)} %copy-done.7), channel_id=1, source_target_pairs={{0,3},{1,0},{2,1},{3,2},{4,7},{5,4},{6,5},{7,6},{8,11},{9,8},{10,9... | collective-permute-start | bytes 196616 | tf_op jit(solution)/shard_map/ppermute | solution.py:354
  32.7 0.0 collective-permute-done.a_ref
  32.7 0.0 collective-permute-done.1.b_ref
  32.7 2.2 %collective-permute-done.2.c_ref = bf16[128,256]{1,0:T(8,128)(2,1)S(1)} collective-permute-done((bf16[128,256]{1,0:T(8,128)(2,1)S(1)}, bf16[128,256]{1,0:T(8,128)(2,1)S(1)}, u32[]{:S(2)}, u32[]{:S(2)}) %collective-permute-start.2) | collective-permute-done | bytes 65568 | tf_op jit(solution)/shard_map/ppermute | solution.py:354
  34.9 0.5 order.1.grads_ref
  35.4 0.0 copy-start.2
  35.4 30.4 %all-to-all-done.arrived_ref = bf16[128,2,3328]{2,1,0:T(2,128)(2,1)S(1)} async-done(((bf16[128,2,3328]{2,1,0:T(2,128)(2,1)}), bf16[128,2,3328]{2,1,0:T(2,128)(2,1)S(1)}, u32[]{:S(2)}, u32[]{:S(2)}) %all-to-all-start) | async-done | bytes 1703968 | tf_op jit(solution)/shard_map/all_to_all | solution.py:388
  65.8 0.0 copy-done.4
  65.8 1.3 %low_rank.1 = f32[4,256,128]{2,1,0:T(8,128)} custom-call(bf16[128,2,3328]{2,1,0:T(2,128)(2,1)S(1)} %all-to-all-done.arrived_ref, bf16[64,2048]{1,0:T(8,128)(2,1)S(1)} %bitcast.20, bf16[64,256]{1,0:T(8,128)(2,1)S(1)} %bitcast.22), custom_call_target="tpu_custom_call" | custom-call | flops 75497472 | bytes 1703936 | tf_op jit(solution)/shard_map/low_rank/pallas_call | solution.py:401
  67.1 4.0 %all-to-all-start.1 = ((f32[4,256,128]{2,1,0:T(8,128)}), f32[4,256,128]{2,1,0:T(8,128)S(1)}, u32[]{:S(2)}, u32[]{:S(2)}) async-start(f32[4,256,128]{2,1,0:T(8,128)} %low_rank.1), calls=%async_computation.1 | async-start | bytes 1048576 | tf_op jit(solution)/shard_map/all_to_all | solution.py:409
  71.2 0.1 weight.1.refs_0_
  71.2 2.9 %collective-permute-start.3 = (bf16[256,1024]{1,0:T(8,128)(2,1)S(1)}, bf16[256,1024]{1,0:T(8,128)(2,1)}, u32[]{:S(2)}, u32[]{:S(2)}) collective-permute-start(bf16[256,1024]{1,0:T(8,128)(2,1)S(1)} %weight.1.refs_0_), channel_id=1, source_target_pairs={{0,8},{4,60},{8,16},{12,4},{16,24},{20,12},{24,32},{28,20},{32,40}... | collective-permute-start | bytes 1572872 | tf_op jit(solution)/shard_map/ppermute | solution.py:313
  74.2 2.8 %collective-permute-start.4 = (bf16[256,1024]{1,0:T(8,128)(2,1)S(1)}, bf16[256,1024]{1,0:T(8,128)(2,1)}, u32[]{:S(2)}, u32[]{:S(2)}) collective-permute-start(bf16[256,1024]{1,0:T(8,128)(2,1)S(1)} %weight.1.refs_0_), channel_id=1, source_target_pairs={{0,448},{4,452},{8,456},{12,460},{16,464},{20,468},{24,472},{28,47... | collective-permute-start | bytes 1572872 | tf_op jit(solution)/shard_map/ppermute | solution.py:313
  77.0 2.4 %collective-permute-start.5 = (bf16[256,1024]{1,0:T(8,128)(2,1)S(1)}, bf16[256,1024]{1,0:T(8,128)(2,1)}, u32[]{:S(2)}, u32[]{:S(2)}) collective-permute-start(bf16[256,1024]{1,0:T(8,128)(2,1)S(1)} %weight.1.refs_0_), channel_id=1, source_target_pairs={{0,64},{4,68},{8,72},{12,76},{16,80},{20,84},{24,88},{28,92},{32,9... | collective-permute-start | bytes 1572872 | tf_op jit(solution)/shard_map/ppermute | solution.py:313
  79.5 0.0 all-to-all-done.1.parts_ref
  79.5 0.5 back.1
  80.0 1.0 copy-done.1
  81.0 10.2 %all-to-all-start.2 = ((bf16[128,2,2304]{2,1,0:T(2,128)(2,1)}), bf16[128,2,2304]{2,1,0:T(2,128)(2,1)}, u32[]{:S(2)}, u32[]{:S(2)}) async-start(bf16[128,2,2304]{2,1,0:T(2,128)(2,1)} %copy-done.1), calls=%async_computation.2 | async-start | bytes 2359296 | tf_op jit(solution)/shard_map/all_to_all | solution.py:431
  91.2 1.2 factor_gradients.1
  92.4 0.0 collective-permute-done.3.refs_1_
  92.4 0.0 collective-permute-done.4.refs_2_
  92.4 0.0 collective-permute-done.5.refs_3_
  92.5 0.0 copy-start
  92.5 2.9 %stack.38.weight_ref = bf16[4,256,1024]{2,1,0:T(8,128)(2,1)} custom-call(bf16[256,1024]{1,0:T(8,128)(2,1)S(1)} %weight.1.refs_0_, bf16[256,1024]{1,0:T(8,128)(2,1)} %collective-permute-done.3.refs_1_, bf16[256,1024]{1,0:T(8,128)(2,1)} %collective-permute-done.4.refs_2_, bf16[256,1024]{1,0:T(8,128)(2,1)} %collective-permute-done.5.refs_3_), custom_call_target="tpu_custom_call" | custom-call | bytes 4194304 | tf_op jit(solution)/shard_map/stack/pallas_call | solution.py:445
  95.4 4.0 %collective-permute-start.6 = (bf16[4,256,1024]{2,1,0:T(8,128)(2,1)}, bf16[4,256,1024]{2,1,0:T(8,128)(2,1)S(1)}, u32[]{:S(2)}, u32[]{:S(2)}) collective-permute-start(bf16[4,256,1024]{2,1,0:T(8,128)(2,1)} %stack.38.weight_ref), channel_id=1, source_target_pairs={{0,4},{4,0},{8,12},{12,8},{16,20},{20,16},{24,28},{28,24},{32,36},... | collective-permute-start | bytes 6291464 | tf_op jit(solution)/shard_map/ppermute | solution.py:317
  99.5 0.1 stack.37.order_ref
  99.6 0.0 copy-done
  99.6 2.7 %base_own.1 = (f32[4,128,256]{2,1,0:T(8,128)S(1)}, f32[4,128,256]{2,1,0:T(8,128)S(1)}) custom-call(s32[9]{0:T(128)S(1)} %stack.37.order_ref, bf16[128,2048]{1,0:T(8,128)(2,1)S(1)} %copy-done, bf16[4,128,256]{2,1,0:T(8,128)(2,1)S(1)} %order.1.grads_ref, bf16[4,256,1024]{2,1,0:T(8,128)(2,1)} %stack.38.weight_ref), custom_call_target="tpu_custom_call" | custom-call | flops 536870912 | bytes 2097152 | tf_op jit(solution)/shard_map/base_own/pallas_call | solution.py:460
  102.3 0.0 copy-start.3
  102.3 0.0 copy-start.5
  102.3 1.0 collective-permute-done.6.weight_ref
  103.3 2.5 %base_forward.1 = (f32[128,256]{1,0:T(8,128)S(1)}, f32[128,256]{1,0:T(8,128)S(1)}, f32[128,256]{1,0:T(8,128)S(1)}, f32[128,256]{1,0:T(8,128)S(1)}) custom-call(s32[9]{0:T(128)S(1)} %stack.37.order_ref, bf16[128,2048]{1,0:T(8,128)(2,1)S(1)} %copy-done, f32[4,128,256]{2,1,0:T(8,128)S(1)} %get-tuple-element.36.totals_ref, ...), custom_call_target="tpu_custom_call" | custom-call | flops 268435456 | bytes 2097152 | tf_op jit(solution)/shard_map/base_forward/pallas_call | solution.py:469
  105.8 3.4 %collective-permute-start.7 = (f32[128,256]{1,0:T(8,128)S(1)}, f32[128,256]{1,0:T(8,128)S(1)}, u32[]{:S(2)}, u32[]{:S(2)}) collective-permute-start(f32[128,256]{1,0:T(8,128)S(1)} %get-tuple-element.38), channel_id=1, source_target_pairs={{0,1},{1,2},{2,3},{3,0},{4,5},{5,6},{6,7},{7,4},{8,9},{9,10},{10,1... | collective-permute-start | bytes 393224 | tf_op jit(solution)/shard_map/ppermute | solution.py:354
  109.2 4.3 %collective-permute-start.8 = (f32[128,256]{1,0:T(8,128)S(1)}, f32[128,256]{1,0:T(8,128)S(1)}, u32[]{:S(2)}, u32[]{:S(2)}) collective-permute-start(f32[128,256]{1,0:T(8,128)S(1)} %get-tuple-element.39), channel_id=1, source_target_pairs={{0,2},{1,3},{2,0},{3,1},{4,6},{5,7},{6,4},{7,5},{8,10},{9,11},{10,... | collective-permute-start | bytes 393224 | tf_op jit(solution)/shard_map/ppermute | solution.py:354
  113.5 3.1 %collective-permute-start.9 = (f32[128,256]{1,0:T(8,128)S(1)}, f32[128,256]{1,0:T(8,128)S(1)}, u32[]{:S(2)}, u32[]{:S(2)}) collective-permute-start(f32[128,256]{1,0:T(8,128)S(1)} %get-tuple-element.40), channel_id=1, source_target_pairs={{0,3},{1,0},{2,1},{3,2},{4,7},{5,4},{6,5},{7,6},{8,11},{9,8},{10,9... | collective-permute-start | bytes 393224 | tf_op jit(solution)/shard_map/ppermute | solution.py:354
  116.6 0.0 collective-permute-done.7.refs_1_
  116.6 1.1 collective-permute-done.8.refs_2_
  117.7 1.9 %collective-permute-done.9.refs_3_ = f32[128,256]{1,0:T(8,128)S(1)} collective-permute-done((f32[128,256]{1,0:T(8,128)S(1)}, f32[128,256]{1,0:T(8,128)S(1)}, u32[]{:S(2)}, u32[]{:S(2)}) %collective-permute-start.9) | collective-permute-done | bytes 131104 | tf_op jit(solution)/shard_map/ppermute | solution.py:354
  119.6 1.0 ready.1.ready_ref
  120.7 3.7 %all-to-all-done.2.returned_ref = bf16[128,2,2304]{2,1,0:T(2,128)(2,1)} async-done(((bf16[128,2,2304]{2,1,0:T(2,128)(2,1)}), bf16[128,2,2304]{2,1,0:T(2,128)(2,1)}, u32[]{:S(2)}, u32[]{:S(2)}) %all-to-all-start.2) | async-done | bytes 1179680 | tf_op jit(solution)/shard_map/all_to_all | solution.py:431
  124.4 2.4 %finish.1 = (bf16[128,256]{1,0:T(8,128)(2,1)}, bf16[128,2048]{1,0:T(8,128)(2,1)}) custom-call(bf16[128,2,2304]{2,1,0:T(2,128)(2,1)} %all-to-all-done.2.returned_ref, f32[128,2560]{1,0:T(8,128)S(1)} %ready.1.ready_ref), custom_call_target="tpu_custom_call" | custom-call | flops 150994944 | bytes 1179648 | tf_op jit(solution)/shard_map/finish/pallas_call | solution.py:491
  (6 shorter events, 0.0 us)
Async XLA Ops:
  3.5 18.6 %copy-start.7 = (bf16[128,256]{1,0:T(8,128)(2,1)S(1)}, bf16[128,256]{1,0:T(8,128)(2,1)}, u32[]{:S(2)}) copy-start(bf16[128,256]{1,0:T(8,128)(2,1)} %own_ref.1) | copy-start | bytes 196612
  3.5 62.3 %copy-start.4 = (bf16[1,2048,64]{1,2,0:T(8,128)(2,1)S(1)}, bf16[1,2048,64]{1,2,0:T(8,128)(2,1)}, u32[]{:S(2)}) copy-start(bf16[1,2048,64]{1,2,0:T(8,128)(2,1)} %param.10) | copy-start | bytes 786436
  3.5 62.3 %copy-start.6 = (bf16[1,64,256]{2,1,0:T(8,128)(2,1)S(1)}, bf16[1,64,256]{2,1,0:T(8,128)(2,1)}, u32[]{:S(2)}) copy-start(bf16[1,64,256]{2,1,0:T(8,128)(2,1)} %param.11) | copy-start | bytes 98308
  3.5 62.3 %all-to-all-start = ((bf16[128,2,3328]{2,1,0:T(2,128)(2,1)}), bf16[128,2,3328]{2,1,0:T(2,128)(2,1)S(1)}, u32[]{:S(2)}, u32[]{:S(2)}) async-start(bf16[128,2,3328]{2,1,0:T(2,128)(2,1)} %get-tuple-element.24), calls=%async_computation | async-start | bytes 3407872 | tf_op jit(solution)/shard_map/all_to_all | solution.py:388
  22.1 10.6 %collective-permute-start = (bf16[128,256]{1,0:T(8,128)(2,1)S(1)}, bf16[128,256]{1,0:T(8,128)(2,1)S(1)}, u32[]{:S(2)}, u32[]{:S(2)}) collective-permute-start(bf16[128,256]{1,0:T(8,128)(2,1)S(1)} %copy-done.7), channel_id=1, source_target_pairs={{0,1},{1,2},{2,3},{3,0},{4,5},{5,6},{6,7},{7,4},{8,9},{9,10},{10,1... | collective-permute-start | bytes 196616 | tf_op jit(solution)/shard_map/ppermute | solution.py:354
  25.2 7.5 %collective-permute-start.1 = (bf16[128,256]{1,0:T(8,128)(2,1)S(1)}, bf16[128,256]{1,0:T(8,128)(2,1)S(1)}, u32[]{:S(2)}, u32[]{:S(2)}) collective-permute-start(bf16[128,256]{1,0:T(8,128)(2,1)S(1)} %copy-done.7), channel_id=1, source_target_pairs={{0,2},{1,3},{2,0},{3,1},{4,6},{5,7},{6,4},{7,5},{8,10},{9,11},{10,... | collective-permute-start | bytes 196616 | tf_op jit(solution)/shard_map/ppermute | solution.py:354
  29.6 5.3 %collective-permute-start.2 = (bf16[128,256]{1,0:T(8,128)(2,1)S(1)}, bf16[128,256]{1,0:T(8,128)(2,1)S(1)}, u32[]{:S(2)}, u32[]{:S(2)}) collective-permute-start(bf16[128,256]{1,0:T(8,128)(2,1)S(1)} %copy-done.7), channel_id=1, source_target_pairs={{0,3},{1,0},{2,1},{3,2},{4,7},{5,4},{6,5},{7,6},{8,11},{9,8},{10,9... | collective-permute-start | bytes 196616 | tf_op jit(solution)/shard_map/ppermute | solution.py:354
  35.4 64.2 %copy-start.2 = (bf16[4,128,256]{2,1,0:T(8,128)(2,1)}, bf16[4,128,256]{2,1,0:T(8,128)(2,1)S(1)}, u32[]{:S(2)}) copy-start(bf16[4,128,256]{2,1,0:T(8,128)(2,1)S(1)} %order.1.grads_ref) | copy-start | bytes 786436
  67.1 12.3 %all-to-all-start.1 = ((f32[4,256,128]{2,1,0:T(8,128)}), f32[4,256,128]{2,1,0:T(8,128)S(1)}, u32[]{:S(2)}, u32[]{:S(2)}) async-start(f32[4,256,128]{2,1,0:T(8,128)} %low_rank.1), calls=%async_computation.1 | async-start | bytes 1048576 | tf_op jit(solution)/shard_map/all_to_all | solution.py:409
  71.2 21.2 %collective-permute-start.3 = (bf16[256,1024]{1,0:T(8,128)(2,1)S(1)}, bf16[256,1024]{1,0:T(8,128)(2,1)}, u32[]{:S(2)}, u32[]{:S(2)}) collective-permute-start(bf16[256,1024]{1,0:T(8,128)(2,1)S(1)} %weight.1.refs_0_), channel_id=1, source_target_pairs={{0,8},{4,60},{8,16},{12,4},{16,24},{20,12},{24,32},{28,20},{32,40}... | collective-permute-start | bytes 1572872 | tf_op jit(solution)/shard_map/ppermute | solution.py:313
  74.2 18.3 %collective-permute-start.4 = (bf16[256,1024]{1,0:T(8,128)(2,1)S(1)}, bf16[256,1024]{1,0:T(8,128)(2,1)}, u32[]{:S(2)}, u32[]{:S(2)}) collective-permute-start(bf16[256,1024]{1,0:T(8,128)(2,1)S(1)} %weight.1.refs_0_), channel_id=1, source_target_pairs={{0,448},{4,452},{8,456},{12,460},{16,464},{20,468},{24,472},{28,47... | collective-permute-start | bytes 1572872 | tf_op jit(solution)/shard_map/ppermute | solution.py:313
  77.0 15.4 %collective-permute-start.5 = (bf16[256,1024]{1,0:T(8,128)(2,1)S(1)}, bf16[256,1024]{1,0:T(8,128)(2,1)}, u32[]{:S(2)}, u32[]{:S(2)}) collective-permute-start(bf16[256,1024]{1,0:T(8,128)(2,1)S(1)} %weight.1.refs_0_), channel_id=1, source_target_pairs={{0,64},{4,68},{8,72},{12,76},{16,80},{20,84},{24,88},{28,92},{32,9... | collective-permute-start | bytes 1572872 | tf_op jit(solution)/shard_map/ppermute | solution.py:313
  80.0 1.0 copy-start.1
  81.0 43.4 %all-to-all-start.2 = ((bf16[128,2,2304]{2,1,0:T(2,128)(2,1)}), bf16[128,2,2304]{2,1,0:T(2,128)(2,1)}, u32[]{:S(2)}, u32[]{:S(2)}) async-start(bf16[128,2,2304]{2,1,0:T(2,128)(2,1)} %copy-done.1), calls=%async_computation.2 | async-start | bytes 2359296 | tf_op jit(solution)/shard_map/all_to_all | solution.py:431
  92.5 7.1 %copy-start = (bf16[128,2048]{1,0:T(8,128)(2,1)S(1)}, bf16[128,2048]{1,0:T(8,128)(2,1)}, u32[]{:S(2)}) copy-start(bf16[128,2048]{1,0:T(8,128)(2,1)} %tokens_ref.3) | copy-start | bytes 1572868
  95.4 8.0 %collective-permute-start.6 = (bf16[4,256,1024]{2,1,0:T(8,128)(2,1)}, bf16[4,256,1024]{2,1,0:T(8,128)(2,1)S(1)}, u32[]{:S(2)}, u32[]{:S(2)}) collective-permute-start(bf16[4,256,1024]{2,1,0:T(8,128)(2,1)} %stack.38.weight_ref), channel_id=1, source_target_pairs={{0,4},{4,0},{8,12},{12,8},{16,20},{20,16},{24,28},{28,24},{32,36},... | collective-permute-start | bytes 6291464 | tf_op jit(solution)/shard_map/ppermute | solution.py:317
  102.3 17.3 %copy-start.3 = (bf16[4,128,256]{2,1,0:T(8,128)(2,1)S(1)}, bf16[4,128,256]{2,1,0:T(8,128)(2,1)}, u32[]{:S(2)}) copy-start(bf16[4,128,256]{2,1,0:T(8,128)(2,1)} %copy-done.2) | copy-start | bytes 786436
  102.3 17.3 %copy-start.5 = (bf16[256,128]{1,0:T(8,128)(2,1)S(1)}, bf16[256,128]{1,0:T(8,128)(2,1)}, u32[]{:S(2)}) copy-start(bf16[256,128]{1,0:T(8,128)(2,1)} %get-tuple-element.35.picks_ref) | copy-start | bytes 196612
  105.8 10.8 %collective-permute-start.7 = (f32[128,256]{1,0:T(8,128)S(1)}, f32[128,256]{1,0:T(8,128)S(1)}, u32[]{:S(2)}, u32[]{:S(2)}) collective-permute-start(f32[128,256]{1,0:T(8,128)S(1)} %get-tuple-element.38), channel_id=1, source_target_pairs={{0,1},{1,2},{2,3},{3,0},{4,5},{5,6},{6,7},{7,4},{8,9},{9,10},{10,1... | collective-permute-start | bytes 393224 | tf_op jit(solution)/shard_map/ppermute | solution.py:354
  109.2 8.5 %collective-permute-start.8 = (f32[128,256]{1,0:T(8,128)S(1)}, f32[128,256]{1,0:T(8,128)S(1)}, u32[]{:S(2)}, u32[]{:S(2)}) collective-permute-start(f32[128,256]{1,0:T(8,128)S(1)} %get-tuple-element.39), channel_id=1, source_target_pairs={{0,2},{1,3},{2,0},{3,1},{4,6},{5,7},{6,4},{7,5},{8,10},{9,11},{10,... | collective-permute-start | bytes 393224 | tf_op jit(solution)/shard_map/ppermute | solution.py:354
  113.5 6.1 %collective-permute-start.9 = (f32[128,256]{1,0:T(8,128)S(1)}, f32[128,256]{1,0:T(8,128)S(1)}, u32[]{:S(2)}, u32[]{:S(2)}) collective-permute-start(f32[128,256]{1,0:T(8,128)S(1)} %get-tuple-element.40), channel_id=1, source_target_pairs={{0,3},{1,0},{2,1},{3,2},{4,7},{5,4},{6,5},{7,6},{8,11},{9,8},{10,9... | collective-permute-start | bytes 393224 | tf_op jit(solution)/shard_map/ppermute | solution.py:354

commit v8 on v7

--- a/solution.py
+++ b/solution.py
@@ -417,8 +417,8 @@
     near = (
         weight,
         neighbour(weight, (0, 1), (0, -1)),
+        neighbour(weight, (1, 0), (1, 0)),
         neighbour(weight, (-1, 0), (-1, 0)),
-        neighbour(weight, (1, 0), (1, 0)),
     )
 
     back = call(
@@ -451,7 +451,7 @@
     )(*near)
     swapped = other_core(gathered)
     mine = chip_class(z, y)
-    offsets = [0, 2, 1, CLASSES - 1]
+    offsets = [0, 2, CLASSES - 1, 1]
     order = [(((mine + offset) % CLASSES) * N_C + core) for offset in offsets]
     order += [(((mine + offset) % CLASSES) * N_C + 1 - core) for offset in offsets]
     order = jnp.stack(order + [across]).astype(jnp.int32)

time: 128 us -> 136 us (1.062)
  the two profiles are of different devices: /device:TPU:1 before, /device:TPU:464 now
where the time goes in v8:
time: 136 us; the launch traced here: 135 us
  starting transfers between devices  57.8 us (42%)
  waiting for transfers between devices  57.3 us (42%)
  Pallas kernels  18 us (13%)
    all_to_all x1, waiting for transfers between devices, body(): lax.all_to_all(outgoing, 'dp', split_axis=0, concat_axis=0, tiled=True)  28.3 us
    ppermute x6, starting transfers between devices, around(): lax.ppermute(value, 'mp', [(i, (i + shift) % parts) for i in range(parts)])  20.4 us
    ppermute x3, waiting for transfers between devices, neighbour(): return lax.ppermute(value, 'dp', pairs)  19.6 us
    all_to_all x1, starting transfers between devices, body(): lax.all_to_all(outgoing, 'dp', split_axis=0, concat_axis=0, tiled=True)  11.7 us
    all_to_all x1, starting transfers between devices, body(): lax.all_to_all(back, 'dp', split_axis=0, concat_axis=0, tiled=True)  11.3 us
    ppermute x3, starting transfers between devices, neighbour(): return lax.ppermute(value, 'dp', pairs)  8.21 us
    ppermute x6, waiting for transfers between devices, around(): lax.ppermute(value, 'mp', [(i, (i + shift) % parts) for i in range(parts)])  7.73 us
    all_to_all x1, starting transfers between devices, body(): lax.all_to_all(low_parts, 'mp', split_axis=0, concat_axis=0, tiled=True)  4.29 us
  transfers between devices with their start and end apart: 13, of which 7 were waited for; matrix products, arithmetic and copies ran while one was open for 0% of the time, Pallas kernels for 8%

profile of v8, /device:TPU:464, one launch (start us, length us, event | category | flops | bytes accessed | tf_op | source)
XLA Modules:
  0.0 135.2 jit_solution(11960139840969989148)
XLA Ops:
  0.6 2.9 %spread.1 = (bf16[128,2,3328]{2,1,0:T(2,128)(2,1)}, bf16[256,128]{1,0:T(8,128)(2,1)}) custom-call(s32[1,128]{1,0:T(1,128)} %bitcast.25, s32[1,128]{1,0:T(1,128)} %bitcast.26, bf16[128,2048]{1,0:T(8,128)(2,1)} %tokens_ref.3, bf16[128,256]{1,0:T(8,128)(2,1)} %own_ref.1, bf16[8,2048]{1,0:T(8,128)(2,1)} %bitcast.24), custom_call_target="tpu_custom_call" | custom-call | flops 218103808 | bytes 2555904 | tf_op jit(solution)/shard_map/spread/pallas_call | solution.py:358
  3.5 0.0 copy-start.7
  3.5 0.0 copy-start.4
  3.5 0.0 copy-start.6
  3.5 11.7 %all-to-all-start = ((bf16[128,2,3328]{2,1,0:T(2,128)(2,1)}), bf16[128,2,3328]{2,1,0:T(2,128)(2,1)S(1)}, u32[]{:S(2)}, u32[]{:S(2)}) async-start(bf16[128,2,3328]{2,1,0:T(2,128)(2,1)} %get-tuple-element.24), calls=%async_computation | async-start | bytes 3407872 | tf_op jit(solution)/shard_map/all_to_all | solution.py:388
  15.2 0.0 copy-done.7
  15.2 3.4 %collective-permute-start = (bf16[128,256]{1,0:T(8,128)(2,1)S(1)}, bf16[128,256]{1,0:T(8,128)(2,1)S(1)}, u32[]{:S(2)}, u32[]{:S(2)}) collective-permute-start(bf16[128,256]{1,0:T(8,128)(2,1)S(1)} %copy-done.7), channel_id=1, source_target_pairs={{0,1},{1,2},{2,3},{3,0},{4,5},{5,6},{6,7},{7,4},{8,9},{9,10},{10,1... | collective-permute-start | bytes 196616 | tf_op jit(solution)/shard_map/ppermute | solution.py:354
  18.7 4.6 %collective-permute-start.1 = (bf16[128,256]{1,0:T(8,128)(2,1)S(1)}, bf16[128,256]{1,0:T(8,128)(2,1)S(1)}, u32[]{:S(2)}, u32[]{:S(2)}) collective-permute-start(bf16[128,256]{1,0:T(8,128)(2,1)S(1)} %copy-done.7), channel_id=1, source_target_pairs={{0,2},{1,3},{2,0},{3,1},{4,6},{5,7},{6,4},{7,5},{8,10},{9,11},{10,... | collective-permute-start | bytes 196616 | tf_op jit(solution)/shard_map/ppermute | solution.py:354
  23.3 3.3 %collective-permute-start.2 = (bf16[128,256]{1,0:T(8,128)(2,1)S(1)}, bf16[128,256]{1,0:T(8,128)(2,1)S(1)}, u32[]{:S(2)}, u32[]{:S(2)}) collective-permute-start(bf16[128,256]{1,0:T(8,128)(2,1)S(1)} %copy-done.7), channel_id=1, source_target_pairs={{0,3},{1,0},{2,1},{3,2},{4,7},{5,4},{6,5},{7,6},{8,11},{9,8},{10,9... | collective-permute-start | bytes 196616 | tf_op jit(solution)/shard_map/ppermute | solution.py:354
  26.7 0.0 collective-permute-done.a_ref
  26.7 0.0 collective-permute-done.1.b_ref
  26.7 2.8 %collective-permute-done.2.c_ref = bf16[128,256]{1,0:T(8,128)(2,1)S(1)} collective-permute-done((bf16[128,256]{1,0:T(8,128)(2,1)S(1)}, bf16[128,256]{1,0:T(8,128)(2,1)S(1)}, u32[]{:S(2)}, u32[]{:S(2)}) %collective-permute-start.2) | collective-permute-done | bytes 65568 | tf_op jit(solution)/shard_map/ppermute | solution.py:354
  29.5 0.5 order.1.grads_ref
  29.9 0.0 copy-start.2
  29.9 28.3 %all-to-all-done.arrived_ref = bf16[128,2,3328]{2,1,0:T(2,128)(2,1)S(1)} async-done(((bf16[128,2,3328]{2,1,0:T(2,128)(2,1)}), bf16[128,2,3328]{2,1,0:T(2,128)(2,1)S(1)}, u32[]{:S(2)}, u32[]{:S(2)}) %all-to-all-start) | async-done | bytes 1703968 | tf_op jit(solution)/shard_map/all_to_all | solution.py:388
  58.2 0.0 copy-done.4
  58.2 1.3 low_rank.1
  59.5 4.3 %all-to-all-start.1 = ((f32[4,256,128]{2,1,0:T(8,128)}), f32[4,256,128]{2,1,0:T(8,128)S(1)}, u32[]{:S(2)}, u32[]{:S(2)}) async-start(f32[4,256,128]{2,1,0:T(8,128)} %low_rank.1), calls=%async_computation.1 | async-start | bytes 1048576 | tf_op jit(solution)/shard_map/all_to_all | solution.py:409
  63.8 0.1 weight.1.refs_0_
  63.9 2.4 %collective-permute-start.3 = (bf16[256,1024]{1,0:T(8,128)(2,1)S(1)}, bf16[256,1024]{1,0:T(8,128)(2,1)}, u32[]{:S(2)}, u32[]{:S(2)}) collective-permute-start(bf16[256,1024]{1,0:T(8,128)(2,1)S(1)} %weight.1.refs_0_), channel_id=1, source_target_pairs={{0,8},{4,60},{8,16},{12,4},{16,24},{20,12},{24,32},{28,20},{32,40}... | collective-permute-start | bytes 1572872 | tf_op jit(solution)/shard_map/ppermute | solution.py:313
  66.3 3.6 %collective-permute-start.4 = (bf16[256,1024]{1,0:T(8,128)(2,1)S(1)}, bf16[256,1024]{1,0:T(8,128)(2,1)}, u32[]{:S(2)}, u32[]{:S(2)}) collective-permute-start(bf16[256,1024]{1,0:T(8,128)(2,1)S(1)} %weight.1.refs_0_), channel_id=1, source_target_pairs={{0,64},{4,68},{8,72},{12,76},{16,80},{20,84},{24,88},{28,92},{32,9... | collective-permute-start | bytes 1572872 | tf_op jit(solution)/shard_map/ppermute | solution.py:313
  69.9 2.2 %collective-permute-start.5 = (bf16[256,1024]{1,0:T(8,128)(2,1)S(1)}, bf16[256,1024]{1,0:T(8,128)(2,1)}, u32[]{:S(2)}, u32[]{:S(2)}) collective-permute-start(bf16[256,1024]{1,0:T(8,128)(2,1)S(1)} %weight.1.refs_0_), channel_id=1, source_target_pairs={{0,448},{4,452},{8,456},{12,460},{16,464},{20,468},{24,472},{28,47... | collective-permute-start | bytes 1572872 | tf_op jit(solution)/shard_map/ppermute | solution.py:313
  72.1 0.3 all-to-all-done.1.parts_ref
  72.4 0.5 back.1
  73.0 1.0 copy-done.1
  74.0 11.3 %all-to-all-start.2 = ((bf16[128,2,2304]{2,1,0:T(2,128)(2,1)}), bf16[128,2,2304]{2,1,0:T(2,128)(2,1)}, u32[]{:S(2)}, u32[]{:S(2)}) async-start(bf16[128,2,2304]{2,1,0:T(2,128)(2,1)} %copy-done.1), calls=%async_computation.2 | async-start | bytes 2359296 | tf_op jit(solution)/shard_map/all_to_all | solution.py:431
  85.3 1.2 factor_gradients.1
  86.5 0.0 collective-permute-done.3.refs_1_
  86.5 0.0 collective-permute-done.4.refs_2_
  86.5 19.6 %collective-permute-done.5.refs_3_ = bf16[256,1024]{1,0:T(8,128)(2,1)} collective-permute-done((bf16[256,1024]{1,0:T(8,128)(2,1)S(1)}, bf16[256,1024]{1,0:T(8,128)(2,1)}, u32[]{:S(2)}, u32[]{:S(2)}) %collective-permute-start.5) | collective-permute-done | bytes 524320 | tf_op jit(solution)/shard_map/ppermute | solution.py:313
  106.1 2.9 %stack.38.weight_ref = bf16[4,256,1024]{2,1,0:T(8,128)(2,1)} custom-call(bf16[256,1024]{1,0:T(8,128)(2,1)S(1)} %weight.1.refs_0_, bf16[256,1024]{1,0:T(8,128)(2,1)} %collective-permute-done.3.refs_1_, bf16[256,1024]{1,0:T(8,128)(2,1)} %collective-permute-done.4.refs_2_, bf16[256,1024]{1,0:T(8,128)(2,1)} %collective-permute-done.5.refs_3_), custom_call_target="tpu_custom_call" | custom-call | bytes 4194304 | tf_op jit(solution)/shard_map/stack/pallas_call | solution.py:445
  109.0 1.9 %collective-permute-start.6 = (bf16[4,256,1024]{2,1,0:T(8,128)(2,1)}, bf16[4,256,1024]{2,1,0:T(8,128)(2,1)S(1)}, u32[]{:S(2)}, u32[]{:S(2)}) collective-permute-start(bf16[4,256,1024]{2,1,0:T(8,128)(2,1)} %stack.38.weight_ref), channel_id=1, source_target_pairs={{0,4},{4,0},{8,12},{12,8},{16,20},{20,16},{24,28},{28,24},{32,36},... | collective-permute-start | bytes 6291464 | tf_op jit(solution)/shard_map/ppermute | solution.py:317
  111.0 0.1 stack.37.order_ref
  111.1 2.7 %base_own.1 = (f32[4,128,256]{2,1,0:T(8,128)S(1)}, f32[4,128,256]{2,1,0:T(8,128)S(1)}) custom-call(s32[9]{0:T(128)S(1)} %stack.37.order_ref, bf16[128,2048]{1,0:T(8,128)(2,1)S(1)} %copy-done, bf16[4,128,256]{2,1,0:T(8,128)(2,1)S(1)} %order.1.grads_ref, bf16[4,256,1024]{2,1,0:T(8,128)(2,1)} %stack.38.weight_ref), custom_call_target="tpu_custom_call" | custom-call | flops 536870912 | bytes 2097152 | tf_op jit(solution)/shard_map/base_own/pallas_call | solution.py:460
  113.8 0.0 copy-start.3
  113.8 0.0 copy-start.5
  113.9 1.4 %collective-permute-done.6.weight_ref = bf16[4,256,1024]{2,1,0:T(8,128)(2,1)S(1)} collective-permute-done((bf16[4,256,1024]{2,1,0:T(8,128)(2,1)}, bf16[4,256,1024]{2,1,0:T(8,128)(2,1)S(1)}, u32[]{:S(2)}, u32[]{:S(2)}) %collective-permute-start.6) | collective-permute-done | bytes 2097184 | tf_op jit(solution)/shard_map/ppermute | solution.py:317
  115.3 2.5 %base_forward.1 = (f32[128,256]{1,0:T(8,128)S(1)}, f32[128,256]{1,0:T(8,128)S(1)}, f32[128,256]{1,0:T(8,128)S(1)}, f32[128,256]{1,0:T(8,128)S(1)}) custom-call(s32[9]{0:T(128)S(1)} %stack.37.order_ref, bf16[128,2048]{1,0:T(8,128)(2,1)S(1)} %copy-done, f32[4,128,256]{2,1,0:T(8,128)S(1)} %get-tuple-element.36.totals_ref, ...), custom_call_target="tpu_custom_call" | custom-call | flops 268435456 | bytes 2097152 | tf_op jit(solution)/shard_map/base_forward/pallas_call | solution.py:469
  117.7 1.9 %collective-permute-start.7 = (f32[128,256]{1,0:T(8,128)S(1)}, f32[128,256]{1,0:T(8,128)S(1)}, u32[]{:S(2)}, u32[]{:S(2)}) collective-permute-start(f32[128,256]{1,0:T(8,128)S(1)} %get-tuple-element.38), channel_id=1, source_target_pairs={{0,1},{1,2},{2,3},{3,0},{4,5},{5,6},{6,7},{7,4},{8,9},{9,10},{10,1... | collective-permute-start | bytes 393224 | tf_op jit(solution)/shard_map/ppermute | solution.py:354
  119.7 1.9 %collective-permute-start.8 = (f32[128,256]{1,0:T(8,128)S(1)}, f32[128,256]{1,0:T(8,128)S(1)}, u32[]{:S(2)}, u32[]{:S(2)}) collective-permute-start(f32[128,256]{1,0:T(8,128)S(1)} %get-tuple-element.39), channel_id=1, source_target_pairs={{0,2},{1,3},{2,0},{3,1},{4,6},{5,7},{6,4},{7,5},{8,10},{9,11},{10,... | collective-permute-start | bytes 393224 | tf_op jit(solution)/shard_map/ppermute | solution.py:354
  121.6 5.1 %collective-permute-start.9 = (f32[128,256]{1,0:T(8,128)S(1)}, f32[128,256]{1,0:T(8,128)S(1)}, u32[]{:S(2)}, u32[]{:S(2)}) collective-permute-start(f32[128,256]{1,0:T(8,128)S(1)} %get-tuple-element.40), channel_id=1, source_target_pairs={{0,3},{1,0},{2,1},{3,2},{4,7},{5,4},{6,5},{7,6},{8,11},{9,8},{10,9... | collective-permute-start | bytes 393224 | tf_op jit(solution)/shard_map/ppermute | solution.py:354
  126.7 2.4 %collective-permute-done.7.refs_1_ = f32[128,256]{1,0:T(8,128)S(1)} collective-permute-done((f32[128,256]{1,0:T(8,128)S(1)}, f32[128,256]{1,0:T(8,128)S(1)}, u32[]{:S(2)}, u32[]{:S(2)}) %collective-permute-start.7) | collective-permute-done | bytes 131104 | tf_op jit(solution)/shard_map/ppermute | solution.py:354
  129.2 0.0 collective-permute-done.8.refs_2_
  129.2 2.5 %collective-permute-done.9.refs_3_ = f32[128,256]{1,0:T(8,128)S(1)} collective-permute-done((f32[128,256]{1,0:T(8,128)S(1)}, f32[128,256]{1,0:T(8,128)S(1)}, u32[]{:S(2)}, u32[]{:S(2)}) %collective-permute-start.9) | collective-permute-done | bytes 131104 | tf_op jit(solution)/shard_map/ppermute | solution.py:354
  131.7 0.0 copy-done.5
  131.7 1.0 ready.1.ready_ref
  132.7 0.0 all-to-all-done.2.returned_ref
  132.7 2.4 %finish.1 = (bf16[128,256]{1,0:T(8,128)(2,1)}, bf16[128,2048]{1,0:T(8,128)(2,1)}) custom-call(bf16[128,2,2304]{2,1,0:T(2,128)(2,1)} %all-to-all-done.2.returned_ref, f32[128,2560]{1,0:T(8,128)S(1)} %ready.1.ready_ref), custom_call_target="tpu_custom_call" | custom-call | flops 150994944 | bytes 1179648 | tf_op jit(solution)/shard_map/finish/pallas_call | solution.py:491
  (6 shorter events, 0.0 us)
Async XLA Ops:
  3.5 11.7 %copy-start.7 = (bf16[128,256]{1,0:T(8,128)(2,1)S(1)}, bf16[128,256]{1,0:T(8,128)(2,1)}, u32[]{:S(2)}) copy-start(bf16[128,256]{1,0:T(8,128)(2,1)} %own_ref.1) | copy-start | bytes 196612
  3.5 54.7 %copy-start.4 = (bf16[1,2048,64]{1,2,0:T(8,128)(2,1)S(1)}, bf16[1,2048,64]{1,2,0:T(8,128)(2,1)}, u32[]{:S(2)}) copy-start(bf16[1,2048,64]{1,2,0:T(8,128)(2,1)} %param.10) | copy-start | bytes 786436
  3.5 54.7 %copy-start.6 = (bf16[1,64,256]{2,1,0:T(8,128)(2,1)S(1)}, bf16[1,64,256]{2,1,0:T(8,128)(2,1)}, u32[]{:S(2)}) copy-start(bf16[1,64,256]{2,1,0:T(8,128)(2,1)} %param.11) | copy-start | bytes 98308
  3.5 54.7 %all-to-all-start = ((bf16[128,2,3328]{2,1,0:T(2,128)(2,1)}), bf16[128,2,3328]{2,1,0:T(2,128)(2,1)S(1)}, u32[]{:S(2)}, u32[]{:S(2)}) async-start(bf16[128,2,3328]{2,1,0:T(2,128)(2,1)} %get-tuple-element.24), calls=%async_computation | async-start | bytes 3407872 | tf_op jit(solution)/shard_map/all_to_all | solution.py:388
  15.2 11.4 %collective-permute-start = (bf16[128,256]{1,0:T(8,128)(2,1)S(1)}, bf16[128,256]{1,0:T(8,128)(2,1)S(1)}, u32[]{:S(2)}, u32[]{:S(2)}) collective-permute-start(bf16[128,256]{1,0:T(8,128)(2,1)S(1)} %copy-done.7), channel_id=1, source_target_pairs={{0,1},{1,2},{2,3},{3,0},{4,5},{5,6},{6,7},{7,4},{8,9},{9,10},{10,1... | collective-permute-start | bytes 196616 | tf_op jit(solution)/shard_map/ppermute | solution.py:354
  18.7 8.0 %collective-permute-start.1 = (bf16[128,256]{1,0:T(8,128)(2,1)S(1)}, bf16[128,256]{1,0:T(8,128)(2,1)S(1)}, u32[]{:S(2)}, u32[]{:S(2)}) collective-permute-start(bf16[128,256]{1,0:T(8,128)(2,1)S(1)} %copy-done.7), channel_id=1, source_target_pairs={{0,2},{1,3},{2,0},{3,1},{4,6},{5,7},{6,4},{7,5},{8,10},{9,11},{10,... | collective-permute-start | bytes 196616 | tf_op jit(solution)/shard_map/ppermute | solution.py:354
  23.3 6.2 %collective-permute-start.2 = (bf16[128,256]{1,0:T(8,128)(2,1)S(1)}, bf16[128,256]{1,0:T(8,128)(2,1)S(1)}, u32[]{:S(2)}, u32[]{:S(2)}) collective-permute-start(bf16[128,256]{1,0:T(8,128)(2,1)S(1)} %copy-done.7), channel_id=1, source_target_pairs={{0,3},{1,0},{2,1},{3,2},{4,7},{5,4},{6,5},{7,6},{8,11},{9,8},{10,9... | collective-permute-start | bytes 196616 | tf_op jit(solution)/shard_map/ppermute | solution.py:354
  29.9 81.2 %copy-start.2 = (bf16[4,128,256]{2,1,0:T(8,128)(2,1)}, bf16[4,128,256]{2,1,0:T(8,128)(2,1)S(1)}, u32[]{:S(2)}) copy-start(bf16[4,128,256]{2,1,0:T(8,128)(2,1)S(1)} %order.1.grads_ref) | copy-start | bytes 786436
  59.5 12.9 %all-to-all-start.1 = ((f32[4,256,128]{2,1,0:T(8,128)}), f32[4,256,128]{2,1,0:T(8,128)S(1)}, u32[]{:S(2)}, u32[]{:S(2)}) async-start(f32[4,256,128]{2,1,0:T(8,128)} %low_rank.1), calls=%async_computation.1 | async-start | bytes 1048576 | tf_op jit(solution)/shard_map/all_to_all | solution.py:409
  63.9 22.6 %collective-permute-start.3 = (bf16[256,1024]{1,0:T(8,128)(2,1)S(1)}, bf16[256,1024]{1,0:T(8,128)(2,1)}, u32[]{:S(2)}, u32[]{:S(2)}) collective-permute-start(bf16[256,1024]{1,0:T(8,128)(2,1)S(1)} %weight.1.refs_0_), channel_id=1, source_target_pairs={{0,8},{4,60},{8,16},{12,4},{16,24},{20,12},{24,32},{28,20},{32,40}... | collective-permute-start | bytes 1572872 | tf_op jit(solution)/shard_map/ppermute | solution.py:313
  66.3 20.3 %collective-permute-start.4 = (bf16[256,1024]{1,0:T(8,128)(2,1)S(1)}, bf16[256,1024]{1,0:T(8,128)(2,1)}, u32[]{:S(2)}, u32[]{:S(2)}) collective-permute-start(bf16[256,1024]{1,0:T(8,128)(2,1)S(1)} %weight.1.refs_0_), channel_id=1, source_target_pairs={{0,64},{4,68},{8,72},{12,76},{16,80},{20,84},{24,88},{28,92},{32,9... | collective-permute-start | bytes 1572872 | tf_op jit(solution)/shard_map/ppermute | solution.py:313
  69.9 36.2 %collective-permute-start.5 = (bf16[256,1024]{1,0:T(8,128)(2,1)S(1)}, bf16[256,1024]{1,0:T(8,128)(2,1)}, u32[]{:S(2)}, u32[]{:S(2)}) collective-permute-start(bf16[256,1024]{1,0:T(8,128)(2,1)S(1)} %weight.1.refs_0_), channel_id=1, source_target_pairs={{0,448},{4,452},{8,456},{12,460},{16,464},{20,468},{24,472},{28,47... | collective-permute-start | bytes 1572872 | tf_op jit(solution)/shard_map/ppermute | solution.py:313
  73.0 1.0 copy-start.1
  74.0 58.7 %all-to-all-start.2 = ((bf16[128,2,2304]{2,1,0:T(2,128)(2,1)}), bf16[128,2,2304]{2,1,0:T(2,128)(2,1)}, u32[]{:S(2)}, u32[]{:S(2)}) async-start(bf16[128,2,2304]{2,1,0:T(2,128)(2,1)} %copy-done.1), calls=%async_computation.2 | async-start | bytes 2359296 | tf_op jit(solution)/shard_map/all_to_all | solution.py:431
  106.1 5.0 %copy-start = (bf16[128,2048]{1,0:T(8,128)(2,1)S(1)}, bf16[128,2048]{1,0:T(8,128)(2,1)}, u32[]{:S(2)}) copy-start(bf16[128,2048]{1,0:T(8,128)(2,1)} %tokens_ref.3) | copy-start | bytes 1572868
  109.0 6.3 %collective-permute-start.6 = (bf16[4,256,1024]{2,1,0:T(8,128)(2,1)}, bf16[4,256,1024]{2,1,0:T(8,128)(2,1)S(1)}, u32[]{:S(2)}, u32[]{:S(2)}) collective-permute-start(bf16[4,256,1024]{2,1,0:T(8,128)(2,1)} %stack.38.weight_ref), channel_id=1, source_target_pairs={{0,4},{4,0},{8,12},{12,8},{16,20},{20,16},{24,28},{28,24},{32,36},... | collective-permute-start | bytes 6291464 | tf_op jit(solution)/shard_map/ppermute | solution.py:317
  113.8 17.9 %copy-start.3 = (bf16[4,128,256]{2,1,0:T(8,128)(2,1)S(1)}, bf16[4,128,256]{2,1,0:T(8,128)(2,1)}, u32[]{:S(2)}) copy-start(bf16[4,128,256]{2,1,0:T(8,128)(2,1)} %copy-done.2) | copy-start | bytes 786436
  113.8 17.8 %copy-start.5 = (bf16[256,128]{1,0:T(8,128)(2,1)S(1)}, bf16[256,128]{1,0:T(8,128)(2,1)}, u32[]{:S(2)}) copy-start(bf16[256,128]{1,0:T(8,128)(2,1)} %get-tuple-element.35.picks_ref) | copy-start | bytes 196612
  117.7 11.4 %collective-permute-start.7 = (f32[128,256]{1,0:T(8,128)S(1)}, f32[128,256]{1,0:T(8,128)S(1)}, u32[]{:S(2)}, u32[]{:S(2)}) collective-permute-start(f32[128,256]{1,0:T(8,128)S(1)} %get-tuple-element.38), channel_id=1, source_target_pairs={{0,1},{1,2},{2,3},{3,0},{4,5},{5,6},{6,7},{7,4},{8,9},{9,10},{10,1... | collective-permute-start | bytes 393224 | tf_op jit(solution)/shard_map/ppermute | solution.py:354
  119.7 9.5 %collective-permute-start.8 = (f32[128,256]{1,0:T(8,128)S(1)}, f32[128,256]{1,0:T(8,128)S(1)}, u32[]{:S(2)}, u32[]{:S(2)}) collective-permute-start(f32[128,256]{1,0:T(8,128)S(1)} %get-tuple-element.39), channel_id=1, source_target_pairs={{0,2},{1,3},{2,0},{3,1},{4,6},{5,7},{6,4},{7,5},{8,10},{9,11},{10,... | collective-permute-start | bytes 393224 | tf_op jit(solution)/shard_map/ppermute | solution.py:354
  121.6 10.1 %collective-permute-start.9 = (f32[128,256]{1,0:T(8,128)S(1)}, f32[128,256]{1,0:T(8,128)S(1)}, u32[]{:S(2)}, u32[]{:S(2)}) collective-permute-start(f32[128,256]{1,0:T(8,128)S(1)} %get-tuple-element.40), channel_id=1, source_target_pairs={{0,3},{1,0},{2,1},{3,2},{4,7},{5,4},{6,5},{7,6},{8,11},{9,8},{10,9... | collective-permute-start | bytes 393224 | tf_op jit(solution)/shard_map/ppermute | solution.py:354
